TPU v7x, 512 devices: a whole 4x8x8 slice. The times are simulated.
512 devices in a mesh: dp: 64 (over z, y_lo, x), fsdp: 8 (over y_hi, core).
Axes of the slice: x: 4, y: 8 (y_hi: 4, y_lo: 2; y = y_hi * 2 + y_lo), z: 8, core: 2. Of those that a mesh axis runs over, the one named last changes fastest.
Arguments:
- adapter_in: bfloat16 [65536, 8192], P(('dp', 'fsdp')), may hold values from -6 to 6
- frozen: bfloat16 [65536, 8192], P(('dp', 'fsdp')), may hold values from -8 to 8
- gain: float32 [8192], replicated, may hold values from 0.25 to 1.75
- adapter_a: bfloat16 [8192, 64], P('fsdp'), may hold values from -0.0625 to 0.0625
- adapter_up_matrix: bfloat16 [64, 8192], P(None, 'fsdp'), may hold values from -0.75 to 0.75
- passages: bfloat16 [2048, 8192], P('dp', 'fsdp'), may hold values from -8 to 8
- positive: int32 [2048], P('dp'), may hold values from 0 to 2047, as said below
Outputs:
- adapter_grads: float32 [2, 64, 8192], P(None, 'fsdp', 'dp')
- loss: float32 [], replicated
Inputs may be any that keep to these rules, and one draw needn't show every extreme that they name: Query i of group g (i from g * 32) has its positive among the passages of the same group, and every passage is the positive of exactly one query.
All inputs are finite; a program needn't handle non-finite values.
Results may differ from a plain program's by a relative error of at most 0.017.
Values may be sent and summed in bfloat16 or wider, within the bound.
No kernel may reach another device: no remote copies, remote signals or barrier semaphores. Data moves between devices by JAX's collectives and lax.ppermute only.
A program may use at most 64 MiB of HBM per device.

v0:
```python
import jax
import jax.numpy as jnp
from jax import lax
from jax.sharding import PartitionSpec as P

LEN = 32


adapter_scale_factor = 0.25
inv_temp = 20.0
norm_eps = 1e-05


def contracted_row_product(left, right):
    return lax.dot_general(
        left, right, (((1,), (1,)), ((), ())), preferred_element_type=jnp.float32
    )


def shards(adapter_in, frozen, gain, adapter_a, adapter_up_matrix, passages, positive):
    whole_a, full_up_matrix = (
        lax.all_gather(adapter_a, "fsdp", axis=0, tiled=True),
        lax.all_gather(adapter_up_matrix, "fsdp", axis=1, tiled=True),
    )
    width = whole_a.shape[0]
    queries = adapter_in.shape[0] // LEN
    latent_code = jnp.dot(adapter_in, whole_a, preferred_element_type=jnp.float32).astype(
        jnp.bfloat16
    )
    hidden_state = frozen.astype(jnp.float32) + adapter_scale_factor * jnp.dot(
        latent_code, full_up_matrix, preferred_element_type=jnp.float32
    )
    inv_rms = lax.rsqrt(jnp.mean(hidden_state * hidden_state, axis=-1, keepdims=True) + norm_eps)
    normed = hidden_state * inv_rms * gain
    pooled = jnp.mean(normed.reshape(queries, LEN, width), axis=1)
    length = jnp.sqrt(jnp.sum(pooled * pooled, axis=-1, keepdims=True))
    unit = pooled / length
    query_feat = lax.all_to_all(
        unit.astype(jnp.bfloat16), "fsdp", split_axis=1, concat_axis=0, tiled=True
    )
    pas = passages.astype(jnp.float32)
    squares = lax.psum(jnp.sum(pas * pas, axis=-1), "fsdp")
    passage_unit = (pas / jnp.sqrt(squares)[:, None]).astype(jnp.bfloat16)
    total_pairs = passage_unit.shape[0] * lax.axis_size("dp")
    columns = jnp.arange(total_pairs, dtype=jnp.int32)
    partial_value = contracted_row_product(
        query_feat, lax.all_gather(passage_unit, "dp", axis=0, tiled=True)
    )
    scores = inv_temp * lax.psum_scatter(partial_value, "fsdp", scatter_dimension=0, tiled=True)
    own_pos = lax.dynamic_slice_in_dim(positive, lax.axis_index("fsdp") * queries, queries, 0)
    expo = jnp.exp(scores - inv_temp)
    row_sum = jnp.sum(expo, axis=1)
    onehot = (own_pos[:, None] == columns[None, :]).astype(jnp.float32)
    local_term = jnp.sum(jnp.log(row_sum)) - 2.0 * jnp.sum(scores * onehot)
    col_sum, summed = lax.psum((jnp.sum(expo, axis=0), local_term), ("dp", "fsdp"))
    loss = (summed + jnp.sum(jnp.log(col_sum))) / (2.0 * total_pairs) + inv_temp
    weights = (0.5 * (expo / row_sum[:, None] + expo / col_sum[None, :]) - onehot).astype(
        jnp.bfloat16
    )
    group_weights = lax.all_gather(weights, "fsdp", axis=0, tiled=True)
    grad_feat = jnp.dot(
        group_weights,
        lax.all_gather(passage_unit, "dp", axis=0, tiled=True),
        preferred_element_type=jnp.float32,
    )
    query_grad = lax.all_to_all(
        inv_temp * grad_feat, "fsdp", split_axis=0, concat_axis=1, tiled=True
    )
    pooled_grad = (query_grad - unit * jnp.sum(unit * query_grad, axis=-1, keepdims=True)) / length
    normed_grad = jnp.repeat(pooled_grad / LEN, LEN, axis=0)
    scaled = normed_grad * gain
    hidden_state_gradient = (
        inv_rms * scaled
        - hidden_state * inv_rms**3 * jnp.mean(scaled * hidden_state, axis=-1, keepdims=True)
    ).astype(jnp.bfloat16)
    latent_code_gradient = (
        adapter_scale_factor * contracted_row_product(hidden_state_gradient, full_up_matrix)
    ).astype(jnp.bfloat16)
    grad_a_t = jnp.dot(latent_code_gradient.T, adapter_in, preferred_element_type=jnp.float32)
    up_matrix_gradient = adapter_scale_factor * jnp.dot(
        latent_code.T, hidden_state_gradient, preferred_element_type=jnp.float32
    )
    stacked = jnp.stack([grad_a_t, up_matrix_gradient])
    group_sum = lax.psum_scatter(
        stacked.astype(jnp.bfloat16), "fsdp", scatter_dimension=1, tiled=True
    ).astype(jnp.float32)
    adapter_grads = lax.psum_scatter(group_sum, "dp", scatter_dimension=2, tiled=True)
    return (adapter_grads, loss)


def solution(mesh):
    placed = (
        P(("dp", "fsdp"), None),
        P(("dp", "fsdp"), None),
        P(),
        P("fsdp", None),
        P(None, "fsdp"),
        P("dp", "fsdp"),
        P("dp"),
    )
    return jax.shard_map(
        shards, mesh=mesh, in_specs=placed, out_specs=(P(None, "fsdp", "dp"), P()), check_vma=False
    )
```

profile of v0, /device:TPU:16, one launch (start us, length us, event | category | flops | bytes accessed | tf_op | source)
XLA Modules:
  0.0 986.8 jit_solution(11670023063035730330)
XLA Ops:
  9.7 15.6 %psum.21 = f32[32]{0:T(128)S(1)} all-reduce(f32[32]{0:T(128)S(1)} %fusion.10), channel_id=1, replica_groups=mesh['dp'=64,'fsdp'=8] {'fsdp'}, use_global_device_ids=true, to_apply=%region_4.0 | all-reduce | flops 32 | bytes 256 | tf_op jit(solution)/shard_map/psum | solution.py:42
  25.2 1.5 fusion.11
  26.8 20.0 %all-gather.5.cloned.1.call-done = bf16[8192,64]{0,1:T(8,128)(2,1)} async-done(((bf16[1024,64]{0,1:T(8,128)(2,1)}), bf16[8192,64]{0,1:T(8,128)(2,1)}) %all-gather.5.cloned.1.call-update) | async-done | bytes 1048592 | tf_op jit(solution)/shard_map/all_gather | solution.py:22
  46.8 2.1 convolution_convert_fusion.1
  48.9 31.0 %all-gather.7.cloned.1.call-done = bf16[64,8192]{1,0:T(8,128)(2,1)} async-done(((bf16[64,1024]{1,0:T(8,128)(2,1)}), bf16[64,8192]{1,0:T(8,128)(2,1)}) %all-gather.7.cloned.1.call-update) | async-done | bytes 1048592 | tf_op jit(solution)/shard_map/all_gather | solution.py:23
  80.0 3.0 multiply_reduce_fusion
  82.9 2.0 copy-done.1
  86.0 10.9 %all_to_all.35 = bf16[4,8,1024]{2,0,1:T(4,128)(2,1)S(1)} all-to-all(bf16[4,8,1024]{2,0,1:T(4,128)(2,1)S(1)} %fusion.21), channel_id=1, replica_groups=mesh['dp'=64,'fsdp'=8] {'fsdp'}, dimensions={1} | all-to-all | bytes 131072 | tf_op jit(solution)/shard_map/all_to_all | solution.py:38
  96.9 291.3 %all-gather.9.cloned.1.call-done = bf16[2048,1024]{1,0:T(8,128)(2,1)} async-done(((bf16[32,1024]{1,0:T(8,128)(2,1)}), bf16[2048,1024]{1,0:T(8,128)(2,1)}) %all-gather.9.cloned.1.call-update) | async-done | bytes 4194320 | tf_op jit(solution)/shard_map/all_gather | solution.py:47
  388.1 4.2 fusion.22
  394.5 69.7 %all-reduce.4.cloned.1.call-done = f32[32,2048]{1,0:T(8,128)} async-done(((f32[32,2048]{1,0:T(8,128)}), f32[32,2048]{1,0:T(8,128)}) %all-reduce.4.cloned.1.call-update) | async-done | bytes 262160
  464.2 1.6 select_reduce_fusion
  467.6 100.8 %all-reduce.1 = (f32[2048]{0:T(1024)S(1)}, f32[]{:T(128)}) all-reduce(f32[2048]{0:T(1024)S(1)} %get-tuple-element.3, f32[]{:T(128)S(6)} %sub.19), channel_id=1, replica_groups=mesh['dp'=64,'fsdp'=8] {'dp','fsdp'}, use_global_device_ids=true, to_apply=%region_8.0 | all-reduce | flops 2049 | bytes 16392 | tf_op jit(solution)/shard_map/psum | solution.py:55
  569.3 14.6 %all-gather = bf16[8,4,2048]{2,1,0:T(4,128)(2,1)S(1)} all-gather(bf16[1,4,2048]{2,1,0:T(4,128)(2,1)S(1)} %fusion.17), channel_id=1, replica_groups=mesh['dp'=64,'fsdp'=8] {'fsdp'}, dimensions={0}, use_global_device_ids=true | all-gather | bytes 147456 | tf_op jit(solution)/shard_map/all_gather | solution.py:60
  583.9 3.0 convolution_multiply_fusion.2
  587.0 13.9 %all_to_all.36 = f32[8,4,1024]{2,1,0:T(4,128)S(1)} all-to-all(f32[8,4,1024]{2,1,0:T(4,128)S(1)} %all_to_all.29), channel_id=1, replica_groups=mesh['dp'=64,'fsdp'=8] {'fsdp'}, dimensions={0} | all-to-all | bytes 262144 | tf_op jit(solution)/shard_map/all_to_all | solution.py:66
  601.3 2.6 fusion.8
  604.7 1.3 copy-done.3
  606.5 4.5 fusion.2
  611.0 1.4 pad_maximum_fusion
  612.4 2.2 copy.9
  614.6 2.5 copy.11
  617.2 38.5 %reduce-scatter.7.cloned.1.call-done = bf16[8,16384]{1,0:T(8,128)(2,1)} async-done(((bf16[64,16384]{1,0:T(8,128)(2,1)}), bf16[8,16384]{1,0:T(8,128)(2,1)}) %reduce-scatter.7.cloned.1.call-update) | async-done | bytes 262160
  659.8 319.0 %reduce-scatter.5.cloned.1.call-done = f32[2,8,128]{2,1,0:T(8,128)} async-done(((f32[2,8,8192]{2,1,0:T(8,128)}), f32[2,8,128]{2,1,0:T(8,128)}) %reduce-scatter.5.cloned.1.call-update) | async-done | bytes 8208 | tf_op jit(solution)/shard_map/reduce_scatter | solution.py:87
  (44 shorter events, 11.1 us)
Async XLA Ops:
  7.2 39.7 %copy-start = (bf16[128,8192]{1,0:T(8,128)(2,1)S(1)}, bf16[128,8192]{1,0:T(8,128)(2,1)}, u32[]{:S(2)}) copy-start(bf16[128,8192]{1,0:T(8,128)(2,1)} %param.7) | copy-start | bytes 6291460
  7.2 39.6 %all-gather.5.cloned.1.call-start = ((), (), s32[]{:S(2)}) async-start(), calls=%async_computation.4 | async-start | bytes 1179648 | tf_op jit(solution)/shard_map/all_gather | solution.py:22
  7.9 72.0 %all-gather.7.cloned.1.call-start = ((), (), s32[]{:S(2)}) async-start(), calls=%async_computation.5 | async-start | bytes 1179648 | tf_op jit(solution)/shard_map/all_gather | solution.py:23
  8.7 379.5 %all-gather.9.cloned.1.call-start = ((), (), s32[]{:S(2)}) async-start(), calls=%async_computation.6 | async-start | bytes 4259840 | tf_op jit(solution)/shard_map/all_gather | solution.py:47
  26.8 437.4 %all-reduce.4.cloned.1.call-start = ((), (), s32[]{:S(2)}) async-start(), calls=%async_computation.9 | async-start | bytes 524288
  48.9 36.0 %copy-start.4 = (f32[8192]{0:T(1024)S(1)}, f32[8192]{0:T(1024)}, u32[]{:S(2)}) copy-start(f32[8192]{0:T(1024)} %param.9) | copy-start | bytes 98308
  82.9 2.0 copy-start.1
  84.9 307.5 %copy-start.5 = (s32[32]{0:T(128)S(1)}, s32[32]{0:T(128)}, u32[]{:S(2)}) copy-start(s32[32]{0:T(128)} %param.13) | copy-start | bytes 388
  392.4 263.3 %reduce-scatter.7.cloned.1.call-start = ((), (), s32[]{:S(2)}) async-start(), calls=%async_computation.8 | async-start | bytes 2359296
  587.0 16.9 %copy-start.2 = (f32[128,8192]{1,0:T(8,128)S(1)}, f32[128,8192]{1,0:T(8,128)}, u32[]{:S(2)}) copy-start(f32[128,8192]{1,0:T(8,128)} %copy-done.1) | copy-start | bytes 12582916
  604.7 1.4 copy-start.3
  617.1 361.7 %reduce-scatter.5.cloned.1.call-start = ((), (), s32[]{:S(2)}) async-start(), calls=%async_computation.7 | async-start | bytes 532480 | tf_op jit(solution)/shard_map/reduce_scatter | solution.py:87
Sparse Core Ops, SparseCore 0:
  10.1 36.6 all-gather.4
  49.0 30.9 all-gather.6
  82.0 306.0 all-gather.8
  392.5 71.5 all-reduce.3
  617.3 38.3 reduce-scatter.6
  659.1 319.6 reduce-scatter.4
where the time goes:
time: 988 us; the launch traced here: 987 us
  waiting for transfers between devices  771 us (78%)
  blocking collectives  156 us (16%)
  between operations  18.7 us (2%)
  matrix products  17.2 us (2%)
  other arithmetic  13.5 us (1%)
  local copies, waits for them, and re-layouts  10.6 us (1%)
    reduce_scatter x1, waiting for transfers between devices, shards(): lax.psum_scatter(group_sum, 'dp', scatter_dimension=2, tiled=True)  319 us
    all_gather x1, waiting for transfers between devices, shards(): lax.all_gather(passage_unit, 'dp', axis=0, tiled=True)  291 us
    unnamed x8, waiting for transfers between devices  110 us
    psum x1, blocking collectives, shards(): lax.psum((jnp.sum(expo, axis=0), local_term), ('dp', 'fsdp'))  101 us
    all_gather x1, waiting for transfers between devices, shards(): lax.all_gather(adapter_up_matrix, 'fsdp', axis=1, tiled=True)  31 us
    all_gather x1, waiting for transfers between devices, shards(): lax.all_gather(adapter_a, 'fsdp', axis=0, tiled=True)  20 us
  transfers between devices with their start and end apart: 6, of which 6 were waited for; matrix products, arithmetic and copies ran while one was open for 1% of the time, Pallas kernels for 0%

commit v1 on v0

v1 whole, which is shorter than its diff:
```python
import jax
import jax.numpy as jnp
from jax import lax
from jax.sharding import Mesh
from jax.sharding import PartitionSpec as P

LEN = 32


adapter_scale_factor = 0.25
inv_temp = 20.0
norm_eps = 1e-05

AXES = ("z", "yl", "x", "yh", "c")
SIZES = (4, 2, 8, 4, 2)


def contracted_row_product(left, right):
    return lax.dot_general(
        left, right, (((1,), (1,)), ((), ())), preferred_element_type=jnp.float32
    )


def exchange(blocks, axes):
    return lax.all_to_all(blocks, axes, 0, 0, tiled=True)


def to_all(block, axes, devices):
    return exchange(jnp.broadcast_to(block[None], (devices, *block.shape)), axes)


def swap_cores(value):
    return lax.ppermute(value, "c", [(0, 1), (1, 0)])


def shards(sizes, adapter_in, frozen, gain, adapter_a, adapter_up_matrix, passages, positive):
    nz, nyl, nx, nyh, nc = sizes
    ny = nyl * nyh
    iz, iyl, ix, iyh, ic = (lax.axis_index(axis) for axis in AXES)
    rank = adapter_up_matrix.shape[0]
    feats = passages.shape[1]
    half = nyh * feats
    width = half * nc
    queries = adapter_in.shape[0] // LEN
    group = passages.shape[0]
    rows = group // nyh

    sent = jnp.broadcast_to(passages.reshape(1, nyh, rows, feats), (nz, nyh, rows, feats))
    got = exchange(sent.reshape(nz * nyh, rows, feats), ("z", "yh"))
    got = got.reshape(nz, nyh, rows, feats).transpose(0, 2, 1, 3).reshape(nz * rows, half)
    got, adapter_a, adapter_up_matrix = lax.optimization_barrier(
        (got, adapter_a, adapter_up_matrix)
    )
    block = lax.all_gather(got, "x", axis=0, tiled=True)

    mine = jnp.where(iyl == 0, adapter_a.T, adapter_up_matrix)
    own = to_all(mine, ("yl", "yh"), ny).reshape(nyl, nyh, rank, feats)
    other = swap_cores(own)
    pair = jnp.where(ic == 0, jnp.stack([own, other]), jnp.stack([other, own]))
    whole = pair.transpose(1, 3, 2, 0, 4).reshape(nyl, rank, width)
    whole_a_t, full_up_matrix = whole[0], whole[1]

    latent_code = contracted_row_product(adapter_in, whole_a_t).astype(jnp.bfloat16)
    hidden_state = frozen.astype(jnp.float32) + adapter_scale_factor * jnp.dot(
        latent_code, full_up_matrix, preferred_element_type=jnp.float32
    )
    inv_rms = lax.rsqrt(jnp.mean(hidden_state * hidden_state, axis=-1, keepdims=True) + norm_eps)
    normed = hidden_state * inv_rms * gain
    pooled = jnp.mean(normed.reshape(queries, LEN, width), axis=1)
    length = jnp.sqrt(jnp.sum(pooled * pooled, axis=-1, keepdims=True))
    unit = pooled / length

    halves = unit.astype(jnp.bfloat16).reshape(queries, nyh, nc, feats).transpose(2, 0, 1, 3)
    halves = jnp.broadcast_to(halves.reshape(1, nc, queries, half), (ny, nc, queries, half))
    ring = ny * nc
    query_feat = exchange(halves.reshape(ring, queries, half), ("yl", "yh", "c"))
    query_feat = query_feat.reshape(ring * queries, half)

    part = contracted_row_product(query_feat, block)
    wide = block.astype(jnp.float32)
    squares = jnp.sum(wide * wide, axis=-1)
    both = jnp.concatenate([part, jnp.broadcast_to(squares[None], (8, squares.shape[0]))])
    both = both + swap_cores(both)
    count = ring * queries
    inv_norm = 1.0 / jnp.sqrt(both[count])
    scores = inv_temp * (both[:count] * inv_norm)
    expo = jnp.exp(scores - inv_temp)

    columns = block.shape[0]
    at = lax.iota(jnp.int32, columns)
    at_x, at_z, at_row = at // (nz * rows), at // rows % nz, at % rows
    passage_id = ((at_z * nyl + iyl) * nx + at_x) * group + iyh * rows + at_row
    own_pos = jnp.where(
        lax.iota(jnp.int32, nyl)[:, None] == iyl, positive[None, :], -1
    ).reshape(count)
    onehot = (own_pos[:, None] == passage_id[None, :]).astype(jnp.float32)

    row_sum = jnp.sum(to_all(jnp.sum(expo, axis=1), ("yl", "yh"), ny), axis=0)
    local_term = jnp.sum(jnp.log(row_sum)) / ny - 2.0 * jnp.sum(scores * onehot)
    sums = jnp.concatenate([jnp.sum(expo, axis=0), jnp.full((128,), local_term)])
    sums = jnp.sum(to_all(sums, ("z", "x"), nz * nx), axis=0)
    col_sum = sums[:columns]
    loss_term = sums[columns] + jnp.sum(jnp.log(col_sum))
    weights = 0.5 * (expo / row_sum[:, None] + expo / col_sum[None, :]) - onehot
    weights = (weights * inv_norm).astype(jnp.bfloat16)
    grad_feat = inv_temp * jnp.dot(weights, block, preferred_element_type=jnp.float32)
    grad_feat = grad_feat.astype(jnp.bfloat16).reshape(ring, queries, half)
    query_grad = exchange(grad_feat, ("yl", "yh", "c")).astype(jnp.float32)
    query_grad = jnp.sum(query_grad.reshape(ny, nc, queries, nyh, feats), axis=0)
    query_grad = query_grad.transpose(1, 2, 0, 3).reshape(queries, width)

    pooled_grad = (query_grad - unit * jnp.sum(unit * query_grad, axis=-1, keepdims=True)) / length
    normed_grad = jnp.repeat(pooled_grad / LEN, LEN, axis=0)
    scaled = normed_grad * gain
    hidden_state_gradient = (
        inv_rms * scaled
        - hidden_state * inv_rms**3 * jnp.mean(scaled * hidden_state, axis=-1, keepdims=True)
    ).astype(jnp.bfloat16)
    latent_code_gradient = (
        adapter_scale_factor * contracted_row_product(hidden_state_gradient, full_up_matrix)
    ).astype(jnp.bfloat16)
    grad_a_t = jnp.dot(latent_code_gradient.T, adapter_in, preferred_element_type=jnp.float32)
    up_matrix_gradient = adapter_scale_factor * jnp.dot(
        latent_code.T, hidden_state_gradient, preferred_element_type=jnp.float32
    )
    out_rows = rank // (nyh * nc)
    cols = width // (nz * nyl * nx)
    stacked = jnp.stack([grad_a_t, up_matrix_gradient]).astype(jnp.bfloat16)
    stacked = stacked.reshape(2, nyh, nc, out_rows, nz, nyl, nx, cols)
    stacked = stacked.transpose(2, 6, 4, 5, 1, 0, 3, 7).reshape(
        nc, nx, nz * ny, 2 * out_rows, cols
    )
    keep = lax.dynamic_index_in_dim(stacked, ic, 0, keepdims=False)
    send = lax.dynamic_index_in_dim(stacked, 1 - ic, 0, keepdims=False)
    chip = (keep.astype(jnp.float32) + swap_cores(send).astype(jnp.float32)).astype(jnp.bfloat16)
    line = jnp.sum(exchange(chip, "x").astype(jnp.float32), axis=0)
    line = jnp.concatenate(
        [line, jnp.broadcast_to(loss_term, (line.shape[0], 8, cols))], axis=1
    )
    last = jnp.sum(exchange(line, ("z", "yl", "yh")), axis=0)
    adapter_grads = last[: 2 * out_rows].reshape(2, out_rows, cols)
    total_pairs = group * nz * nyl * nx
    loss = last[2 * out_rows, 0] / nz / (2.0 * total_pairs) + inv_temp
    return (adapter_grads, loss)


def build(mesh, sizes):
    split = Mesh(mesh.devices.reshape(sizes), AXES)
    dp, fsdp = ("z", "yl", "x"), ("yh", "c")
    placed = (
        P(AXES, None),
        P(AXES, None),
        P(),
        P(fsdp, None),
        P(None, fsdp),
        P(dp, fsdp),
        P(dp),
    )
    return jax.shard_map(
        lambda *args: shards(sizes, *args),
        mesh=split,
        in_specs=placed,
        out_specs=(P(None, fsdp, dp), P()),
        check_vma=False,
    )


def solution(mesh):
    return build(mesh, SIZES)
```

time: 988 us -> 277 us (0.28)
  the two profiles are of different devices: /device:TPU:16 before, /device:TPU:8 now
where the time goes in v1:
time: 277 us; the launch traced here: 275 us
  waiting for transfers between devices  73.8 us (27%)
  blocking collectives  69.8 us (25%)
  starting transfers between devices  48.4 us (17%)
  local copies, waits for them, and re-layouts  26.9 us (10%)
  other arithmetic  22.5 us (8%)
  between operations  18.8 us (7%)
  matrix products  15.1 us (5%)
    all_to_all x3, blocking collectives, exchange(): return lax.all_to_all(blocks, axes, 0, 0, tiled=True)  69.8 us
    all_to_all x5, waiting for transfers between devices, exchange(): return lax.all_to_all(blocks, axes, 0, 0, tiled=True)  48.1 us
    all_to_all x5, starting transfers between devices, exchange(): return lax.all_to_all(blocks, axes, 0, 0, tiled=True)  41.9 us
    all_gather x1, waiting for transfers between devices, shards(): block = lax.all_gather(got, 'x', axis=0, tiled=True)  19.4 us
    ppermute x3, starting transfers between devices, swap_cores(): return lax.ppermute(value, 'c', [(0, 1), (1, 0)])  6.49 us
    ppermute x3, waiting for transfers between devices, swap_cores(): return lax.ppermute(value, 'c', [(0, 1), (1, 0)])  6.33 us
    slice x3, local copies, waits for them, and re-layouts, shards(): whole_a_t, full_up_matrix = (whole[0], whole[1])  5.65 us
  transfers between devices with their start and end apart: 9, of which 8 were waited for; matrix products, arithmetic and copies ran while one was open for 9% of the time, Pallas kernels for 0%

profile of v1, /device:TPU:8, one launch (start us, length us, event | category | flops | bytes accessed | tf_op | source)
XLA Modules:
  0.0 275.3 jit_solution(7623194364892860457)
XLA Ops:
  8.9 14.8 %all-to-all-start = ((bf16[16,8,1024]{2,1,0:T(8,128)(2,1)}), bf16[16,8,1024]{2,1,0:T(8,128)(2,1)S(1)}, u32[]{:S(2)}, u32[]{:S(2)}) async-start(bf16[16,8,1024]{2,1,0:T(8,128)(2,1)} %bitcast.1), calls=%async_computation | async-start | bytes 524288 | tf_op jit(solution)/shard_map/all_to_all | solution.py:25
  23.7 13.6 %all-to-all-done = bf16[16,8,1024]{2,1,0:T(8,128)(2,1)S(1)} async-done(((bf16[16,8,1024]{2,1,0:T(8,128)(2,1)}), bf16[16,8,1024]{2,1,0:T(8,128)(2,1)S(1)}, u32[]{:S(2)}, u32[]{:S(2)}) %all-to-all-start) | async-done | bytes 262176 | tf_op jit(solution)/shard_map/all_to_all | solution.py:25
  38.5 29.1 %all_to_all.42 = bf16[8,64,1024]{2,1,0:T(8,128)(2,1)S(1)} all-to-all(bf16[8,64,1024]{2,1,0:T(8,128)(2,1)S(1)} %broadcast_in_dim.40), channel_id=1, replica_groups=mesh['z'=4,'yl'=2,'x'=8,'yh'=4,'c'=2] {'yl','yh'}, dimensions={0} | all-to-all | bytes 2097152 | tf_op jit(solution)/shard_map/all_to_all | solution.py:25
  69.5 2.7 collective-permute-done
  78.1 3.3 %copy.29 = bf16[1,64,4,2,1024]{4,3,2,1,0:T(2,128)(2,1)} copy(bf16[1,64,4,2,1024]{4,1,2,0,3:T(8,128)(2,1)} %get-tuple-element.13) | data formatting | bytes 2097152 | tf_op jit(solution)/shard_map/slice | solution.py:61
  83.2 2.2 convolution_convert_fusion.1
  92.7 6.9 %all-to-all-start.2 = ((bf16[16,4,4096]{2,1,0:T(4,128)(2,1)}), bf16[16,4,4096]{2,1,0:T(4,128)(2,1)}, u32[]{:S(2)}, u32[]{:S(2)}) async-start(bf16[16,4,4096]{2,1,0:T(4,128)(2,1)} %bitcast.67), calls=%async_computation.2 | async-start | bytes 1048576 | tf_op jit(solution)/shard_map/all_to_all | solution.py:25
  100.5 19.4 %all-gather.2.cloned.1.call-done = bf16[256,4096]{1,0:T(8,128)(2,1)} async-done(((bf16[32,4096]{1,0:T(8,128)(2,1)}), bf16[256,4096]{1,0:T(8,128)(2,1)}) %all-gather.2.cloned.1.call-update) | async-done | bytes 2097168 | tf_op jit(solution)/shard_map/all_gather | solution.py:54
  124.0 2.5 fusion.43
  131.0 8.7 %all-to-all-start.3 = ((f32[8,1,64]{2,1,0:T(1,128)}), f32[8,1,64]{2,1,0:T(1,128)S(1)}, u32[]{:S(2)}, u32[]{:S(2)}) async-start(f32[8,1,64]{2,1,0:T(1,128)} %broadcast_in_dim.44), calls=%async_computation.3 | async-start | bytes 8192 | tf_op jit(solution)/shard_map/all_to_all | solution.py:25
  140.3 7.9 %all-to-all-done.3 = f32[8,1,64]{2,1,0:T(1,128)S(1)} async-done(((f32[8,1,64]{2,1,0:T(1,128)}), f32[8,1,64]{2,1,0:T(1,128)S(1)}, u32[]{:S(2)}, u32[]{:S(2)}) %all-to-all-start.3) | async-done | bytes 2080 | tf_op jit(solution)/shard_map/all_to_all | solution.py:25
  149.5 19.4 %all_to_all.43 = f32[32,1,384]{2,1,0:T(1,128)} all-to-all(f32[32,1,384]{2,1,0:T(1,128)S(1)} %broadcast_in_dim.48), channel_id=1, replica_groups=mesh['z'=4,'yl'=2,'x'=8,'yh'=4,'c'=2] {'z','x'}, dimensions={0} | all-to-all | bytes 98304 | tf_op jit(solution)/shard_map/all_to_all | solution.py:25
  170.4 2.9 %fusion.2 = bf16[64,4096]{1,0:T(8,128)(2,1)} fusion(bf16[256,4096]{1,0:T(8,128)(2,1)} %all-gather.2.cloned.1.call-done, f32[256]{0:T(256)S(1)} %get-tuple-element.18, s32[256]{0:T(256)S(1)} %fusion.28, f32[64]{0:T(128)} %copy-done.13, f32[256]{0:T(256)S(1)} %bitcast.73, s32[64]{0:T(128)} %copy-done.12, f32[72,256]{1,0:T(8,128)S(1)} %fusion.41), kind=kOutput, calls=%fused_computation.6 | convolution fusion | flops 134938624 | bytes 2690560 | tf_op jit(solution)/shard_map/dot_general | solution.py:106
  175.4 4.4 %all-to-all-start.5 = ((bf16[16,4,4096]{2,1,0:T(4,128)(2,1)}), bf16[16,4,4096]{2,1,0:T(4,128)(2,1)}, u32[]{:S(2)}, u32[]{:S(2)}) async-start(bf16[16,4,4096]{2,1,0:T(4,128)(2,1)} %reshape.197), calls=%async_computation.5 | async-start | bytes 1048576 | tf_op jit(solution)/shard_map/all_to_all | solution.py:25
  179.9 14.3 %all-to-all-done.5 = bf16[16,4,4096]{2,1,0:T(4,128)(2,1)} async-done(((bf16[16,4,4096]{2,1,0:T(4,128)(2,1)}), bf16[16,4,4096]{2,1,0:T(4,128)(2,1)}, u32[]{:S(2)}, u32[]{:S(2)}) %all-to-all-start.5) | async-done | bytes 524320 | tf_op jit(solution)/shard_map/all_to_all | solution.py:25
  194.1 2.5 reshape.205
  199.9 2.7 fusion.7
  205.5 4.2 %convolution_convert_fusion = bf16[64,8192]{1,0:T(8,128)(2,1)} fusion(bf16[128,8192]{1,0:T(8,128)(2,1)S(1)} %copy-done, bf16[128,8192]{1,0:T(8,128)(2,1)} %fusion.6, bf16[64,8192]{1,0:T(8,128)(2,1)S(1)} %squeeze.17), kind=kOutput, calls=%fused_computation.4 | convolution fusion | flops 268976128 | bytes 6291456 | tf_op jit(solution)/shard_map/dot_general | solution.py:122
  214.2 2.7 collective-permute-start.2
  216.9 2.4 collective-permute-done.2
  219.2 2.8 %fusion.9 = bf16[8,32,16,128]{3,2,1,0:T(8,128)(2,1)} fusion(bf16[8,32,16,128]{3,2,1,0:T(8,128)(2,1)} %collective-permute-done.2, bf16[2,8,32,16,128]{4,3,2,1,0:T(8,128)(2,1)} %bitcast.62, s32[]{:T(128)S(6)} %select_n.79), kind=kLoop, calls=%fused_computation.21 | loop fusion | flops 2097152 | bytes 3145732 | tf_op jit(solution)/shard_map/convert_element_type | solution.py:135
  222.0 7.1 %all-to-all-start.6 = ((bf16[8,32,16,128]{3,2,1,0:T(8,128)(2,1)}), bf16[8,32,16,128]{3,2,1,0:T(8,128)(2,1)S(1)}, u32[]{:S(2)}, u32[]{:S(2)}) async-start(bf16[8,32,16,128]{3,2,1,0:T(8,128)(2,1)} %fusion.9), calls=%async_computation.6 | async-start | bytes 2097152 | tf_op jit(solution)/shard_map/all_to_all | solution.py:25
  231.7 12.3 %all-to-all-done.6 = bf16[8,32,16,128]{3,2,1,0:T(8,128)(2,1)S(1)} async-done(((bf16[8,32,16,128]{3,2,1,0:T(8,128)(2,1)}), bf16[8,32,16,128]{3,2,1,0:T(8,128)(2,1)S(1)}, u32[]{:S(2)}, u32[]{:S(2)}) %all-to-all-start.6) | async-done | bytes 1048608 | tf_op jit(solution)/shard_map/all_to_all | solution.py:25
  244.2 21.3 %all_to_all.44 = f32[32,24,128]{2,1,0:T(8,128)S(1)} all-to-all(f32[32,24,128]{2,1,0:T(8,128)S(1)} %concatenate.13), channel_id=1, replica_groups=mesh['z'=4,'yl'=2,'x'=8,'yh'=4,'c'=2] {'z','yl','yh'}, dimensions={0} | all-to-all | bytes 786432 | tf_op jit(solution)/shard_map/all_to_all | solution.py:25
  (89 shorter events, 46.3 us)
Async XLA Ops:
  7.2 76.0 %copy-start = (bf16[128,8192]{1,0:T(8,128)(2,1)S(1)}, bf16[128,8192]{1,0:T(8,128)(2,1)}, u32[]{:S(2)}) copy-start(bf16[128,8192]{1,0:T(8,128)(2,1)} %param.7) | copy-start | bytes 6291460
  8.9 28.4 %all-to-all-start = ((bf16[16,8,1024]{2,1,0:T(8,128)(2,1)}), bf16[16,8,1024]{2,1,0:T(8,128)(2,1)S(1)}, u32[]{:S(2)}, u32[]{:S(2)}) async-start(bf16[16,8,1024]{2,1,0:T(8,128)(2,1)} %bitcast.1), calls=%async_computation | async-start | bytes 524288 | tf_op jit(solution)/shard_map/all_to_all | solution.py:25
  23.7 96.2 %all-gather.2.cloned.1.call-start = ((), (), s32[]{:S(2)}) async-start(), calls=%async_computation.8 | async-start | bytes 2359296 | tf_op jit(solution)/shard_map/all_gather | solution.py:54
  37.3 32.2 %copy-start.6 = (bf16[16,8,1024]{2,1,0:T(8,128)(2,1)}, bf16[16,8,1024]{2,1,0:T(8,128)(2,1)S(1)}, u32[]{:S(2)}) copy-start(bf16[16,8,1024]{2,1,0:T(8,128)(2,1)S(1)} %all-to-all-done) | copy-start | bytes 786436
  67.5 4.7 %collective-permute-start = (bf16[2,4,64,1024]{3,2,1,0:T(8,128)(2,1)S(1)}, bf16[2,4,64,1024]{3,2,1,0:T(8,128)(2,1)}, u32[]{:S(2)}, u32[]{:S(2)}) collective-permute-start(bf16[2,4,64,1024]{3,2,1,0:T(8,128)(2,1)S(1)} %bitcast.63), channel_id=1, source_target_pairs={{0,1},{1,0},{2,3},{3,2},{4,5},{5,4},{6,7},{7,6},{8,9},{9,8},{10,11... | collective-permute-start | bytes 3145736 | tf_op jit(solution)/shard_map/ppermute | solution.py:33
  83.2 2.2 copy-start.5
  85.5 1.7 copy-start.7
  86.6 1.9 copy-start.1
  87.1 1.4 copy-start.10
  92.7 29.3 %all-to-all-start.2 = ((bf16[16,4,4096]{2,1,0:T(4,128)(2,1)}), bf16[16,4,4096]{2,1,0:T(4,128)(2,1)}, u32[]{:S(2)}, u32[]{:S(2)}) async-start(bf16[16,4,4096]{2,1,0:T(4,128)(2,1)} %bitcast.67), calls=%async_computation.2 | async-start | bytes 1048576 | tf_op jit(solution)/shard_map/all_to_all | solution.py:25
  100.5 29.2 %copy-start.12 = (s32[64]{0:T(128)}, s32[64]{0:T(128)S(1)}, u32[]{:S(2)}) copy-start(s32[64]{0:T(128)S(1)} %select_n.74) | copy-start | bytes 772
  126.5 3.2 %collective-permute-start.1 = (f32[72,256]{1,0:T(8,128)S(1)}, f32[72,256]{1,0:T(8,128)S(1)}, u32[]{:S(2)}, u32[]{:S(2)}) collective-permute-start(f32[72,256]{1,0:T(8,128)S(1)} %pad_maximum_fusion.1), channel_id=1, source_target_pairs={{0,1},{1,0},{2,3},{3,2},{4,5},{5,4},{6,7},{7,6},{8,9},{9,8},{10,11... | collective-permute-start | bytes 221192 | tf_op jit(solution)/shard_map/ppermute | solution.py:33
  131.0 17.2 %all-to-all-start.3 = ((f32[8,1,64]{2,1,0:T(1,128)}), f32[8,1,64]{2,1,0:T(1,128)S(1)}, u32[]{:S(2)}, u32[]{:S(2)}) async-start(f32[8,1,64]{2,1,0:T(1,128)} %broadcast_in_dim.44), calls=%async_computation.3 | async-start | bytes 8192 | tf_op jit(solution)/shard_map/all_to_all | solution.py:25
  148.2 1.3 copy-start.13
  169.8 5.7 %copy-start.9 = (f32[384]{0:T(512)}, f32[384]{0:T(512)S(1)}, u32[]{:S(2)}) copy-start(f32[384]{0:T(512)S(1)} %reduce_sum.153) | copy-start | bytes 4612
  175.4 18.7 %all-to-all-start.5 = ((bf16[16,4,4096]{2,1,0:T(4,128)(2,1)}), bf16[16,4,4096]{2,1,0:T(4,128)(2,1)}, u32[]{:S(2)}, u32[]{:S(2)}) async-start(bf16[16,4,4096]{2,1,0:T(4,128)(2,1)} %reshape.197), calls=%async_computation.5 | async-start | bytes 1048576 | tf_op jit(solution)/shard_map/all_to_all | solution.py:25
  199.8 3.5 %copy-start.2 = (f32[128,8192]{1,0:T(8,128)S(1)}, f32[128,8192]{1,0:T(8,128)}, u32[]{:S(2)}) copy-start(f32[128,8192]{1,0:T(8,128)} %copy-done.1) | copy-start | bytes 12582916
  199.8 3.5 %copy-start.8 = (f32[8192]{0:T(1024)S(1)}, f32[8192]{0:T(1024)}, u32[]{:S(2)}) copy-start(f32[8192]{0:T(1024)} %param.9) | copy-start | bytes 98308
  199.8 3.4 %copy-start.11 = (f32[128]{0:T(128)S(1)}, f32[128]{0:T(128)}, u32[]{:S(2)}) copy-start(f32[128]{0:T(128)} %copy-done.10) | copy-start | bytes 1540
  199.8 3.4 %copy-start.14 = (f32[128]{0:T(128)S(1)}, f32[128]{0:T(128)}, u32[]{:S(2)}) copy-start(f32[128]{0:T(128)} %get-tuple-element.19) | copy-start | bytes 1540
  209.7 2.1 copy-start.4
  212.6 1.4 copy-start.3
  214.2 5.1 %collective-permute-start.2 = (bf16[8,32,16,128]{3,2,1,0:T(8,128)(2,1)S(1)}, bf16[8,32,16,128]{3,2,1,0:T(8,128)(2,1)}, u32[]{:S(2)}, u32[]{:S(2)}) collective-permute-start(bf16[8,32,16,128]{3,2,1,0:T(8,128)(2,1)S(1)} %dynamic-slice_bitcast_fusion), channel_id=1, source_target_pairs={{0,1},{1,0},{2,3},{3,2},{4,5},{5,4},{6,7},{7,6},{8,9},{9,8},{10,11... | collective-permute-start | bytes 3145736 | tf_op jit(solution)/shard_map/ppermute | solution.py:33
  222.0 22.0 %all-to-all-start.6 = ((bf16[8,32,16,128]{3,2,1,0:T(8,128)(2,1)}), bf16[8,32,16,128]{3,2,1,0:T(8,128)(2,1)S(1)}, u32[]{:S(2)}, u32[]{:S(2)}) async-start(bf16[8,32,16,128]{3,2,1,0:T(8,128)(2,1)} %fusion.9), calls=%async_computation.6 | async-start | bytes 2097152 | tf_op jit(solution)/shard_map/all_to_all | solution.py:25
Sparse Core Ops, SparseCore 0:
  69.6 50.2 all-gather.1

commit v2 on v1

v2 whole, which is shorter than its diff:
```python
import functools

import jax
import jax.numpy as jnp
from jax import lax
from jax.experimental import pallas as pl
from jax.experimental.pallas import tpu as pltpu
from jax.sharding import Mesh
from jax.sharding import PartitionSpec as P

LEN = 32


adapter_scale_factor = 0.25
inv_temp = 20.0
norm_eps = 1e-05

AXES = ("z", "yl", "x", "yh", "c")
SIZES = (4, 2, 8, 4, 2)
MIB = 1 << 20
f32, bf16 = jnp.float32, jnp.bfloat16


def dot(left, right):
    return jnp.dot(left, right, preferred_element_type=f32)


def dot_rows(left, right):
    return lax.dot_general(left, right, (((1,), (1,)), ((), ())), preferred_element_type=f32)


def exchange(blocks, axes):
    return lax.all_to_all(blocks, axes, 0, 0, tiled=True)


def swap_cores(value):
    return lax.ppermute(value, "c", [(0, 1), (1, 0)])


def call(kernel, outs, args, scratch=(), scalars=0, flops=0):
    size = sum(a.size * a.dtype.itemsize for a in list(args[scalars:]) + list(outs))
    spare = [pltpu.VMEM(shape, kind) for shape, kind in scratch]
    spare_size = sum(a.size * a.dtype.itemsize for a in map(shape_of, scratch))
    return pl.pallas_call(
        kernel,
        out_shape=outs,
        in_specs=[pl.BlockSpec(memory_space=pltpu.SMEM)] * scalars
        + [pl.BlockSpec(memory_space=pltpu.VMEM)] * (len(args) - scalars),
        out_specs=[pl.BlockSpec(memory_space=pltpu.VMEM)] * len(outs),
        scratch_shapes=spare,
        compiler_params=pltpu.CompilerParams(
            vmem_limit_bytes=min(48 * MIB, size + spare_size + 12 * MIB)
        ),
        cost_estimate=pl.CostEstimate(flops=flops, bytes_accessed=size, transcendentals=0),
    )(*args)


def shape_of(pair):
    return jax.ShapeDtypeStruct(*pair)


def forward(nyh, nc, in_ref, frozen_ref, gain_ref, mats_ref,
            latent_ref, hidden_ref, inv_ref, unit_ref, length_ref, send_ref, part_ref):
    slices, both, feats = mats_ref.shape
    rank = both // 2
    tokens, width = in_ref.shape
    queries = tokens // LEN
    acc = jnp.zeros((tokens, rank), f32)
    acc_t = jnp.zeros((rank, tokens), f32)
    for f in range(slices):
        part = in_ref[:, f * feats:(f + 1) * feats]
        down = mats_ref[f, :rank]
        acc += dot_rows(part, down)
        acc_t += dot_rows(down, part)
    latent = acc.astype(bf16)
    latent_ref[...] = acc_t.astype(bf16)
    squares = jnp.zeros((tokens, 1), f32)
    for f in range(slices):
        at = slice(f * feats, (f + 1) * feats)
        hidden = frozen_ref[:, at].astype(f32) + adapter_scale_factor * dot(
            latent, mats_ref[f, rank:]
        )
        hidden_ref[:, at] = hidden
        squares += jnp.sum(hidden * hidden, axis=1, keepdims=True)
    inv = lax.rsqrt(squares / width + norm_eps)
    inv_ref[...] = jnp.broadcast_to(inv, inv_ref.shape)
    total = jnp.zeros((queries, 1), f32)
    for f in range(slices):
        at = slice(f * feats, (f + 1) * feats)
        scaled = hidden_ref[:, at] * inv
        for q in range(queries):
            one = jnp.sum(scaled[q * LEN:(q + 1) * LEN], axis=0, keepdims=True)
            unit_ref[q:q + 1, at] = one * gain_ref[:, at] / LEN
        pooled = unit_ref[:, at]
        total += jnp.sum(pooled * pooled, axis=1, keepdims=True)
    length = jnp.sqrt(total)
    length_ref[...] = jnp.broadcast_to(length, length_ref.shape)
    for f in range(slices):
        at = slice(f * feats, (f + 1) * feats)
        unit = unit_ref[:, at] / length
        unit_ref[:, at] = unit
        part_ref[f % nc, f // nc * queries:(f // nc + 1) * queries, :] = unit
    for c in range(nc):
        rows = part_ref[c].astype(bf16)
        for y in range(send_ref.shape[0] // nc):
            send_ref[y * nc + c] = rows


def row_index(shape):
    return lax.broadcasted_iota(jnp.int32, shape, 0)


def score(nyh, query_ref, block_ref, out_ref):
    ring, rows, feats = query_ref.shape
    queries = rows // nyh
    columns = block_ref.shape[0]
    query = query_ref[...].reshape(ring * rows, feats)
    mine = row_index((ring * rows, columns)) // queries % nyh
    total = jnp.zeros((ring * rows, columns), f32)
    gram = jnp.zeros((columns, columns), f32)
    for k in range(nyh):
        part = block_ref[:, k * feats:(k + 1) * feats]
        total = jnp.where(mine == k, dot_rows(query, part), total)
        gram += dot_rows(part, part)
    total = total.reshape(ring, rows // 8, 8, columns)
    total = functools.reduce(jnp.add, [total[:, i] for i in range(rows // 8)])
    total = total.reshape(ring * 8, columns)
    count = ring * 8
    upper = row_index(total.shape) % 8 < 4
    total += jnp.where(upper, pltpu.roll(total, count - 4, 0), pltpu.roll(total, 4, 0))
    same = row_index(gram.shape) == lax.broadcasted_iota(jnp.int32, gram.shape, 1)
    norms = jnp.sum(jnp.where(same, gram, 0.0), axis=0, keepdims=True)
    out_ref[:count] = total
    out_ref[count:] = jnp.broadcast_to(norms, (8, columns))


def across(row):
    n = row.size
    return jnp.transpose(jnp.broadcast_to(row, (n, n)))


def widen(row, lanes):
    if row.shape[1] == lanes:
        return row
    return jnp.concatenate([row, jnp.zeros((1, lanes - row.shape[1]), f32)], axis=1)


def exponentials(members, iy_ref, own_ref, other_ref, onehot_ref, expo_ref, aux_ref, send_ref):
    count = expo_ref.shape[0]
    columns = expo_ref.shape[1]
    inv_norm = 1.0 / jnp.sqrt(own_ref[count:count + 1] + other_ref[count:count + 1])
    scores = inv_temp * ((own_ref[:count] + other_ref[:count]) * inv_norm)
    expo = jnp.exp(scores - inv_temp)
    expo_ref[...] = expo
    hits = 0.5 * jnp.sum(scores * onehot_ref[...])
    aux_ref[0:1] = inv_norm
    aux_ref[1:2] = jnp.full((1, columns), hits)
    row = across(jnp.sum(expo, axis=1, keepdims=True))[0:1]
    row = widen(row, send_ref.shape[1])
    col = widen(0.5 * jnp.sum(expo, axis=0, keepdims=True), send_ref.shape[1])
    same_y = row_index(send_ref.shape) // members == iy_ref[0]
    send_ref[...] = jnp.where(same_y, col, row)


def weigh(nyh, members, iy_ref, ixz_ref, expo_ref, aux_ref, onehot_ref, sums_ref, block_ref,
          out_ref, loss_ref, total_ref):
    count, columns = expo_ref.shape
    ring, rows, feats = out_ref.shape
    queries = rows // nyh
    sums = sums_ref[...]
    peer = row_index(sums.shape)
    same_y = peer // members == iy_ref[0]
    col = jnp.sum(jnp.where(same_y, sums, 0.0), axis=0, keepdims=True)[:, :columns]
    same_xz = jnp.logical_and(peer % members == ixz_ref[0], jnp.logical_not(same_y))
    rest = jnp.sum(jnp.where(same_xz, sums, 0.0), axis=0, keepdims=True)[:, :count]
    expo = expo_ref[...]
    row = across(rest)[:, :1] + jnp.sum(expo, axis=1, keepdims=True)
    peers = sums.shape[0]
    loss = (
        0.5 * jnp.sum(jnp.log(row), axis=0, keepdims=True) / (peers // members)
        + jnp.sum(jnp.log(col), axis=1, keepdims=True) / members
        - 2.0 * aux_ref[1:2, 0:1]
    )
    loss_ref[...] = jnp.broadcast_to(loss, loss_ref.shape)
    weights = 0.5 * (expo / row + expo / col) - onehot_ref[...]
    weights = (weights * aux_ref[0:1]).reshape(ring, 1, 8, columns)
    weights = jnp.broadcast_to(weights, (ring, rows // 8, 8, columns))
    weights = weights.reshape(ring * rows, columns).astype(bf16)
    mine = row_index((ring * rows, feats)) // queries % nyh
    for k in range(nyh):
        part = inv_temp * dot(weights, block_ref[:, k * feats:(k + 1) * feats])
        if k == 0:
            total_ref[...] = part
        else:
            total_ref[...] = jnp.where(mine == k, part, total_ref[...])
    out_ref[...] = total_ref[...].astype(bf16).reshape(out_ref.shape)


def backward(nyh, nc, core_ref, got_ref, unit_ref, length_ref, inv_ref, hidden_ref, gain_ref,
             in_ref, mats_ref, latent_ref, keep_ref, send_ref, grad_ref, scaled_ref, up_ref, hg_ref):
    slices, both, feats = mats_ref.shape
    rank = both // 2
    tokens, width = in_ref.shape
    queries = tokens // LEN
    nx, _, pair_rows, cols = keep_ref.shape
    out_rows = pair_rows // 2
    for c in range(nc):
        total = got_ref[c].astype(f32)
        for y in range(1, got_ref.shape[0] // nc):
            total += got_ref[y * nc + c].astype(f32)
        grad_ref[c] = total
    inner = jnp.zeros((queries, 1), f32)
    for f in range(slices):
        at = slice(f * feats, (f + 1) * feats)
        grad = grad_ref[f % nc, f // nc * queries:(f // nc + 1) * queries, :]
        inner += jnp.sum(unit_ref[:, at] * grad, axis=1, keepdims=True)
    length = length_ref[:, :1]
    mean = [jnp.zeros((LEN, 1), f32) for q in range(queries)]
    for f in range(slices):
        at = slice(f * feats, (f + 1) * feats)
        grad = grad_ref[f % nc, f // nc * queries:(f // nc + 1) * queries, :]
        pooled_grad = (grad - unit_ref[:, at] * inner) / length
        scaled_ref[:, at] = pooled_grad / LEN * gain_ref[:, at]
        for q in range(queries):
            product = hidden_ref[q * LEN:(q + 1) * LEN, at] * scaled_ref[q:q + 1, at]
            mean[q] += jnp.sum(product, axis=1, keepdims=True)
    inv = inv_ref[:, :1]
    factor = inv * inv * inv * (jnp.concatenate(mean, axis=0) / width)
    latent_t = latent_ref[...]
    acc = jnp.zeros((rank, tokens), f32)
    for f in range(slices):
        at = slice(f * feats, (f + 1) * feats)
        for q in range(queries):
            of = slice(q * LEN, (q + 1) * LEN)
            hg_ref[of] = (
                inv[of] * scaled_ref[q:q + 1, at] - hidden_ref[of, at] * factor[of]
            ).astype(bf16)
        hidden_grad = hg_ref[...]
        acc += dot_rows(mats_ref[f, rank:], hidden_grad)
        up_ref[:, at] = adapter_scale_factor * dot(latent_t, hidden_grad)
    latent_grad = (adapter_scale_factor * acc).astype(bf16)
    first = core_ref[0] == 0
    for f in range(slices):
        down = dot(latent_grad, in_ref[:, f * feats:(f + 1) * feats])
        for x in range(nx):
            lanes = slice(x * cols, (x + 1) * cols)
            spot = slice(f * feats + x * cols, f * feats + (x + 1) * cols)
            for yh in range(nyh):
                tiles = []
                for c in range(nc):
                    of = slice((yh * nc + c) * out_rows, (yh * nc + c + 1) * out_rows)
                    tiles.append(
                        jnp.concatenate([down[of, lanes], up_ref[of, spot]], axis=0).astype(bf16)
                    )
                keep_ref[x, f * nyh + yh] = jnp.where(first, tiles[0], tiles[1])
                send_ref[x, f * nyh + yh] = jnp.where(first, tiles[1], tiles[0])


def join(keep_ref, got_ref, loss_ref, out_ref):
    nx, blocks, rows, cols = keep_ref.shape
    high = loss_ref[0:1].astype(bf16).astype(f32)
    rest = loss_ref[0:1] - high
    middle = rest.astype(bf16).astype(f32)
    low = rest - middle
    at = row_index((rows, loss_ref.shape[1]))
    parts = jnp.where(at == 0, high, jnp.where(at == 1, middle, jnp.where(at == 2, low, 0.0)))
    parts = jnp.concatenate([parts] * (cols // loss_ref.shape[1]), axis=1).astype(bf16)
    for x in range(nx):
        out_ref[x, :blocks] = (
            keep_ref[x].astype(f32) + got_ref[x].astype(f32)
        ).astype(bf16)
        out_ref[x, blocks] = parts


def add_line(got_ref, out_ref):
    total = got_ref[0].astype(f32)
    for x in range(1, got_ref.shape[0]):
        total += got_ref[x].astype(f32)
    blocks, _, cols = out_ref.shape
    rows = got_ref.shape[2]
    loss = jnp.sum(total[blocks], axis=0, keepdims=True)
    out_ref[:, :rows] = total[:blocks]
    out_ref[:, rows:] = jnp.broadcast_to(loss[None], (blocks, 8, cols))


def shards(sizes, adapter_in, frozen, gain, adapter_a, adapter_up_matrix, passages, positive):
    nz, nyl, nx, nyh, nc = sizes
    ny = nyl * nyh
    iz, iyl, ix, iyh, ic = (lax.axis_index(axis) for axis in AXES)
    rank = adapter_up_matrix.shape[0]
    feats = passages.shape[1]
    half = nyh * feats
    width = half * nc
    tokens = adapter_in.shape[0]
    queries = tokens // LEN
    group = passages.shape[0]
    rows = group // nyh
    ring = ny * nc
    members = nz * nx
    shape = jax.ShapeDtypeStruct
    gain = gain.reshape(1, width)

    mine = jnp.concatenate([adapter_a.T, adapter_up_matrix], axis=0)
    mats = lax.all_gather(mine, ("yh", "c"), axis=0, tiled=False)

    sent = jnp.broadcast_to(passages.reshape(1, nyh, rows, feats), (nz, nyh, rows, feats))
    got = exchange(sent.reshape(nz * nyh, rows, feats), ("z", "yh"))
    got = got.reshape(nz, nyh, rows, feats).transpose(0, 2, 1, 3).reshape(nz * rows, half)
    got = jnp.broadcast_to(got[None], (nx, nz * rows, half))
    block = exchange(got, "x").reshape(nx * nz * rows, half)
    columns = block.shape[0]

    latent_t, hidden, inv, unit, length, sent = call(
        functools.partial(forward, nyh, nc),
        [
            shape((rank, tokens), bf16),
            shape((tokens, width), f32),
            shape((tokens, 128), f32),
            shape((queries, width), f32),
            shape((queries, 128), f32),
            shape((ring, nyh * queries, feats), bf16),
        ],
        [adapter_in, frozen, gain, mats],
        scratch=[((nc, nyh * queries, feats), f32)],
        flops=6 * tokens * rank * width,
    )
    query = exchange(sent, ("yl", "yh", "c"))

    count = ring * 8
    at = lax.iota(jnp.int32, columns)
    at_x, at_z, at_row = at // (nz * rows), at // rows % nz, at % rows
    passage_id = ((at_z * nyl + iyl) * nx + at_x) * group + iyh * rows + at_row
    own_pos = jnp.where(
        lax.iota(jnp.int32, nyl)[:, None] == iyl, positive[None, :], -1
    ).reshape(ring, 1, queries)
    own_pos = jnp.broadcast_to(own_pos, (ring, 8 // queries, queries)).reshape(count)
    onehot = (own_pos[:, None] == passage_id[None, :]).astype(f32)
    iy = (iyl * nyh + iyh).astype(jnp.int32).reshape(1)
    ixz = (iz * nx + ix).astype(jnp.int32).reshape(1)

    (own,) = call(
        functools.partial(score, nyh),
        [shape((count + 8, columns), f32)],
        [query, block],
        flops=4 * ring * nyh * queries * columns * half,
    )
    other = swap_cores(own)
    expo, aux, sent = call(
        functools.partial(exponentials, members),
        [shape((count, columns), f32), shape((8, columns), f32), shape((ny * members, max(columns, count)), f32)],
        [iy, own, other, onehot],
        scalars=1,
    )
    sums = exchange(sent, ("yl", "yh", "z", "x"))
    sent, loss = call(
        functools.partial(weigh, nyh, members),
        [shape((ring, nyh * queries, feats), bf16), shape((8, 128), f32)],
        [iy, ixz, expo, aux, onehot, sums, block],
        scratch=[((ring * nyh * queries, feats), f32)],
        scalars=2,
        flops=2 * ring * nyh * queries * columns * half,
    )
    got = exchange(sent, ("yl", "yh", "c"))

    out_rows = rank // (nyh * nc)
    cols = width // (nz * nyl * nx)
    blocks = nz * ny
    keep, send = call(
        functools.partial(backward, nyh, nc),
        [shape((nx, blocks, 2 * out_rows, cols), bf16)] * 2,
        [ic.astype(jnp.int32).reshape(1), got, unit, length, inv, hidden, gain, adapter_in, mats, latent_t],
        scratch=[
            ((nc, nyh * queries, feats), f32),
            ((queries, width), f32),
            ((rank, width), f32),
            ((tokens, feats), bf16),
        ],
        scalars=1,
        flops=6 * tokens * rank * width,
    )
    (chip,) = call(
        join,
        [shape((nx, blocks + 1, 2 * out_rows, cols), bf16)],
        [keep, swap_cores(send), loss],
    )
    (line,) = call(
        add_line, [shape((blocks, 2 * out_rows + 8, cols), f32)], [exchange(chip, "x")]
    )
    last = jnp.sum(exchange(line, ("z", "yl", "yh")), axis=0)
    adapter_grads = last[: 2 * out_rows].reshape(2, out_rows, cols)
    total_pairs = group * nz * nyl * nx
    loss = last[2 * out_rows, 0] / (2.0 * total_pairs) + inv_temp
    return (adapter_grads, loss)


def build(mesh, sizes):
    split = Mesh(mesh.devices.reshape(sizes), AXES)
    dp, fsdp = ("z", "yl", "x"), ("yh", "c")
    placed = (
        P(AXES, None),
        P(AXES, None),
        P(),
        P(fsdp, None),
        P(None, fsdp),
        P(dp, fsdp),
        P(dp),
    )
    return jax.shard_map(
        lambda *args: shards(sizes, *args),
        mesh=split,
        in_specs=placed,
        out_specs=(P(None, fsdp, dp), P()),
        check_vma=False,
    )


def solution(mesh):
    return build(mesh, SIZES)
```

time: 277 us -> 231 us (0.83)
  the two profiles are of different devices: /device:TPU:8 before, /device:TPU:16 now
where the time goes in v2:
time: 231 us; the launch traced here: 230 us
  waiting for transfers between devices  92.4 us (40%)
  starting transfers between devices  49.3 us (21%)
  blocking collectives  41.5 us (18%)
  between operations  15.9 us (7%)
  local copies, waits for them, and re-layouts  14.9 us (6%)
  Pallas kernels  14.1 us (6%)
    all_to_all x5, waiting for transfers between devices, exchange(): return lax.all_to_all(blocks, axes, 0, 0, tiled=True)  60.8 us
    all_to_all x5, starting transfers between devices, exchange(): return lax.all_to_all(blocks, axes, 0, 0, tiled=True)  44.3 us
    all_to_all x2, blocking collectives, exchange(): return lax.all_to_all(blocks, axes, 0, 0, tiled=True)  41.5 us
    all_gather x1, waiting for transfers between devices, shards(): mats = lax.all_gather(mine, ('yh', 'c'), axis=0, tiled=False)  28.2 us
    pallas_call x7, Pallas kernels, call(): pl.pallas_call(kernel, out_shape=outs, in_specs=[pl.BlockSpec(memory_spac...  14.1 us
    unnamed x17, local copies, waits for them, and re-layouts  8.94 us
    ppermute x2, starting transfers between devices, swap_cores(): return lax.ppermute(value, 'c', [(0, 1), (1, 0)])  4.96 us
  transfers between devices with their start and end apart: 8, of which 8 were waited for; matrix products, arithmetic and copies ran while one was open for 2% of the time, Pallas kernels for 2%

profile of v2, /device:TPU:16, one launch (start us, length us, event | category | flops | bytes accessed | tf_op | source)
XLA Modules:
  0.0 230.0 jit_solution(13109310566549598172)
XLA Ops:
  8.7 15.9 %all-to-all-start.1 = ((bf16[16,8,1024]{2,1,0:T(8,128)(2,1)}), bf16[16,8,1024]{2,1,0:T(8,128)(2,1)S(1)}, u32[]{:S(2)}, u32[]{:S(2)}) async-start(bf16[16,8,1024]{2,1,0:T(8,128)(2,1)} %bitcast.7), calls=%async_computation.1 | async-start | bytes 524288 | tf_op jit(solution)/shard_map/all_to_all | solution.py:33
  24.7 1.7 pad_maximum_fusion
  26.4 12.2 %all-to-all-done.1 = bf16[16,8,1024]{2,1,0:T(8,128)(2,1)S(1)} async-done(((bf16[16,8,1024]{2,1,0:T(8,128)(2,1)}), bf16[16,8,1024]{2,1,0:T(8,128)(2,1)S(1)}, u32[]{:S(2)}, u32[]{:S(2)}) %all-to-all-start.1) | async-done | bytes 262176 | tf_op jit(solution)/shard_map/all_to_all | solution.py:33
  38.6 1.6 broadcast_in_dim.53
  40.2 4.5 %all-to-all-start.2 = ((bf16[8,32,4096]{2,1,0:T(8,128)(2,1)}), bf16[8,32,4096]{2,1,0:T(8,128)(2,1)}, u32[]{:S(2)}, u32[]{:S(2)}) async-start(bf16[8,32,4096]{2,1,0:T(8,128)(2,1)} %broadcast_in_dim.53), calls=%async_computation.2 | async-start | bytes 4194304 | tf_op jit(solution)/shard_map/all_to_all | solution.py:33
  44.7 28.2 %all-gather.3.cloned.1.call-done = bf16[1024,1024]{1,0:T(8,128)(2,1)} async-done(((bf16[128,1024]{1,0:T(8,128)(2,1)}), bf16[1024,1024]{1,0:T(8,128)(2,1)}) %all-gather.3.cloned.1.call-update) | async-done | bytes 2097168 | tf_op jit(solution)/shard_map/all_gather | solution.py:304
  76.1 4.3 %shard_map.86 = (bf16[64,128]{1,0:T(8,128)(2,1)S(1)}, f32[128,8192]{1,0:T(8,128)S(1)}, f32[128,128]{1,0:T(8,128)S(1)}, f32[4,8192]{1,0:T(4,128)S(1)}, f32[4,128]...) custom-call(bf16[128,8192]{1,0:T(8,128)(2,1)S(1)} %copy-done, bf16[128,8192]{1,0:T(8,128)(2,1)S(1)} %copy-done.5, ...), custom_call_target="tpu_custom_call" | custom-call | flops 402653184 | bytes 11257856 | tf_op jit(solution)/shard_map/pallas_call | solution.py:44
  80.4 1.9 copy-done.3
  82.4 3.0 %all-to-all-done.2 = bf16[8,32,4096]{2,1,0:T(8,128)(2,1)} async-done(((bf16[8,32,4096]{2,1,0:T(8,128)(2,1)}), bf16[8,32,4096]{2,1,0:T(8,128)(2,1)}, u32[]{:S(2)}, u32[]{:S(2)}) %all-to-all-start.2) | async-done | bytes 2097184 | tf_op jit(solution)/shard_map/all_to_all | solution.py:33
  85.3 6.2 %all-to-all-start = ((bf16[16,16,1024]{2,1,0:T(8,128)(2,1)}), bf16[16,16,1024]{2,1,0:T(8,128)(2,1)S(1)}, u32[]{:S(2)}, u32[]{:S(2)}) async-start(bf16[16,16,1024]{2,1,0:T(8,128)(2,1)} %get-tuple-element.15), calls=%async_computation | async-start | bytes 1048576 | tf_op jit(solution)/shard_map/all_to_all | solution.py:33
  92.2 15.2 %all-to-all-done.query_ref = bf16[16,16,1024]{2,1,0:T(8,128)(2,1)S(1)} async-done(((bf16[16,16,1024]{2,1,0:T(8,128)(2,1)}), bf16[16,16,1024]{2,1,0:T(8,128)(2,1)S(1)}, u32[]{:S(2)}, u32[]{:S(2)}) %all-to-all-start) | async-done | bytes 524320 | tf_op jit(solution)/shard_map/all_to_all | solution.py:33
  107.4 2.9 %shard_map.87.own_ref = f32[136,256]{1,0:T(8,128)S(1)} custom-call(bf16[16,16,1024]{2,1,0:T(8,128)(2,1)S(1)} %all-to-all-done.query_ref, bf16[256,4096]{1,0:T(8,128)(2,1)} %bitcast.11.block_ref), custom_call_target="tpu_custom_call" | custom-call | flops 1073741824 | bytes 2760704 | tf_op jit(solution)/shard_map/pallas_call | solution.py:44
  110.3 2.0 collective-permute-start
  114.7 12.4 %all-to-all-start.3 = ((f32[256,1,256]{2,1,0:T(1,128)}), f32[256,1,256]{2,1,0:T(1,128)S(1)}, u32[]{:S(2)}, u32[]{:S(2)}) async-start(f32[256,1,256]{2,1,0:T(1,128)} %copy.15), calls=%async_computation.3 | async-start | bytes 524288 | tf_op jit(solution)/shard_map/all_to_all | solution.py:33
  127.1 15.6 %all-to-all-done.3 = f32[256,1,256]{2,1,0:T(1,128)S(1)} async-done(((f32[256,1,256]{2,1,0:T(1,128)}), f32[256,1,256]{2,1,0:T(1,128)S(1)}, u32[]{:S(2)}, u32[]{:S(2)}) %all-to-all-start.3) | async-done | bytes 262176 | tf_op jit(solution)/shard_map/all_to_all | solution.py:33
  142.7 3.5 %shard_map.89 = (bf16[16,16,1024]{2,1,0:T(8,128)(2,1)}, f32[8,128]{1,0:T(8,128)S(1)}) custom-call(s32[1]{0:T(128)} %bitcast.1.iy_ref, s32[1]{0:T(128)} %bitcast.2.ixz_ref, f32[128,256]{1,0:T(8,128)S(1)} %get-tuple-element.16.expo_ref, f32[8,256]{1,0:T(8,128)S(1)} %get-tuple-element.17.aux_ref, f32[128,256]{1,0:T(8,128)S(1)} %compare_convert_fusion.onehot_ref, ...), custom_call_target="tpu_custom_call" | custom-call | flops 536870912 | bytes 3158016 | tf_op jit(solution)/shard_map/pallas_call | solution.py:44
  146.2 5.4 %all-to-all-start.4 = ((bf16[16,16,1024]{2,1,0:T(8,128)(2,1)}), bf16[16,16,1024]{2,1,0:T(8,128)(2,1)S(1)}, u32[]{:S(2)}, u32[]{:S(2)}) async-start(bf16[16,16,1024]{2,1,0:T(8,128)(2,1)} %get-tuple-element.19), calls=%async_computation.4 | async-start | bytes 1048576 | tf_op jit(solution)/shard_map/all_to_all | solution.py:33
  151.6 14.8 %all-to-all-done.4.got_ref = bf16[16,16,1024]{2,1,0:T(8,128)(2,1)S(1)} async-done(((bf16[16,16,1024]{2,1,0:T(8,128)(2,1)}), bf16[16,16,1024]{2,1,0:T(8,128)(2,1)S(1)}, u32[]{:S(2)}, u32[]{:S(2)}) %all-to-all-start.4) | async-done | bytes 524320 | tf_op jit(solution)/shard_map/all_to_all | solution.py:33
  168.0 2.2 copy-done.4
  170.2 2.9 %shard_map.90 = (bf16[8,32,16,128]{3,2,1,0:T(8,128)(2,1)S(1)}, bf16[8,32,16,128]{3,2,1,0:T(8,128)(2,1)S(1)}) custom-call(s32[1]{0:T(128)} %bitcast.core_ref, bf16[16,16,1024]{2,1,0:T(8,128)(2,1)S(1)} %all-to-all-done.4.got_ref, f32[4,8192]{1,0:T(4,128)S(1)} %get-tuple-element.20.unit_ref, f32[4,128]{1,0:T(4,128)S(1)} %get-tuple-element.21.length_ref, ...), custom_call_target="tpu_custom_call" | custom-call | flops 402653184 | bytes 11257856 | tf_op jit(solution)/shard_map/pallas_call | solution.py:44
  173.1 2.9 %collective-permute-start.1 = (bf16[8,32,16,128]{3,2,1,0:T(8,128)(2,1)S(1)}, bf16[8,32,16,128]{3,2,1,0:T(8,128)(2,1)S(1)}, u32[]{:S(2)}, u32[]{:S(2)}) collective-permute-start(bf16[8,32,16,128]{3,2,1,0:T(8,128)(2,1)S(1)} %get-tuple-element.26), channel_id=1, source_target_pairs={{0,1},{1,0},{2,3},{3,2},{4,5},{5,4},{6,7},{7,6},{8,9},{9,8},{10,11... | collective-permute-start | bytes 3145736 | tf_op jit(solution)/shard_map/ppermute | solution.py:37
  176.0 2.3 collective-permute-done.1.got_ref
  178.5 19.5 %all_to_all.41.got_ref = bf16[8,33,16,128]{3,2,1,0:T(8,128)(2,1)S(1)} all-to-all(bf16[8,33,16,128]{3,2,1,0:T(8,128)(2,1)S(1)} %shard_map.91), channel_id=1, replica_groups=mesh['z'=4,'yl'=2,'x'=8,'yh'=4,'c'=2] {'x'}, dimensions={0} | all-to-all | bytes 2162688 | tf_op jit(solution)/shard_map/all_to_all | solution.py:33
  198.2 22.0 %all_to_all.42 = f32[32,24,128]{2,1,0:T(8,128)S(1)} all-to-all(f32[32,24,128]{2,1,0:T(8,128)S(1)} %shard_map.92), channel_id=1, replica_groups=mesh['z'=4,'yl'=2,'x'=8,'yh'=4,'c'=2] {'z','yl','yh'}, dimensions={0} | all-to-all | bytes 786432 | tf_op jit(solution)/shard_map/all_to_all | solution.py:33
  (39 shorter events, 11.0 us)
Async XLA Ops:
  8.7 29.9 %all-to-all-start.1 = ((bf16[16,8,1024]{2,1,0:T(8,128)(2,1)}), bf16[16,8,1024]{2,1,0:T(8,128)(2,1)S(1)}, u32[]{:S(2)}, u32[]{:S(2)}) async-start(bf16[16,8,1024]{2,1,0:T(8,128)(2,1)} %bitcast.7), calls=%async_computation.1 | async-start | bytes 524288 | tf_op jit(solution)/shard_map/all_to_all | solution.py:33
  24.7 48.3 %all-gather.3.cloned.1.call-start = ((), (), s32[]{:S(2)}) async-start(), calls=%async_computation.7 | async-start | bytes 2359296 | tf_op jit(solution)/shard_map/all_gather | solution.py:304
  40.2 32.7 %copy-start = (bf16[128,8192]{1,0:T(8,128)(2,1)S(1)}, bf16[128,8192]{1,0:T(8,128)(2,1)}, u32[]{:S(2)}) copy-start(bf16[128,8192]{1,0:T(8,128)(2,1)} %in_ref.3) | copy-start | bytes 6291460
  40.2 32.7 %copy-start.6 = (f32[8192]{0:T(1024)S(1)}, f32[8192]{0:T(1024)}, u32[]{:S(2)}) copy-start(f32[8192]{0:T(1024)} %param.9) | copy-start | bytes 98308
  40.2 45.1 %all-to-all-start.2 = ((bf16[8,32,4096]{2,1,0:T(8,128)(2,1)}), bf16[8,32,4096]{2,1,0:T(8,128)(2,1)}, u32[]{:S(2)}, u32[]{:S(2)}) async-start(bf16[8,32,4096]{2,1,0:T(8,128)(2,1)} %broadcast_in_dim.53), calls=%async_computation.2 | async-start | bytes 4194304 | tf_op jit(solution)/shard_map/all_to_all | solution.py:33
  72.9 1.6 copy-start.1
  74.5 1.6 copy-start.5
  76.1 15.6 %copy-start.7 = (s32[32]{0:T(128)S(1)}, s32[32]{0:T(128)}, u32[]{:S(2)}) copy-start(s32[32]{0:T(128)} %param.13) | copy-start | bytes 388
  80.4 1.9 copy-start.3
  85.3 22.1 %all-to-all-start = ((bf16[16,16,1024]{2,1,0:T(8,128)(2,1)}), bf16[16,16,1024]{2,1,0:T(8,128)(2,1)S(1)}, u32[]{:S(2)}, u32[]{:S(2)}) async-start(bf16[16,16,1024]{2,1,0:T(8,128)(2,1)} %get-tuple-element.15), calls=%async_computation | async-start | bytes 1048576 | tf_op jit(solution)/shard_map/all_to_all | solution.py:33
  110.3 3.3 %collective-permute-start = (f32[136,256]{1,0:T(8,128)S(1)}, f32[136,256]{1,0:T(8,128)S(1)}, u32[]{:S(2)}, u32[]{:S(2)}) collective-permute-start(f32[136,256]{1,0:T(8,128)S(1)} %shard_map.87.own_ref), channel_id=1, source_target_pairs={{0,1},{1,0},{2,3},{3,2},{4,5},{5,4},{6,7},{7,6},{8,9},{9,8},{10,11... | collective-permute-start | bytes 417800 | tf_op jit(solution)/shard_map/ppermute | solution.py:37
  114.7 28.0 %all-to-all-start.3 = ((f32[256,1,256]{2,1,0:T(1,128)}), f32[256,1,256]{2,1,0:T(1,128)S(1)}, u32[]{:S(2)}, u32[]{:S(2)}) async-start(f32[256,1,256]{2,1,0:T(1,128)} %copy.15), calls=%async_computation.3 | async-start | bytes 524288 | tf_op jit(solution)/shard_map/all_to_all | solution.py:33
  146.2 20.2 %all-to-all-start.4 = ((bf16[16,16,1024]{2,1,0:T(8,128)(2,1)}), bf16[16,16,1024]{2,1,0:T(8,128)(2,1)S(1)}, u32[]{:S(2)}, u32[]{:S(2)}) async-start(bf16[16,16,1024]{2,1,0:T(8,128)(2,1)} %get-tuple-element.19), calls=%async_computation.4 | async-start | bytes 1048576 | tf_op jit(solution)/shard_map/all_to_all | solution.py:33
  166.4 1.6 copy-start.2
  168.0 2.2 copy-start.4
  173.1 5.2 %collective-permute-start.1 = (bf16[8,32,16,128]{3,2,1,0:T(8,128)(2,1)S(1)}, bf16[8,32,16,128]{3,2,1,0:T(8,128)(2,1)S(1)}, u32[]{:S(2)}, u32[]{:S(2)}) collective-permute-start(bf16[8,32,16,128]{3,2,1,0:T(8,128)(2,1)S(1)} %get-tuple-element.26), channel_id=1, source_target_pairs={{0,1},{1,0},{2,3},{3,2},{4,5},{5,4},{6,7},{7,6},{8,9},{9,8},{10,11... | collective-permute-start | bytes 3145736 | tf_op jit(solution)/shard_map/ppermute | solution.py:37
Sparse Core Ops, SparseCore 0:
  27.6 45.2 all-gather.2

commit v3 on v2

--- a/solution.py
+++ b/solution.py
@@ -49,7 +49,7 @@
         out_specs=[pl.BlockSpec(memory_space=pltpu.VMEM)] * len(outs),
         scratch_shapes=spare,
         compiler_params=pltpu.CompilerParams(
-            vmem_limit_bytes=min(48 * MIB, size + spare_size + 12 * MIB)
+            vmem_limit_bytes=spare_size + 8 * MIB
         ),
         cost_estimate=pl.CostEstimate(flops=flops, bytes_accessed=size, transcendentals=0),
     )(*args)
@@ -59,26 +59,34 @@
     return jax.ShapeDtypeStruct(*pair)
 
 
-def forward(nyh, nc, in_ref, frozen_ref, gain_ref, mats_ref,
+def adapter_slices(place_ref, own_ref, other_ref):
+    nyh, _, feats = own_ref.shape
+    for k in range(nyh):
+        for ref, core in ((own_ref, place_ref[1]), (other_ref, 1 - place_ref[1])):
+            at = (lax.rem(place_ref[0] + k, nyh) * 2 + core) * feats
+            yield ref.at[k], pl.ds(pl.multiple_of(at, feats), feats)
+
+
+def forward(nyh, nc, place_ref, in_ref, frozen_ref, gain_ref, own_ref, other_ref,
             latent_ref, hidden_ref, inv_ref, unit_ref, length_ref, send_ref, part_ref):
-    slices, both, feats = mats_ref.shape
+    _, both, feats = own_ref.shape
+    slices = nyh * nc
     rank = both // 2
     tokens, width = in_ref.shape
     queries = tokens // LEN
     acc = jnp.zeros((tokens, rank), f32)
     acc_t = jnp.zeros((rank, tokens), f32)
-    for f in range(slices):
-        part = in_ref[:, f * feats:(f + 1) * feats]
-        down = mats_ref[f, :rank]
+    for mats_ref, at in adapter_slices(place_ref, own_ref, other_ref):
+        part = in_ref[:, at]
+        down = mats_ref[:rank]
         acc += dot_rows(part, down)
         acc_t += dot_rows(down, part)
     latent = acc.astype(bf16)
     latent_ref[...] = acc_t.astype(bf16)
     squares = jnp.zeros((tokens, 1), f32)
-    for f in range(slices):
-        at = slice(f * feats, (f + 1) * feats)
+    for mats_ref, at in adapter_slices(place_ref, own_ref, other_ref):
         hidden = frozen_ref[:, at].astype(f32) + adapter_scale_factor * dot(
-            latent, mats_ref[f, rank:]
+            latent, mats_ref[rank:]
         )
         hidden_ref[:, at] = hidden
         squares += jnp.sum(hidden * hidden, axis=1, keepdims=True)
@@ -196,9 +204,11 @@
     out_ref[...] = total_ref[...].astype(bf16).reshape(out_ref.shape)
 
 
-def backward(nyh, nc, core_ref, got_ref, unit_ref, length_ref, inv_ref, hidden_ref, gain_ref,
-             in_ref, mats_ref, latent_ref, keep_ref, send_ref, grad_ref, scaled_ref, up_ref, hg_ref):
-    slices, both, feats = mats_ref.shape
+def backward(nyh, nc, place_ref, got_ref, unit_ref, length_ref, inv_ref, hidden_ref, gain_ref,
+             in_ref, own_ref, other_ref, latent_ref, keep_ref, send_ref,
+             grad_ref, scaled_ref, up_ref, hg_ref):
+    _, both, feats = own_ref.shape
+    slices = nyh * nc
     rank = both // 2
     tokens, width = in_ref.shape
     queries = tokens // LEN
@@ -228,18 +238,17 @@
     factor = inv * inv * inv * (jnp.concatenate(mean, axis=0) / width)
     latent_t = latent_ref[...]
     acc = jnp.zeros((rank, tokens), f32)
-    for f in range(slices):
-        at = slice(f * feats, (f + 1) * feats)
+    for mats_ref, at in adapter_slices(place_ref, own_ref, other_ref):
         for q in range(queries):
             of = slice(q * LEN, (q + 1) * LEN)
             hg_ref[of] = (
                 inv[of] * scaled_ref[q:q + 1, at] - hidden_ref[of, at] * factor[of]
             ).astype(bf16)
         hidden_grad = hg_ref[...]
-        acc += dot_rows(mats_ref[f, rank:], hidden_grad)
+        acc += dot_rows(mats_ref[rank:], hidden_grad)
         up_ref[:, at] = adapter_scale_factor * dot(latent_t, hidden_grad)
     latent_grad = (adapter_scale_factor * acc).astype(bf16)
-    first = core_ref[0] == 0
+    first = place_ref[1] == 0
     for f in range(slices):
         down = dot(latent_grad, in_ref[:, f * feats:(f + 1) * feats])
         for x in range(nx):
@@ -300,12 +309,24 @@
     shape = jax.ShapeDtypeStruct
     gain = gain.reshape(1, width)
 
-    mine = jnp.concatenate([adapter_a.T, adapter_up_matrix], axis=0)
-    mats = lax.all_gather(mine, ("yh", "c"), axis=0, tiled=False)
-
     sent = jnp.broadcast_to(passages.reshape(1, nyh, rows, feats), (nz, nyh, rows, feats))
     got = exchange(sent.reshape(nz * nyh, rows, feats), ("z", "yh"))
     got = got.reshape(nz, nyh, rows, feats).transpose(0, 2, 1, 3).reshape(nz * rows, half)
+
+    mine = jnp.concatenate([adapter_a.T, adapter_up_matrix], axis=0)
+    pieces = [mine]
+    for k in range(1, nyh):
+        flip = 2 * k == nyh
+        pairs = []
+        for yl in range(nyl):
+            for yh in range(nyh):
+                source = (nyl - 1 - yl if flip else yl) * nyh + (yh + k) % nyh
+                pairs.append((source, yl * nyh + yh))
+        pieces.append(lax.ppermute(mine, ("yl", "yh"), pairs))
+    own_mats, got = lax.optimization_barrier((jnp.stack(pieces), got))
+    other_mats = swap_cores(own_mats)
+    place = jnp.stack([iyh, ic]).astype(jnp.int32)
+
     got = jnp.broadcast_to(got[None], (nx, nz * rows, half))
     block = exchange(got, "x").reshape(nx * nz * rows, half)
     columns = block.shape[0]
@@ -320,10 +341,12 @@
             shape((queries, 128), f32),
             shape((ring, nyh * queries, feats), bf16),
         ],
-        [adapter_in, frozen, gain, mats],
+        [place, adapter_in, frozen, gain, own_mats, other_mats],
         scratch=[((nc, nyh * queries, feats), f32)],
+        scalars=1,
         flops=6 * tokens * rank * width,
     )
+    sent, block = lax.optimization_barrier((sent, block))
     query = exchange(sent, ("yl", "yh", "c"))
 
     count = ring * 8
@@ -368,7 +391,7 @@
     keep, send = call(
         functools.partial(backward, nyh, nc),
         [shape((nx, blocks, 2 * out_rows, cols), bf16)] * 2,
-        [ic.astype(jnp.int32).reshape(1), got, unit, length, inv, hidden, gain, adapter_in, mats, latent_t],
+        [place, got, unit, length, inv, hidden, gain, adapter_in, own_mats, other_mats, latent_t],
         scratch=[
             ((nc, nyh * queries, feats), f32),
             ((queries, width), f32),

time: 231 us -> 222 us (0.961)
  waiting for transfers between devices: 92.4 us -> 60.8 us
  starting transfers between devices: 49.3 us -> 70.4 us
  blocking collectives: 41.5 us -> 57.6 us
  between operations: 15.9 us -> 2.61 us
    all_gather x1 -> x0, waiting for transfers between devices: 28.2 us -> none  [shards(): mats = lax.all_gather(mine, ('yh', 'c'), axis=0, tiled=False)]
    all_to_all x5 -> x4, waiting for transfers between devices: 60.8 us -> 38.2 us  [exchange(): return lax.all_to_all(blocks, axes, 0, 0, tiled=True)]
    ppermute x0 -> x3, waiting for transfers between devices: none -> 16.8 us  [shards(): pieces.append(lax.ppermute(mine, ('yl', 'yh'), pairs))]
    all_to_all x2 -> x3, blocking collectives: 41.5 us -> 57.6 us  [exchange(): return lax.all_to_all(blocks, axes, 0, 0, tiled=True)]
    ppermute x0 -> x3, starting transfers between devices: none -> 14.3 us  [shards(): pieces.append(lax.ppermute(mine, ('yl', 'yh'), pairs))]
    ppermute x2 -> x3, starting transfers between devices: 4.96 us -> 14.6 us  [swap_cores(): return lax.ppermute(value, 'c', [(0, 1), (1, 0)])]
    all_to_all x5 -> x4, starting transfers between devices: 44.3 us -> 41.5 us  [exchange(): return lax.all_to_all(blocks, axes, 0, 0, tiled=True)]
    ppermute x2 -> x3, waiting for transfers between devices: 3.39 us -> 5.82 us  [swap_cores(): return lax.ppermute(value, 'c', [(0, 1), (1, 0)])]
  transfers between devices with their start and end apart: 8 -> 10, of which waited for: 8 -> 8; matrix products, arithmetic and copies ran while one was open for 2% -> 1% of each run, Pallas kernels for 2% -> 2%
where the time goes in v3:
time: 222 us; the launch traced here: 221 us
  starting transfers between devices  70.4 us (32%)
  waiting for transfers between devices  60.8 us (27%)
  blocking collectives  57.6 us (26%)
  Pallas kernels  14.8 us (7%)
  local copies, waits for them, and re-layouts  13.1 us (6%)
  between operations  2.61 us (1%)
    all_to_all x3, blocking collectives, exchange(): return lax.all_to_all(blocks, axes, 0, 0, tiled=True)  57.6 us
    all_to_all x4, starting transfers between devices, exchange(): return lax.all_to_all(blocks, axes, 0, 0, tiled=True)  41.5 us
    all_to_all x4, waiting for transfers between devices, exchange(): return lax.all_to_all(blocks, axes, 0, 0, tiled=True)  38.2 us
    ppermute x3, waiting for transfers between devices, shards(): pieces.append(lax.ppermute(mine, ('yl', 'yh'), pairs))  16.8 us
    pallas_call x7, Pallas kernels, call(): pl.pallas_call(kernel, out_shape=outs, in_specs=[pl.BlockSpec(memory_spac...  14.8 us
    ppermute x3, starting transfers between devices, swap_cores(): return lax.ppermute(value, 'c', [(0, 1), (1, 0)])  14.6 us
    ppermute x3, starting transfers between devices, shards(): pieces.append(lax.ppermute(mine, ('yl', 'yh'), pairs))  14.3 us
    unnamed x19, local copies, waits for them, and re-layouts  7.21 us
  transfers between devices with their start and end apart: 10, of which 8 were waited for; matrix products, arithmetic and copies ran while one was open for 1% of the time, Pallas kernels for 2%

profile of v3, /device:TPU:16, one launch (start us, length us, event | category | flops | bytes accessed | tf_op | source)
XLA Modules:
  0.0 220.6 jit_solution(12835210403345680800)
XLA Ops:
  2.2 15.9 %all-to-all-start = ((bf16[16,8,1024]{2,1,0:T(8,128)(2,1)}), bf16[16,8,1024]{2,1,0:T(8,128)(2,1)S(1)}, u32[]{:S(2)}, u32[]{:S(2)}) async-start(bf16[16,8,1024]{2,1,0:T(8,128)(2,1)} %bitcast.11), calls=%async_computation | async-start | bytes 524288 | tf_op jit(solution)/shard_map/all_to_all | solution.py:33
  19.1 6.4 %collective-permute-start.1 = (bf16[128,1024]{1,0:T(8,128)(2,1)S(1)}, bf16[128,1024]{1,0:T(8,128)(2,1)S(1)}, u32[]{:S(2)}, u32[]{:S(2)}) collective-permute-start(bf16[128,1024]{1,0:T(8,128)(2,1)S(1)} %get-tuple-element.37), channel_id=1, source_target_pairs={{68,0},{70,2},{64,4},{66,6},{4,64},{6,66},{0,68},{2,70},{69,1},{71... | collective-permute-start | bytes 786440 | tf_op jit(solution)/shard_map/ppermute | solution.py:325
  25.5 4.3 %collective-permute-start = (bf16[128,1024]{1,0:T(8,128)(2,1)S(1)}, bf16[128,1024]{1,0:T(8,128)(2,1)S(1)}, u32[]{:S(2)}, u32[]{:S(2)}) collective-permute-start(bf16[128,1024]{1,0:T(8,128)(2,1)S(1)} %get-tuple-element.37), channel_id=1, source_target_pairs={{2,0},{4,2},{6,4},{0,6},{66,64},{68,66},{70,68},{64,70},{3,1},{5,3... | collective-permute-start | bytes 786440 | tf_op jit(solution)/shard_map/ppermute | solution.py:325
  29.8 3.7 %collective-permute-start.2 = (bf16[128,1024]{1,0:T(8,128)(2,1)S(1)}, bf16[128,1024]{1,0:T(8,128)(2,1)S(1)}, u32[]{:S(2)}, u32[]{:S(2)}) collective-permute-start(bf16[128,1024]{1,0:T(8,128)(2,1)S(1)} %get-tuple-element.37), channel_id=1, source_target_pairs={{6,0},{0,2},{2,4},{4,6},{70,64},{64,66},{66,68},{68,70},{7,1},{1,3... | collective-permute-start | bytes 786440 | tf_op jit(solution)/shard_map/ppermute | solution.py:325
  33.5 4.3 %collective-permute-done.1 = bf16[128,1024]{1,0:T(8,128)(2,1)S(1)} collective-permute-done((bf16[128,1024]{1,0:T(8,128)(2,1)S(1)}, bf16[128,1024]{1,0:T(8,128)(2,1)S(1)}, u32[]{:S(2)}, u32[]{:S(2)}) %collective-permute-start.1) | collective-permute-done | bytes 262176 | tf_op jit(solution)/shard_map/ppermute | solution.py:325
  37.8 12.5 %collective-permute-done = bf16[128,1024]{1,0:T(8,128)(2,1)S(1)} collective-permute-done((bf16[128,1024]{1,0:T(8,128)(2,1)S(1)}, bf16[128,1024]{1,0:T(8,128)(2,1)S(1)}, u32[]{:S(2)}, u32[]{:S(2)}) %collective-permute-start) | collective-permute-done | bytes 262176 | tf_op jit(solution)/shard_map/ppermute | solution.py:325
  52.1 5.2 %all-to-all-start.1 = ((bf16[8,32,4096]{2,1,0:T(8,128)(2,1)}), bf16[8,32,4096]{2,1,0:T(8,128)(2,1)}, u32[]{:S(2)}, u32[]{:S(2)}) async-start(bf16[8,32,4096]{2,1,0:T(8,128)(2,1)} %broadcast_in_dim.51), calls=%async_computation.1 | async-start | bytes 4194304 | tf_op jit(solution)/shard_map/all_to_all | solution.py:33
  59.3 2.7 %collective-permute-done.3.other_ref = bf16[4,128,1024]{2,1,0:T(8,128)(2,1)} collective-permute-done((bf16[4,128,1024]{2,1,0:T(8,128)(2,1)S(1)}, bf16[4,128,1024]{2,1,0:T(8,128)(2,1)}, u32[]{:S(2)}, u32[]{:S(2)}) %collective-permute-start.3) | collective-permute-done | bytes 1048608 | tf_op jit(solution)/shard_map/ppermute | solution.py:37
  63.6 4.4 %shard_map.86 = (bf16[64,128]{1,0:T(8,128)(2,1)S(1)}, f32[128,8192]{1,0:T(8,128)S(1)}, f32[128,128]{1,0:T(8,128)S(1)}, f32[4,8192]{1,0:T(4,128)S(1)}, f32[4,128]...) custom-call(s32[2]{0:T(128)S(1)} %pad_add_fusion.place_ref, bf16[128,8192]{1,0:T(8,128)(2,1)S(1)} %copy-done, ...), custom_call_target="tpu_custom_call" | custom-call | flops 402653184 | bytes 11257856 | tf_op jit(solution)/shard_map/pallas_call | solution.py:44
  68.0 1.9 copy-done.1
  70.7 12.9 %all-to-all-done.1 = bf16[8,32,4096]{2,1,0:T(8,128)(2,1)} async-done(((bf16[8,32,4096]{2,1,0:T(8,128)(2,1)}), bf16[8,32,4096]{2,1,0:T(8,128)(2,1)}, u32[]{:S(2)}, u32[]{:S(2)}) %all-to-all-start.1) | async-done | bytes 2097184 | tf_op jit(solution)/shard_map/all_to_all | solution.py:33
  83.6 5.4 %all-to-all-start.2 = ((bf16[16,16,1024]{2,1,0:T(8,128)(2,1)}), bf16[16,16,1024]{2,1,0:T(8,128)(2,1)}, u32[]{:S(2)}, u32[]{:S(2)}) async-start(bf16[16,16,1024]{2,1,0:T(8,128)(2,1)} %copy-done.4), calls=%async_computation.2 | async-start | bytes 1048576 | tf_op jit(solution)/shard_map/all_to_all | solution.py:33
  89.7 10.5 %all-to-all-done.2.query_ref = bf16[16,16,1024]{2,1,0:T(8,128)(2,1)} async-done(((bf16[16,16,1024]{2,1,0:T(8,128)(2,1)}), bf16[16,16,1024]{2,1,0:T(8,128)(2,1)}, u32[]{:S(2)}, u32[]{:S(2)}) %all-to-all-start.2) | async-done | bytes 524320 | tf_op jit(solution)/shard_map/all_to_all | solution.py:33
  100.2 3.1 %shard_map.87.own_ref = f32[136,256]{1,0:T(8,128)S(1)} custom-call(bf16[16,16,1024]{2,1,0:T(8,128)(2,1)} %all-to-all-done.2.query_ref, bf16[256,4096]{1,0:T(8,128)(2,1)} %bitcast.15.block_ref), custom_call_target="tpu_custom_call" | custom-call | flops 1073741824 | bytes 2760704 | tf_op jit(solution)/shard_map/pallas_call | solution.py:44
  103.3 6.7 %collective-permute-start.4 = (f32[136,256]{1,0:T(8,128)S(1)}, f32[136,256]{1,0:T(8,128)S(1)}, u32[]{:S(2)}, u32[]{:S(2)}) collective-permute-start(f32[136,256]{1,0:T(8,128)S(1)} %shard_map.87.own_ref), channel_id=1, source_target_pairs={{0,1},{1,0},{2,3},{3,2},{4,5},{5,4},{6,7},{7,6},{8,9},{9,8},{10,11... | collective-permute-start | bytes 417800 | tf_op jit(solution)/shard_map/ppermute | solution.py:37
  112.8 14.9 %all-to-all-start.3 = ((f32[256,1,256]{2,1,0:T(1,128)}), f32[256,1,256]{2,1,0:T(1,128)}, u32[]{:S(2)}, u32[]{:S(2)}) async-start(f32[256,1,256]{2,1,0:T(1,128)} %copy.15), calls=%async_computation.3 | async-start | bytes 524288 | tf_op jit(solution)/shard_map/all_to_all | solution.py:33
  127.7 14.7 %all-to-all-done.3 = f32[256,1,256]{2,1,0:T(1,128)} async-done(((f32[256,1,256]{2,1,0:T(1,128)}), f32[256,1,256]{2,1,0:T(1,128)}, u32[]{:S(2)}, u32[]{:S(2)}) %all-to-all-start.3) | async-done | bytes 262176 | tf_op jit(solution)/shard_map/all_to_all | solution.py:33
  144.7 2.6 %shard_map.89 = (bf16[16,16,1024]{2,1,0:T(8,128)(2,1)S(1)}, f32[8,128]{1,0:T(8,128)S(1)}) custom-call(s32[1]{0:T(128)} %bitcast.2.iy_ref, s32[1]{0:T(128)} %bitcast.3.ixz_ref, f32[128,256]{1,0:T(8,128)S(1)} %copy-done.7, f32[8,256]{1,0:T(8,128)S(1)} %get-tuple-element.25.aux_ref, f32[128,256]{1,0:T(8,128)S(1)} %compare_convert_fusion.onehot_ref, ...), custom_call_target="tpu_custom_call" | custom-call | flops 536870912 | bytes 3158016 | tf_op jit(solution)/shard_map/pallas_call | solution.py:44
  147.3 16.6 %all_to_all.41.got_ref = bf16[16,16,1024]{2,1,0:T(8,128)(2,1)S(1)} all-to-all(bf16[16,16,1024]{2,1,0:T(8,128)(2,1)S(1)} %get-tuple-element.27), channel_id=1, replica_groups=mesh['z'=4,'yl'=2,'x'=8,'yh'=4,'c'=2] {'yl','yh','c'}, dimensions={0} | all-to-all | bytes 1048576 | tf_op jit(solution)/shard_map/all_to_all | solution.py:33
  163.9 4.2 %shard_map.90 = (bf16[8,32,16,128]{3,2,1,0:T(8,128)(2,1)S(1)}, bf16[8,32,16,128]{3,2,1,0:T(8,128)(2,1)S(1)}) custom-call(s32[2]{0:T(128)S(1)} %pad_add_fusion.place_ref, bf16[16,16,1024]{2,1,0:T(8,128)(2,1)S(1)} %all_to_all.41.got_ref, f32[4,8192]{1,0:T(4,128)S(1)} %get-tuple-element.28.unit_ref, f32[4,128]{1,0:T(4,128)S(1)} %get-tuple-element.29.length_ref, ...), custom_call_target="tpu_custom_call" | custom-call | flops 402653184 | bytes 11257856 | tf_op jit(solution)/shard_map/pallas_call | solution.py:44
  168.1 6.0 %collective-permute-start.5 = (bf16[8,32,16,128]{3,2,1,0:T(8,128)(2,1)S(1)}, bf16[8,32,16,128]{3,2,1,0:T(8,128)(2,1)S(1)}, u32[]{:S(2)}, u32[]{:S(2)}) collective-permute-start(bf16[8,32,16,128]{3,2,1,0:T(8,128)(2,1)S(1)} %get-tuple-element.34), channel_id=1, source_target_pairs={{0,1},{1,0},{2,3},{3,2},{4,5},{5,4},{6,7},{7,6},{8,9},{9,8},{10,11... | collective-permute-start | bytes 3145736 | tf_op jit(solution)/shard_map/ppermute | solution.py:37
  174.1 2.3 %collective-permute-done.5.got_ref = bf16[8,32,16,128]{3,2,1,0:T(8,128)(2,1)S(1)} collective-permute-done((bf16[8,32,16,128]{3,2,1,0:T(8,128)(2,1)S(1)}, bf16[8,32,16,128]{3,2,1,0:T(8,128)(2,1)S(1)}, u32[]{:S(2)}, u32[]{:S(2)}) %collective-permute-start.5) | collective-permute-done | bytes 1048608 | tf_op jit(solution)/shard_map/ppermute | solution.py:37
  176.6 19.5 %all_to_all.42.got_ref = bf16[8,33,16,128]{3,2,1,0:T(8,128)(2,1)S(1)} all-to-all(bf16[8,33,16,128]{3,2,1,0:T(8,128)(2,1)S(1)} %shard_map.91), channel_id=1, replica_groups=mesh['z'=4,'yl'=2,'x'=8,'yh'=4,'c'=2] {'x'}, dimensions={0} | all-to-all | bytes 2162688 | tf_op jit(solution)/shard_map/all_to_all | solution.py:33
  196.2 21.5 %all_to_all.43 = f32[32,24,128]{2,1,0:T(8,128)S(1)} all-to-all(f32[32,24,128]{2,1,0:T(8,128)S(1)} %shard_map.92), channel_id=1, replica_groups=mesh['z'=4,'yl'=2,'x'=8,'yh'=4,'c'=2] {'z','yl','yh'}, dimensions={0} | all-to-all | bytes 786432 | tf_op jit(solution)/shard_map/all_to_all | solution.py:33
  (47 shorter events, 15.9 us)
Async XLA Ops:
  2.2 48.3 %all-to-all-start = ((bf16[16,8,1024]{2,1,0:T(8,128)(2,1)}), bf16[16,8,1024]{2,1,0:T(8,128)(2,1)S(1)}, u32[]{:S(2)}, u32[]{:S(2)}) async-start(bf16[16,8,1024]{2,1,0:T(8,128)(2,1)} %bitcast.11), calls=%async_computation | async-start | bytes 524288 | tf_op jit(solution)/shard_map/all_to_all | solution.py:33
  19.1 18.7 %collective-permute-start.1 = (bf16[128,1024]{1,0:T(8,128)(2,1)S(1)}, bf16[128,1024]{1,0:T(8,128)(2,1)S(1)}, u32[]{:S(2)}, u32[]{:S(2)}) collective-permute-start(bf16[128,1024]{1,0:T(8,128)(2,1)S(1)} %get-tuple-element.37), channel_id=1, source_target_pairs={{68,0},{70,2},{64,4},{66,6},{4,64},{6,66},{0,68},{2,70},{69,1},{71... | collective-permute-start | bytes 786440 | tf_op jit(solution)/shard_map/ppermute | solution.py:325
  25.5 24.8 %collective-permute-start = (bf16[128,1024]{1,0:T(8,128)(2,1)S(1)}, bf16[128,1024]{1,0:T(8,128)(2,1)S(1)}, u32[]{:S(2)}, u32[]{:S(2)}) collective-permute-start(bf16[128,1024]{1,0:T(8,128)(2,1)S(1)} %get-tuple-element.37), channel_id=1, source_target_pairs={{2,0},{4,2},{6,4},{0,6},{66,64},{68,66},{70,68},{64,70},{3,1},{5,3... | collective-permute-start | bytes 786440 | tf_op jit(solution)/shard_map/ppermute | solution.py:325
  29.8 20.5 %collective-permute-start.2 = (bf16[128,1024]{1,0:T(8,128)(2,1)S(1)}, bf16[128,1024]{1,0:T(8,128)(2,1)S(1)}, u32[]{:S(2)}, u32[]{:S(2)}) collective-permute-start(bf16[128,1024]{1,0:T(8,128)(2,1)S(1)} %get-tuple-element.37), channel_id=1, source_target_pairs={{6,0},{0,2},{2,4},{4,6},{70,64},{64,66},{66,68},{68,70},{7,1},{1,3... | collective-permute-start | bytes 786440 | tf_op jit(solution)/shard_map/ppermute | solution.py:325
  52.1 9.9 %copy-start = (bf16[128,8192]{1,0:T(8,128)(2,1)S(1)}, bf16[128,8192]{1,0:T(8,128)(2,1)}, u32[]{:S(2)}) copy-start(bf16[128,8192]{1,0:T(8,128)(2,1)} %in_ref.3) | copy-start | bytes 6291460
  52.1 9.9 %copy-start.5 = (f32[8192]{0:T(1024)S(1)}, f32[8192]{0:T(1024)}, u32[]{:S(2)}) copy-start(f32[8192]{0:T(1024)} %param.9) | copy-start | bytes 98308
  52.1 31.5 %all-to-all-start.1 = ((bf16[8,32,4096]{2,1,0:T(8,128)(2,1)}), bf16[8,32,4096]{2,1,0:T(8,128)(2,1)}, u32[]{:S(2)}, u32[]{:S(2)}) async-start(bf16[8,32,4096]{2,1,0:T(8,128)(2,1)} %broadcast_in_dim.51), calls=%async_computation.1 | async-start | bytes 4194304 | tf_op jit(solution)/shard_map/all_to_all | solution.py:33
  57.3 4.7 %collective-permute-start.3 = (bf16[4,128,1024]{2,1,0:T(8,128)(2,1)S(1)}, bf16[4,128,1024]{2,1,0:T(8,128)(2,1)}, u32[]{:S(2)}, u32[]{:S(2)}) collective-permute-start(bf16[4,128,1024]{2,1,0:T(8,128)(2,1)S(1)} %pad_maximum_fusion.own_ref), channel_id=1, source_target_pairs={{0,1},{1,0},{2,3},{3,2},{4,5},{5,4},{6,7},{7,6},{8,9},{9,8},{10,11... | collective-permute-start | bytes 3145736 | tf_op jit(solution)/shard_map/ppermute | solution.py:37
  62.0 1.6 copy-start.3
  63.6 25.6 %copy-start.8 = (s32[32]{0:T(128)S(1)}, s32[32]{0:T(128)}, u32[]{:S(2)}) copy-start(s32[32]{0:T(128)} %param.13) | copy-start | bytes 388
  67.9 1.9 copy-start.1
  69.9 0.8 copy-start.4
  83.6 16.6 %all-to-all-start.2 = ((bf16[16,16,1024]{2,1,0:T(8,128)(2,1)}), bf16[16,16,1024]{2,1,0:T(8,128)(2,1)}, u32[]{:S(2)}, u32[]{:S(2)}) async-start(bf16[16,16,1024]{2,1,0:T(8,128)(2,1)} %copy-done.4), calls=%async_computation.2 | async-start | bytes 1048576 | tf_op jit(solution)/shard_map/all_to_all | solution.py:33
  103.3 7.7 %collective-permute-start.4 = (f32[136,256]{1,0:T(8,128)S(1)}, f32[136,256]{1,0:T(8,128)S(1)}, u32[]{:S(2)}, u32[]{:S(2)}) collective-permute-start(f32[136,256]{1,0:T(8,128)S(1)} %shard_map.87.own_ref), channel_id=1, source_target_pairs={{0,1},{1,0},{2,3},{3,2},{4,5},{5,4},{6,7},{7,6},{8,9},{9,8},{10,11... | collective-permute-start | bytes 417800 | tf_op jit(solution)/shard_map/ppermute | solution.py:37
  111.1 0.7 copy-start.6
  112.8 29.7 %all-to-all-start.3 = ((f32[256,1,256]{2,1,0:T(1,128)}), f32[256,1,256]{2,1,0:T(1,128)}, u32[]{:S(2)}, u32[]{:S(2)}) async-start(f32[256,1,256]{2,1,0:T(1,128)} %copy.15), calls=%async_computation.3 | async-start | bytes 524288 | tf_op jit(solution)/shard_map/all_to_all | solution.py:33
  142.4 21.4 %copy-start.2 = (f32[128,8192]{1,0:T(8,128)S(1)}, f32[128,8192]{1,0:T(8,128)}, u32[]{:S(2)}) copy-start(f32[128,8192]{1,0:T(8,128)} %copy-done.1) | copy-start | bytes 12582916
  143.6 1.1 copy-start.7
  168.1 8.3 %collective-permute-start.5 = (bf16[8,32,16,128]{3,2,1,0:T(8,128)(2,1)S(1)}, bf16[8,32,16,128]{3,2,1,0:T(8,128)(2,1)S(1)}, u32[]{:S(2)}, u32[]{:S(2)}) collective-permute-start(bf16[8,32,16,128]{3,2,1,0:T(8,128)(2,1)S(1)} %get-tuple-element.34), channel_id=1, source_target_pairs={{0,1},{1,0},{2,3},{3,2},{4,5},{5,4},{6,7},{7,6},{8,9},{9,8},{10,11... | collective-permute-start | bytes 3145736 | tf_op jit(solution)/shard_map/ppermute | solution.py:37

commit v4 on v3

--- a/solution.py
+++ b/solution.py
@@ -147,15 +147,8 @@
     return jnp.transpose(jnp.broadcast_to(row, (n, n)))
 
 
-def widen(row, lanes):
-    if row.shape[1] == lanes:
-        return row
-    return jnp.concatenate([row, jnp.zeros((1, lanes - row.shape[1]), f32)], axis=1)
-
-
-def exponentials(members, iy_ref, own_ref, other_ref, onehot_ref, expo_ref, aux_ref, send_ref):
-    count = expo_ref.shape[0]
-    columns = expo_ref.shape[1]
+def exponentials(own_ref, other_ref, onehot_ref, expo_ref, aux_ref, rows_ref, cols_ref):
+    count, columns = expo_ref.shape
     inv_norm = 1.0 / jnp.sqrt(own_ref[count:count + 1] + other_ref[count:count + 1])
     scores = inv_temp * ((own_ref[:count] + other_ref[:count]) * inv_norm)
     expo = jnp.exp(scores - inv_temp)
@@ -164,33 +157,29 @@
     aux_ref[0:1] = inv_norm
     aux_ref[1:2] = jnp.full((1, columns), hits)
     row = across(jnp.sum(expo, axis=1, keepdims=True))[0:1]
-    row = widen(row, send_ref.shape[1])
-    col = widen(0.5 * jnp.sum(expo, axis=0, keepdims=True), send_ref.shape[1])
-    same_y = row_index(send_ref.shape) // members == iy_ref[0]
-    send_ref[...] = jnp.where(same_y, col, row)
-
-
-def weigh(nyh, members, iy_ref, ixz_ref, expo_ref, aux_ref, onehot_ref, sums_ref, block_ref,
+    for y in range(rows_ref.shape[0]):
+        rows_ref[y] = row
+    col = 0.5 * jnp.sum(expo, axis=0, keepdims=True)
+    for i in range(cols_ref.shape[0]):
+        cols_ref[i] = col
+
+
+def weigh(nyh, expo_ref, aux_ref, onehot_ref, rows_ref, cols_ref, block_ref,
           out_ref, loss_ref, total_ref):
     count, columns = expo_ref.shape
     ring, rows, feats = out_ref.shape
     queries = rows // nyh
-    sums = sums_ref[...]
-    peer = row_index(sums.shape)
-    same_y = peer // members == iy_ref[0]
-    col = jnp.sum(jnp.where(same_y, sums, 0.0), axis=0, keepdims=True)[:, :columns]
-    same_xz = jnp.logical_and(peer % members == ixz_ref[0], jnp.logical_not(same_y))
-    rest = jnp.sum(jnp.where(same_xz, sums, 0.0), axis=0, keepdims=True)[:, :count]
-    expo = expo_ref[...]
-    row = across(rest)[:, :1] + jnp.sum(expo, axis=1, keepdims=True)
-    peers = sums.shape[0]
+    ny, members = rows_ref.shape[0], cols_ref.shape[0]
+    row = functools.reduce(jnp.add, [rows_ref[y] for y in range(ny)])
+    col = functools.reduce(jnp.add, [cols_ref[i] for i in range(members)])
     loss = (
-        0.5 * jnp.sum(jnp.log(row), axis=0, keepdims=True) / (peers // members)
+        0.5 * jnp.sum(jnp.log(row), axis=1, keepdims=True) / ny
         + jnp.sum(jnp.log(col), axis=1, keepdims=True) / members
         - 2.0 * aux_ref[1:2, 0:1]
     )
     loss_ref[...] = jnp.broadcast_to(loss, loss_ref.shape)
-    weights = 0.5 * (expo / row + expo / col) - onehot_ref[...]
+    expo = expo_ref[...]
+    weights = 0.5 * (expo / across(row)[:, :1] + expo / col) - onehot_ref[...]
     weights = (weights * aux_ref[0:1]).reshape(ring, 1, 8, columns)
     weights = jnp.broadcast_to(weights, (ring, rows // 8, 8, columns))
     weights = weights.reshape(ring * rows, columns).astype(bf16)
@@ -265,15 +254,18 @@
                 send_ref[x, f * nyh + yh] = jnp.where(first, tiles[1], tiles[0])
 
 
+def split_rows(value, rows, cols):
+    high = value.astype(bf16).astype(f32)
+    middle = (value - high).astype(bf16).astype(f32)
+    low = value - high - middle
+    at = row_index((rows, value.shape[1]))
+    parts = jnp.where(at == 0, high, jnp.where(at == 1, middle, jnp.where(at == 2, low, 0.0)))
+    return jnp.concatenate([parts] * (cols // value.shape[1]), axis=1).astype(bf16)
+
+
 def join(keep_ref, got_ref, loss_ref, out_ref):
     nx, blocks, rows, cols = keep_ref.shape
-    high = loss_ref[0:1].astype(bf16).astype(f32)
-    rest = loss_ref[0:1] - high
-    middle = rest.astype(bf16).astype(f32)
-    low = rest - middle
-    at = row_index((rows, loss_ref.shape[1]))
-    parts = jnp.where(at == 0, high, jnp.where(at == 1, middle, jnp.where(at == 2, low, 0.0)))
-    parts = jnp.concatenate([parts] * (cols // loss_ref.shape[1]), axis=1).astype(bf16)
+    parts = split_rows(loss_ref[0:1], rows, cols)
     for x in range(nx):
         out_ref[x, :blocks] = (
             keep_ref[x].astype(f32) + got_ref[x].astype(f32)
@@ -287,9 +279,19 @@
         total += got_ref[x].astype(f32)
     blocks, _, cols = out_ref.shape
     rows = got_ref.shape[2]
-    loss = jnp.sum(total[blocks], axis=0, keepdims=True)
-    out_ref[:, :rows] = total[:blocks]
-    out_ref[:, rows:] = jnp.broadcast_to(loss[None], (blocks, 8, cols))
+    loss = jnp.sum(total[blocks], axis=0, keepdims=True)[:, :128]
+    out_ref[:, :rows] = total[:blocks].astype(bf16)
+    out_ref[:, rows:] = jnp.broadcast_to(split_rows(loss, rows, cols)[None], (blocks, rows, cols))
+
+
+def add_last(got_ref, out_ref):
+    total = got_ref[0].astype(f32)
+    for i in range(1, got_ref.shape[0]):
+        total += got_ref[i].astype(f32)
+    rows = out_ref.shape[0] - 8
+    out_ref[:rows] = total[:rows]
+    loss = jnp.sum(total[rows:], axis=0, keepdims=True)
+    out_ref[rows:] = jnp.broadcast_to(loss, (8, out_ref.shape[1]))
 
 
 def shards(sizes, adapter_in, frozen, gain, adapter_a, adapter_up_matrix, passages, positive):
@@ -309,9 +311,9 @@
     shape = jax.ShapeDtypeStruct
     gain = gain.reshape(1, width)
 
-    sent = jnp.broadcast_to(passages.reshape(1, nyh, rows, feats), (nz, nyh, rows, feats))
-    got = exchange(sent.reshape(nz * nyh, rows, feats), ("z", "yh"))
-    got = got.reshape(nz, nyh, rows, feats).transpose(0, 2, 1, 3).reshape(nz * rows, half)
+    sent = jnp.broadcast_to(passages.reshape(1, nyh, rows, feats), (nx, nyh, rows, feats))
+    got = exchange(sent.reshape(nx * nyh, rows, feats), ("x", "yh"))
+    got = got.reshape(nx, nyh, rows, feats).transpose(0, 2, 1, 3).reshape(nx * rows, half)
 
     mine = jnp.concatenate([adapter_a.T, adapter_up_matrix], axis=0)
     pieces = [mine]
@@ -323,12 +325,16 @@
                 source = (nyl - 1 - yl if flip else yl) * nyh + (yh + k) % nyh
                 pairs.append((source, yl * nyh + yh))
         pieces.append(lax.ppermute(mine, ("yl", "yh"), pairs))
-    own_mats, got = lax.optimization_barrier((jnp.stack(pieces), got))
+    early = [k for k in range(1, nyh) if 2 * k != nyh]
+    got, *arrived = lax.optimization_barrier((got, *[pieces[k] for k in early]))
+    for k, piece in zip(early, arrived):
+        pieces[k] = piece
+    own_mats = jnp.stack(pieces)
     other_mats = swap_cores(own_mats)
     place = jnp.stack([iyh, ic]).astype(jnp.int32)
 
-    got = jnp.broadcast_to(got[None], (nx, nz * rows, half))
-    block = exchange(got, "x").reshape(nx * nz * rows, half)
+    got = jnp.broadcast_to(got[None], (nz, nx * rows, half))
+    block = exchange(got, "z").reshape(members * rows, half)
     columns = block.shape[0]
 
     latent_t, hidden, inv, unit, length, sent = call(
@@ -351,16 +357,13 @@
 
     count = ring * 8
     at = lax.iota(jnp.int32, columns)
-    at_x, at_z, at_row = at // (nz * rows), at // rows % nz, at % rows
+    at_z, at_x, at_row = at // (nx * rows), at // rows % nx, at % rows
     passage_id = ((at_z * nyl + iyl) * nx + at_x) * group + iyh * rows + at_row
     own_pos = jnp.where(
         lax.iota(jnp.int32, nyl)[:, None] == iyl, positive[None, :], -1
     ).reshape(ring, 1, queries)
     own_pos = jnp.broadcast_to(own_pos, (ring, 8 // queries, queries)).reshape(count)
     onehot = (own_pos[:, None] == passage_id[None, :]).astype(f32)
-    iy = (iyl * nyh + iyh).astype(jnp.int32).reshape(1)
-    ixz = (iz * nx + ix).astype(jnp.int32).reshape(1)
-
     (own,) = call(
         functools.partial(score, nyh),
         [shape((count + 8, columns), f32)],
@@ -368,19 +371,23 @@
         flops=4 * ring * nyh * queries * columns * half,
     )
     other = swap_cores(own)
-    expo, aux, sent = call(
-        functools.partial(exponentials, members),
-        [shape((count, columns), f32), shape((8, columns), f32), shape((ny * members, max(columns, count)), f32)],
-        [iy, own, other, onehot],
-        scalars=1,
-    )
-    sums = exchange(sent, ("yl", "yh", "z", "x"))
+    expo, aux, by_row, by_col = call(
+        exponentials,
+        [
+            shape((count, columns), f32),
+            shape((8, columns), f32),
+            shape((ny, 1, count), f32),
+            shape((members, 1, columns), f32),
+        ],
+        [own, other, onehot],
+    )
+    by_row = exchange(by_row, ("yl", "yh"))
+    by_col = exchange(by_col, ("z", "x"))
     sent, loss = call(
-        functools.partial(weigh, nyh, members),
+        functools.partial(weigh, nyh),
         [shape((ring, nyh * queries, feats), bf16), shape((8, 128), f32)],
-        [iy, ixz, expo, aux, onehot, sums, block],
+        [expo, aux, onehot, by_row, by_col, block],
         scratch=[((ring * nyh * queries, feats), f32)],
-        scalars=2,
         flops=2 * ring * nyh * queries * columns * half,
     )
     got = exchange(sent, ("yl", "yh", "c"))
@@ -407,9 +414,13 @@
         [keep, swap_cores(send), loss],
     )
     (line,) = call(
-        add_line, [shape((blocks, 2 * out_rows + 8, cols), f32)], [exchange(chip, "x")]
-    )
-    last = jnp.sum(exchange(line, ("z", "yl", "yh")), axis=0)
+        add_line, [shape((blocks, 4 * out_rows, cols), bf16)], [exchange(chip, "x")]
+    )
+    (last,) = call(
+        add_last,
+        [shape((2 * out_rows + 8, cols), f32)],
+        [exchange(line, ("z", "yl", "yh"))],
+    )
     adapter_grads = last[: 2 * out_rows].reshape(2, out_rows, cols)
     total_pairs = group * nz * nyl * nx
     loss = last[2 * out_rows, 0] / (2.0 * total_pairs) + inv_temp

time: 222 us -> 237 us (1.068)
  the two profiles are of different devices: /device:TPU:16 before, /device:TPU:8 now
where the time goes in v4:
time: 237 us; the launch traced here: 236 us
  blocking collectives  84.7 us (36%)
  waiting for transfers between devices  74.6 us (31%)
  starting transfers between devices  46.4 us (20%)
  Pallas kernels  14.8 us (6%)
  local copies, waits for them, and re-layouts  10.2 us (4%)
  between operations  2.59 us (1%)
  other arithmetic  2.37 us (1%)
    all_to_all x5, blocking collectives, exchange(): return lax.all_to_all(blocks, axes, 0, 0, tiled=True)  84.7 us
    all_to_all x3, waiting for transfers between devices, exchange(): return lax.all_to_all(blocks, axes, 0, 0, tiled=True)  35.5 us
    ppermute x3, waiting for transfers between devices, shards(): pieces.append(lax.ppermute(mine, ('yl', 'yh'), pairs))  32.9 us
    all_to_all x3, starting transfers between devices, exchange(): return lax.all_to_all(blocks, axes, 0, 0, tiled=True)  25.6 us
    pallas_call x8, Pallas kernels, call(): pl.pallas_call(kernel, out_shape=outs, in_specs=[pl.BlockSpec(memory_spac...  14.8 us
    ppermute x3, starting transfers between devices, shards(): pieces.append(lax.ppermute(mine, ('yl', 'yh'), pairs))  14.1 us
    ppermute x3, starting transfers between devices, swap_cores(): return lax.ppermute(value, 'c', [(0, 1), (1, 0)])  6.6 us
    ppermute x3, waiting for transfers between devices, swap_cores(): return lax.ppermute(value, 'c', [(0, 1), (1, 0)])  6.18 us
  transfers between devices with their start and end apart: 9, of which 7 were waited for; matrix products, arithmetic and copies ran while one was open for 1% of the time, Pallas kernels for 2%

profile of v4, /device:TPU:8, one launch (start us, length us, event | category | flops | bytes accessed | tf_op | source)
XLA Modules:
  0.0 235.5 jit_solution(14811762905588868609)
XLA Ops:
  2.3 10.2 %all-to-all-start = ((bf16[32,8,1024]{2,1,0:T(8,128)(2,1)}), bf16[32,8,1024]{2,1,0:T(8,128)(2,1)S(1)}, u32[]{:S(2)}, u32[]{:S(2)}) async-start(bf16[32,8,1024]{2,1,0:T(8,128)(2,1)} %bitcast.6), calls=%async_computation | async-start | bytes 1048576 | tf_op jit(solution)/shard_map/all_to_all | solution.py:33
  13.5 4.3 %collective-permute-start.1 = (bf16[128,1024]{1,0:T(8,128)(2,1)S(1)}, bf16[128,1024]{1,0:T(8,128)(2,1)S(1)}, u32[]{:S(2)}, u32[]{:S(2)}) collective-permute-start(bf16[128,1024]{1,0:T(8,128)(2,1)S(1)} %get-tuple-element.41), channel_id=1, source_target_pairs={{6,0},{0,2},{2,4},{4,6},{70,64},{64,66},{66,68},{68,70},{7,1},{1,3... | collective-permute-start | bytes 786440 | tf_op jit(solution)/shard_map/ppermute | solution.py:327
  17.8 3.7 %collective-permute-start = (bf16[128,1024]{1,0:T(8,128)(2,1)S(1)}, bf16[128,1024]{1,0:T(8,128)(2,1)S(1)}, u32[]{:S(2)}, u32[]{:S(2)}) collective-permute-start(bf16[128,1024]{1,0:T(8,128)(2,1)S(1)} %get-tuple-element.41), channel_id=1, source_target_pairs={{2,0},{4,2},{6,4},{0,6},{66,64},{68,66},{70,68},{64,70},{3,1},{5,3... | collective-permute-start | bytes 786440 | tf_op jit(solution)/shard_map/ppermute | solution.py:327
  21.5 16.4 %collective-permute-done.1 = bf16[128,1024]{1,0:T(8,128)(2,1)S(1)} collective-permute-done((bf16[128,1024]{1,0:T(8,128)(2,1)S(1)}, bf16[128,1024]{1,0:T(8,128)(2,1)S(1)}, u32[]{:S(2)}, u32[]{:S(2)}) %collective-permute-start.1) | collective-permute-done | bytes 262176 | tf_op jit(solution)/shard_map/ppermute | solution.py:327
  40.3 10.4 %all-to-all-start.1 = ((bf16[4,64,4096]{2,1,0:T(8,128)(2,1)}), bf16[4,64,4096]{2,1,0:T(8,128)(2,1)}, u32[]{:S(2)}, u32[]{:S(2)}) async-start(bf16[4,64,4096]{2,1,0:T(8,128)(2,1)} %broadcast_in_dim.51), calls=%async_computation.1 | async-start | bytes 4194304 | tf_op jit(solution)/shard_map/all_to_all | solution.py:33
  50.7 6.2 %collective-permute-start.2 = (bf16[128,1024]{1,0:T(8,128)(2,1)S(1)}, bf16[128,1024]{1,0:T(8,128)(2,1)S(1)}, u32[]{:S(2)}, u32[]{:S(2)}) collective-permute-start(bf16[128,1024]{1,0:T(8,128)(2,1)S(1)} %get-tuple-element.41), channel_id=1, source_target_pairs={{68,0},{70,2},{64,4},{66,6},{4,64},{6,66},{0,68},{2,70},{69,1},{71... | collective-permute-start | bytes 786440 | tf_op jit(solution)/shard_map/ppermute | solution.py:327
  56.9 16.5 %collective-permute-done.2 = bf16[128,1024]{1,0:T(8,128)(2,1)S(1)} collective-permute-done((bf16[128,1024]{1,0:T(8,128)(2,1)S(1)}, bf16[128,1024]{1,0:T(8,128)(2,1)S(1)}, u32[]{:S(2)}, u32[]{:S(2)}) %collective-permute-start.2) | collective-permute-done | bytes 262176 | tf_op jit(solution)/shard_map/ppermute | solution.py:327
  74.6 1.9 collective-permute-start.3
  76.6 2.7 %collective-permute-done.3.other_ref = bf16[4,128,1024]{2,1,0:T(8,128)(2,1)} collective-permute-done((bf16[4,128,1024]{2,1,0:T(8,128)(2,1)S(1)}, bf16[4,128,1024]{2,1,0:T(8,128)(2,1)}, u32[]{:S(2)}, u32[]{:S(2)}) %collective-permute-start.3) | collective-permute-done | bytes 1048608 | tf_op jit(solution)/shard_map/ppermute | solution.py:37
  80.9 4.3 %shard_map.86 = (bf16[64,128]{1,0:T(8,128)(2,1)S(1)}, f32[128,8192]{1,0:T(8,128)S(1)}, f32[128,128]{1,0:T(8,128)S(1)}, f32[4,8192]{1,0:T(4,128)S(1)}, f32[4,128]...) custom-call(s32[2]{0:T(128)S(1)} %pad_add_fusion.place_ref, bf16[128,8192]{1,0:T(8,128)(2,1)S(1)} %copy-done, ...), custom_call_target="tpu_custom_call" | custom-call | flops 402653184 | bytes 11257856 | tf_op jit(solution)/shard_map/pallas_call | solution.py:44
  85.2 1.9 copy-done.1
  87.9 18.9 %all-to-all-done.1 = bf16[4,64,4096]{2,1,0:T(8,128)(2,1)} async-done(((bf16[4,64,4096]{2,1,0:T(8,128)(2,1)}), bf16[4,64,4096]{2,1,0:T(8,128)(2,1)}, u32[]{:S(2)}, u32[]{:S(2)}) %all-to-all-start.1) | async-done | bytes 2097184 | tf_op jit(solution)/shard_map/all_to_all | solution.py:33
  106.8 5.0 %all-to-all-start.2 = ((bf16[16,16,1024]{2,1,0:T(8,128)(2,1)}), bf16[16,16,1024]{2,1,0:T(8,128)(2,1)}, u32[]{:S(2)}, u32[]{:S(2)}) async-start(bf16[16,16,1024]{2,1,0:T(8,128)(2,1)} %copy-done.4), calls=%async_computation.2 | async-start | bytes 1048576 | tf_op jit(solution)/shard_map/all_to_all | solution.py:33
  112.5 16.6 %all-to-all-done.2.query_ref = bf16[16,16,1024]{2,1,0:T(8,128)(2,1)} async-done(((bf16[16,16,1024]{2,1,0:T(8,128)(2,1)}), bf16[16,16,1024]{2,1,0:T(8,128)(2,1)}, u32[]{:S(2)}, u32[]{:S(2)}) %all-to-all-start.2) | async-done | bytes 524320 | tf_op jit(solution)/shard_map/all_to_all | solution.py:33
  129.2 3.2 %shard_map.87.own_ref = f32[136,256]{1,0:T(8,128)S(1)} custom-call(bf16[16,16,1024]{2,1,0:T(8,128)(2,1)} %all-to-all-done.2.query_ref, bf16[256,4096]{1,0:T(8,128)(2,1)} %bitcast.13.block_ref), custom_call_target="tpu_custom_call" | custom-call | flops 1073741824 | bytes 2760704 | tf_op jit(solution)/shard_map/pallas_call | solution.py:44
  135.8 11.8 %all_to_all.40.rows_ref = f32[8,1,128]{2,1,0:T(1,128)S(1)} all-to-all(f32[8,1,128]{2,1,0:T(1,128)S(1)} %get-tuple-element.29), channel_id=1, replica_groups=mesh['z'=4,'yl'=2,'x'=8,'yh'=4,'c'=2] {'yl','yh'}, dimensions={0} | all-to-all | bytes 8192 | tf_op jit(solution)/shard_map/all_to_all | solution.py:33
  147.6 16.4 %all_to_all.41.cols_ref = f32[32,1,256]{2,1,0:T(1,128)S(1)} all-to-all(f32[32,1,256]{2,1,0:T(1,128)S(1)} %get-tuple-element.30), channel_id=1, replica_groups=mesh['z'=4,'yl'=2,'x'=8,'yh'=4,'c'=2] {'z','x'}, dimensions={0} | all-to-all | bytes 65536 | tf_op jit(solution)/shard_map/all_to_all | solution.py:33
  164.0 2.4 %shard_map.89 = (bf16[16,16,1024]{2,1,0:T(8,128)(2,1)S(1)}, f32[8,128]{1,0:T(8,128)S(1)}) custom-call(f32[128,256]{1,0:T(8,128)S(1)} %get-tuple-element.27.expo_ref, f32[8,256]{1,0:T(8,128)S(1)} %get-tuple-element.28.aux_ref, f32[128,256]{1,0:T(8,128)S(1)} %compare_convert_fusion.onehot_ref, f32[8,1,128]{2,1,0:T(1,128)S(1)} %all_to_all.40.rows_ref, ...), custom_call_target="tpu_custom_call" | custom-call | flops 536870912 | bytes 2932736 | tf_op jit(solution)/shard_map/pallas_call | solution.py:44
  166.4 16.9 %all_to_all.42.got_ref = bf16[16,16,1024]{2,1,0:T(8,128)(2,1)S(1)} all-to-all(bf16[16,16,1024]{2,1,0:T(8,128)(2,1)S(1)} %get-tuple-element.31), channel_id=1, replica_groups=mesh['z'=4,'yl'=2,'x'=8,'yh'=4,'c'=2] {'yl','yh','c'}, dimensions={0} | all-to-all | bytes 1048576 | tf_op jit(solution)/shard_map/all_to_all | solution.py:33
  183.3 4.2 %shard_map.90 = (bf16[8,32,16,128]{3,2,1,0:T(8,128)(2,1)S(1)}, bf16[8,32,16,128]{3,2,1,0:T(8,128)(2,1)S(1)}) custom-call(s32[2]{0:T(128)S(1)} %pad_add_fusion.place_ref, bf16[16,16,1024]{2,1,0:T(8,128)(2,1)S(1)} %all_to_all.42.got_ref, f32[4,8192]{1,0:T(4,128)S(1)} %get-tuple-element.32.unit_ref, f32[4,128]{1,0:T(4,128)S(1)} %get-tuple-element.33.length_ref, ...), custom_call_target="tpu_custom_call" | custom-call | flops 402653184 | bytes 11257856 | tf_op jit(solution)/shard_map/pallas_call | solution.py:44
  187.5 2.8 %collective-permute-start.5 = (bf16[8,32,16,128]{3,2,1,0:T(8,128)(2,1)S(1)}, bf16[8,32,16,128]{3,2,1,0:T(8,128)(2,1)S(1)}, u32[]{:S(2)}, u32[]{:S(2)}) collective-permute-start(bf16[8,32,16,128]{3,2,1,0:T(8,128)(2,1)S(1)} %get-tuple-element.38), channel_id=1, source_target_pairs={{0,1},{1,0},{2,3},{3,2},{4,5},{5,4},{6,7},{7,6},{8,9},{9,8},{10,11... | collective-permute-start | bytes 3145736 | tf_op jit(solution)/shard_map/ppermute | solution.py:37
  190.2 2.3 collective-permute-done.5.got_ref
  192.7 21.6 %all_to_all.43.got_ref = bf16[8,33,16,128]{3,2,1,0:T(8,128)(2,1)S(1)} all-to-all(bf16[8,33,16,128]{3,2,1,0:T(8,128)(2,1)S(1)} %shard_map.91), channel_id=1, replica_groups=mesh['z'=4,'yl'=2,'x'=8,'yh'=4,'c'=2] {'x'}, dimensions={0} | all-to-all | bytes 2162688 | tf_op jit(solution)/shard_map/all_to_all | solution.py:33
  214.5 18.1 %all_to_all.44.got_ref = bf16[32,32,128]{2,1,0:T(8,128)(2,1)S(1)} all-to-all(bf16[32,32,128]{2,1,0:T(8,128)(2,1)S(1)} %shard_map.92), channel_id=1, replica_groups=mesh['z'=4,'yl'=2,'x'=8,'yh'=4,'c'=2] {'z','yl','yh'}, dimensions={0} | all-to-all | bytes 524288 | tf_op jit(solution)/shard_map/all_to_all | solution.py:33
  (45 shorter events, 14.4 us)
Async XLA Ops:
  2.3 35.6 %all-to-all-start = ((bf16[32,8,1024]{2,1,0:T(8,128)(2,1)}), bf16[32,8,1024]{2,1,0:T(8,128)(2,1)S(1)}, u32[]{:S(2)}, u32[]{:S(2)}) async-start(bf16[32,8,1024]{2,1,0:T(8,128)(2,1)} %bitcast.6), calls=%async_computation | async-start | bytes 1048576 | tf_op jit(solution)/shard_map/all_to_all | solution.py:33
  13.5 24.3 %collective-permute-start.1 = (bf16[128,1024]{1,0:T(8,128)(2,1)S(1)}, bf16[128,1024]{1,0:T(8,128)(2,1)S(1)}, u32[]{:S(2)}, u32[]{:S(2)}) collective-permute-start(bf16[128,1024]{1,0:T(8,128)(2,1)S(1)} %get-tuple-element.41), channel_id=1, source_target_pairs={{6,0},{0,2},{2,4},{4,6},{70,64},{64,66},{66,68},{68,70},{7,1},{1,3... | collective-permute-start | bytes 786440 | tf_op jit(solution)/shard_map/ppermute | solution.py:327
  17.8 20.1 %collective-permute-start = (bf16[128,1024]{1,0:T(8,128)(2,1)S(1)}, bf16[128,1024]{1,0:T(8,128)(2,1)S(1)}, u32[]{:S(2)}, u32[]{:S(2)}) collective-permute-start(bf16[128,1024]{1,0:T(8,128)(2,1)S(1)} %get-tuple-element.41), channel_id=1, source_target_pairs={{2,0},{4,2},{6,4},{0,6},{66,64},{68,66},{70,68},{64,70},{3,1},{5,3... | collective-permute-start | bytes 786440 | tf_op jit(solution)/shard_map/ppermute | solution.py:327
  37.9 2.4 %copy-start.6 = (bf16[128,1024]{1,0:T(8,128)(2,1)}, bf16[128,1024]{1,0:T(8,128)(2,1)S(1)}, u32[]{:S(2)}) copy-start(bf16[128,1024]{1,0:T(8,128)(2,1)S(1)} %collective-permute-done.1) | copy-start | bytes 786436
  37.9 0.7 copy-start.7
  40.3 39.0 %copy-start.5 = (f32[8192]{0:T(1024)S(1)}, f32[8192]{0:T(1024)}, u32[]{:S(2)}) copy-start(f32[8192]{0:T(1024)} %param.9) | copy-start | bytes 98308
  40.3 66.6 %all-to-all-start.1 = ((bf16[4,64,4096]{2,1,0:T(8,128)(2,1)}), bf16[4,64,4096]{2,1,0:T(8,128)(2,1)}, u32[]{:S(2)}, u32[]{:S(2)}) async-start(bf16[4,64,4096]{2,1,0:T(8,128)(2,1)} %broadcast_in_dim.51), calls=%async_computation.1 | async-start | bytes 4194304 | tf_op jit(solution)/shard_map/all_to_all | solution.py:33
  50.7 28.6 %copy-start = (bf16[128,8192]{1,0:T(8,128)(2,1)S(1)}, bf16[128,8192]{1,0:T(8,128)(2,1)}, u32[]{:S(2)}) copy-start(bf16[128,8192]{1,0:T(8,128)(2,1)} %in_ref.3) | copy-start | bytes 6291460
  50.7 22.7 %collective-permute-start.2 = (bf16[128,1024]{1,0:T(8,128)(2,1)S(1)}, bf16[128,1024]{1,0:T(8,128)(2,1)S(1)}, u32[]{:S(2)}, u32[]{:S(2)}) collective-permute-start(bf16[128,1024]{1,0:T(8,128)(2,1)S(1)} %get-tuple-element.41), channel_id=1, source_target_pairs={{68,0},{70,2},{64,4},{66,6},{4,64},{6,66},{0,68},{2,70},{69,1},{71... | collective-permute-start | bytes 786440 | tf_op jit(solution)/shard_map/ppermute | solution.py:327
  74.6 4.7 %collective-permute-start.3 = (bf16[4,128,1024]{2,1,0:T(8,128)(2,1)S(1)}, bf16[4,128,1024]{2,1,0:T(8,128)(2,1)}, u32[]{:S(2)}, u32[]{:S(2)}) collective-permute-start(bf16[4,128,1024]{2,1,0:T(8,128)(2,1)S(1)} %pad_maximum_fusion.own_ref), channel_id=1, source_target_pairs={{0,1},{1,0},{2,3},{3,2},{4,5},{5,4},{6,7},{7,6},{8,9},{9,8},{10,11... | collective-permute-start | bytes 3145736 | tf_op jit(solution)/shard_map/ppermute | solution.py:37
  79.3 1.6 copy-start.3
  80.9 31.2 %copy-start.8 = (s32[32]{0:T(128)S(1)}, s32[32]{0:T(128)}, u32[]{:S(2)}) copy-start(s32[32]{0:T(128)} %param.13) | copy-start | bytes 388
  85.2 1.9 copy-start.1
  87.2 0.8 copy-start.4
  106.8 22.3 %all-to-all-start.2 = ((bf16[16,16,1024]{2,1,0:T(8,128)(2,1)}), bf16[16,16,1024]{2,1,0:T(8,128)(2,1)}, u32[]{:S(2)}, u32[]{:S(2)}) async-start(bf16[16,16,1024]{2,1,0:T(8,128)(2,1)} %copy-done.4), calls=%async_computation.2 | async-start | bytes 1048576 | tf_op jit(solution)/shard_map/all_to_all | solution.py:33
  129.2 54.1 %copy-start.2 = (f32[128,8192]{1,0:T(8,128)S(1)}, f32[128,8192]{1,0:T(8,128)}, u32[]{:S(2)}) copy-start(f32[128,8192]{1,0:T(8,128)} %copy-done.1) | copy-start | bytes 12582916
  132.4 3.3 %collective-permute-start.4 = (f32[136,256]{1,0:T(8,128)S(1)}, f32[136,256]{1,0:T(8,128)S(1)}, u32[]{:S(2)}, u32[]{:S(2)}) collective-permute-start(f32[136,256]{1,0:T(8,128)S(1)} %shard_map.87.own_ref), channel_id=1, source_target_pairs={{0,1},{1,0},{2,3},{3,2},{4,5},{5,4},{6,7},{7,6},{8,9},{9,8},{10,11... | collective-permute-start | bytes 417800 | tf_op jit(solution)/shard_map/ppermute | solution.py:37
  187.5 5.0 %collective-permute-start.5 = (bf16[8,32,16,128]{3,2,1,0:T(8,128)(2,1)S(1)}, bf16[8,32,16,128]{3,2,1,0:T(8,128)(2,1)S(1)}, u32[]{:S(2)}, u32[]{:S(2)}) collective-permute-start(bf16[8,32,16,128]{3,2,1,0:T(8,128)(2,1)S(1)} %get-tuple-element.38), channel_id=1, source_target_pairs={{0,1},{1,0},{2,3},{3,2},{4,5},{5,4},{6,7},{7,6},{8,9},{9,8},{10,11... | collective-permute-start | bytes 3145736 | tf_op jit(solution)/shard_map/ppermute | solution.py:37

commit v5 on v4

--- a/solution.py
+++ b/solution.py
@@ -15,8 +15,9 @@
 inv_temp = 20.0
 norm_eps = 1e-05
 
-AXES = ("z", "yl", "x", "yh", "c")
-SIZES = (4, 2, 8, 4, 2)
+AXES = ("zh", "zl", "yl", "x", "yh", "c")
+SIZES = (4, 2, 2, 4, 4, 2)
+ROW, COLUMN, RING = ("zl", "yh"), ("zh", "yl", "x"), ("zl", "yh", "c")
 MIB = 1 << 20
 f32, bf16 = jnp.float32, jnp.bfloat16
 
@@ -59,15 +60,44 @@
     return jax.ShapeDtypeStruct(*pair)
 
 
-def adapter_slices(place_ref, own_ref, other_ref):
+def pack(nyh, zh_ref, down_ref, up_ref, passages_ref, out_ref):
+    peers, both, _ = out_ref.shape
+    nzh = peers // nyh
+    part = 2 * down_ref.shape[0] // nzh
+    at = pl.ds(pl.multiple_of(lax.rem(zh_ref[0], nzh // 2) * part, part), part)
+    mine = jnp.where(zh_ref[0] < nzh // 2, down_ref[at, :].astype(f32), up_ref[at, :].astype(f32))
+    passages = passages_ref[...].astype(f32)
+    rows = both - part
+    for yh in range(nyh):
+        block = jnp.concatenate([mine, passages[yh * rows:(yh + 1) * rows]], axis=0).astype(bf16)
+        for zh in range(nzh):
+            out_ref[zh * nyh + yh] = block
+
+
+def unpack(nyh, got_ref, mats_ref, out_ref):
+    peers, both, feats = got_ref.shape
+    nzh = peers // nyh
+    part = mats_ref.shape[1] // nzh
+    for yh in range(nyh):
+        passages = []
+        for zh in range(nzh):
+            block = got_ref[zh * nyh + yh].astype(f32)
+            mats_ref[yh, zh * part:(zh + 1) * part, :] = block[:part].astype(bf16)
+            passages.append(block[part:])
+        passages = jnp.concatenate(passages, axis=0).astype(bf16)
+        for i in range(out_ref.shape[0]):
+            out_ref[i, :, yh * feats:(yh + 1) * feats] = passages
+
+
+def adapter_slices(core_ref, own_ref, other_ref):
     nyh, _, feats = own_ref.shape
-    for k in range(nyh):
-        for ref, core in ((own_ref, place_ref[1]), (other_ref, 1 - place_ref[1])):
-            at = (lax.rem(place_ref[0] + k, nyh) * 2 + core) * feats
-            yield ref.at[k], pl.ds(pl.multiple_of(at, feats), feats)
-
-
-def forward(nyh, nc, place_ref, in_ref, frozen_ref, gain_ref, own_ref, other_ref,
+    for yh in range(nyh):
+        for ref, core in ((own_ref, core_ref[0]), (other_ref, 1 - core_ref[0])):
+            at = (yh * 2 + core) * feats
+            yield ref.at[yh], pl.ds(pl.multiple_of(at, feats), feats)
+
+
+def forward(nyh, nc, core_ref, in_ref, frozen_ref, gain_ref, own_ref, other_ref,
             latent_ref, hidden_ref, inv_ref, unit_ref, length_ref, send_ref, part_ref):
     _, both, feats = own_ref.shape
     slices = nyh * nc
@@ -76,7 +106,7 @@
     queries = tokens // LEN
     acc = jnp.zeros((tokens, rank), f32)
     acc_t = jnp.zeros((rank, tokens), f32)
-    for mats_ref, at in adapter_slices(place_ref, own_ref, other_ref):
+    for mats_ref, at in adapter_slices(core_ref, own_ref, other_ref):
         part = in_ref[:, at]
         down = mats_ref[:rank]
         acc += dot_rows(part, down)
@@ -84,7 +114,7 @@
     latent = acc.astype(bf16)
     latent_ref[...] = acc_t.astype(bf16)
     squares = jnp.zeros((tokens, 1), f32)
-    for mats_ref, at in adapter_slices(place_ref, own_ref, other_ref):
+    for mats_ref, at in adapter_slices(core_ref, own_ref, other_ref):
         hidden = frozen_ref[:, at].astype(f32) + adapter_scale_factor * dot(
             latent, mats_ref[rank:]
         )
@@ -193,7 +223,7 @@
     out_ref[...] = total_ref[...].astype(bf16).reshape(out_ref.shape)
 
 
-def backward(nyh, nc, place_ref, got_ref, unit_ref, length_ref, inv_ref, hidden_ref, gain_ref,
+def backward(nyh, nc, core_ref, got_ref, unit_ref, length_ref, inv_ref, hidden_ref, gain_ref,
              in_ref, own_ref, other_ref, latent_ref, keep_ref, send_ref,
              grad_ref, scaled_ref, up_ref, hg_ref):
     _, both, feats = own_ref.shape
@@ -227,7 +257,7 @@
     factor = inv * inv * inv * (jnp.concatenate(mean, axis=0) / width)
     latent_t = latent_ref[...]
     acc = jnp.zeros((rank, tokens), f32)
-    for mats_ref, at in adapter_slices(place_ref, own_ref, other_ref):
+    for mats_ref, at in adapter_slices(core_ref, own_ref, other_ref):
         for q in range(queries):
             of = slice(q * LEN, (q + 1) * LEN)
             hg_ref[of] = (
@@ -237,7 +267,7 @@
         acc += dot_rows(mats_ref[rank:], hidden_grad)
         up_ref[:, at] = adapter_scale_factor * dot(latent_t, hidden_grad)
     latent_grad = (adapter_scale_factor * acc).astype(bf16)
-    first = place_ref[1] == 0
+    first = core_ref[0] == 0
     for f in range(slices):
         down = dot(latent_grad, in_ref[:, f * feats:(f + 1) * feats])
         for x in range(nx):
@@ -295,9 +325,8 @@
 
 
 def shards(sizes, adapter_in, frozen, gain, adapter_a, adapter_up_matrix, passages, positive):
-    nz, nyl, nx, nyh, nc = sizes
-    ny = nyl * nyh
-    iz, iyl, ix, iyh, ic = (lax.axis_index(axis) for axis in AXES)
+    nzh, nzl, nyl, nx, nyh, nc = sizes
+    izh, izl, iyl, ix, iyh, ic = (lax.axis_index(axis) for axis in AXES)
     rank = adapter_up_matrix.shape[0]
     feats = passages.shape[1]
     half = nyh * feats
@@ -306,35 +335,30 @@
     queries = tokens // LEN
     group = passages.shape[0]
     rows = group // nyh
+    ny = nzl * nyh
     ring = ny * nc
-    members = nz * nx
+    members = nzh * nyl * nx
     shape = jax.ShapeDtypeStruct
     gain = gain.reshape(1, width)
-
-    sent = jnp.broadcast_to(passages.reshape(1, nyh, rows, feats), (nx, nyh, rows, feats))
-    got = exchange(sent.reshape(nx * nyh, rows, feats), ("x", "yh"))
-    got = got.reshape(nx, nyh, rows, feats).transpose(0, 2, 1, 3).reshape(nx * rows, half)
-
-    mine = jnp.concatenate([adapter_a.T, adapter_up_matrix], axis=0)
-    pieces = [mine]
-    for k in range(1, nyh):
-        flip = 2 * k == nyh
-        pairs = []
-        for yl in range(nyl):
-            for yh in range(nyh):
-                source = (nyl - 1 - yl if flip else yl) * nyh + (yh + k) % nyh
-                pairs.append((source, yl * nyh + yh))
-        pieces.append(lax.ppermute(mine, ("yl", "yh"), pairs))
-    early = [k for k in range(1, nyh) if 2 * k != nyh]
-    got, *arrived = lax.optimization_barrier((got, *[pieces[k] for k in early]))
-    for k, piece in zip(early, arrived):
-        pieces[k] = piece
-    own_mats = jnp.stack(pieces)
+    core = ic.astype(jnp.int32).reshape(1)
+
+    part = 2 * rank // nzh
+    (sent,) = call(
+        functools.partial(pack, nyh),
+        [shape((nzh * nyh, part + rows, feats), bf16)],
+        [izh.astype(jnp.int32).reshape(1), adapter_a.T, adapter_up_matrix, passages],
+        scalars=1,
+    )
+    own_mats, sent = call(
+        functools.partial(unpack, nyh),
+        [
+            shape((nyh, 2 * rank, feats), bf16),
+            shape((nyl * nx, nzh * rows, half), bf16),
+        ],
+        [exchange(sent, ("zh", "yh"))],
+    )
     other_mats = swap_cores(own_mats)
-    place = jnp.stack([iyh, ic]).astype(jnp.int32)
-
-    got = jnp.broadcast_to(got[None], (nz, nx * rows, half))
-    block = exchange(got, "z").reshape(members * rows, half)
+    block = exchange(sent, ("yl", "x")).reshape(members * rows, half)
     columns = block.shape[0]
 
     latent_t, hidden, inv, unit, length, sent = call(
@@ -347,20 +371,20 @@
             shape((queries, 128), f32),
             shape((ring, nyh * queries, feats), bf16),
         ],
-        [place, adapter_in, frozen, gain, own_mats, other_mats],
+        [core, adapter_in, frozen, gain, own_mats, other_mats],
         scratch=[((nc, nyh * queries, feats), f32)],
         scalars=1,
         flops=6 * tokens * rank * width,
     )
     sent, block = lax.optimization_barrier((sent, block))
-    query = exchange(sent, ("yl", "yh", "c"))
+    query = exchange(sent, RING)
 
     count = ring * 8
     at = lax.iota(jnp.int32, columns)
-    at_z, at_x, at_row = at // (nx * rows), at // rows % nx, at % rows
-    passage_id = ((at_z * nyl + iyl) * nx + at_x) * group + iyh * rows + at_row
+    at_xy, at_zh, at_row = at // (nzh * rows), at // rows % nzh, at % rows
+    passage_id = ((at_zh * nzl + izl) * nyl * nx + at_xy) * group + iyh * rows + at_row
     own_pos = jnp.where(
-        lax.iota(jnp.int32, nyl)[:, None] == iyl, positive[None, :], -1
+        lax.iota(jnp.int32, nzl)[:, None] == izl, positive[None, :], -1
     ).reshape(ring, 1, queries)
     own_pos = jnp.broadcast_to(own_pos, (ring, 8 // queries, queries)).reshape(count)
     onehot = (own_pos[:, None] == passage_id[None, :]).astype(f32)
@@ -381,8 +405,8 @@
         ],
         [own, other, onehot],
     )
-    by_row = exchange(by_row, ("yl", "yh"))
-    by_col = exchange(by_col, ("z", "x"))
+    by_row = exchange(by_row, ROW)
+    by_col = exchange(by_col, COLUMN)
     sent, loss = call(
         functools.partial(weigh, nyh),
         [shape((ring, nyh * queries, feats), bf16), shape((8, 128), f32)],
@@ -390,15 +414,15 @@
         scratch=[((ring * nyh * queries, feats), f32)],
         flops=2 * ring * nyh * queries * columns * half,
     )
-    got = exchange(sent, ("yl", "yh", "c"))
+    got = exchange(sent, RING)
 
     out_rows = rank // (nyh * nc)
-    cols = width // (nz * nyl * nx)
-    blocks = nz * ny
+    cols = width // (nzh * nzl * nyl * nx)
+    blocks = nzh * ny
     keep, send = call(
         functools.partial(backward, nyh, nc),
-        [shape((nx, blocks, 2 * out_rows, cols), bf16)] * 2,
-        [place, got, unit, length, inv, hidden, gain, adapter_in, own_mats, other_mats, latent_t],
+        [shape((nyl * nx, blocks, 2 * out_rows, cols), bf16)] * 2,
+        [core, got, unit, length, inv, hidden, gain, adapter_in, own_mats, other_mats, latent_t],
         scratch=[
             ((nc, nyh * queries, feats), f32),
             ((queries, width), f32),
@@ -410,26 +434,26 @@
     )
     (chip,) = call(
         join,
-        [shape((nx, blocks + 1, 2 * out_rows, cols), bf16)],
+        [shape((nyl * nx, blocks + 1, 2 * out_rows, cols), bf16)],
         [keep, swap_cores(send), loss],
     )
     (line,) = call(
-        add_line, [shape((blocks, 4 * out_rows, cols), bf16)], [exchange(chip, "x")]
+        add_line, [shape((blocks, 4 * out_rows, cols), bf16)], [exchange(chip, ("yl", "x"))]
     )
     (last,) = call(
         add_last,
         [shape((2 * out_rows + 8, cols), f32)],
-        [exchange(line, ("z", "yl", "yh"))],
+        [exchange(line, ("zh", "zl", "yh"))],
     )
     adapter_grads = last[: 2 * out_rows].reshape(2, out_rows, cols)
-    total_pairs = group * nz * nyl * nx
+    total_pairs = group * nzl * members
     loss = last[2 * out_rows, 0] / (2.0 * total_pairs) + inv_temp
     return (adapter_grads, loss)
 
 
 def build(mesh, sizes):
     split = Mesh(mesh.devices.reshape(sizes), AXES)
-    dp, fsdp = ("z", "yl", "x"), ("yh", "c")
+    dp, fsdp = ("zh", "zl", "yl", "x"), ("yh", "c")
     placed = (
         P(AXES, None),
         P(AXES, None),

time: 237 us -> 220 us (0.928)
  blocking collectives: 84.7 us -> 132 us
  waiting for transfers between devices: 74.6 us -> 33.6 us
  starting transfers between devices: 46.4 us -> 25.3 us
    all_to_all x5 -> x6, blocking collectives: 84.7 us -> 132 us  [exchange(): return lax.all_to_all(blocks, axes, 0, 0, tiled=True)]
    ppermute x3 -> x0, waiting for transfers between devices: 32.9 us -> none  [shards(): pieces.append(lax.ppermute(mine, ('yl', 'yh'), pairs))]
    ppermute x3 -> x0, starting transfers between devices: 14.1 us -> none  [shards(): pieces.append(lax.ppermute(mine, ('yl', 'yh'), pairs))]
    all_to_all x3 -> x2, waiting for transfers between devices: 35.5 us -> 27.3 us  [exchange(): return lax.all_to_all(blocks, axes, 0, 0, tiled=True)]
    all_to_all x3 -> x2, starting transfers between devices: 25.6 us -> 18.6 us  [exchange(): return lax.all_to_all(blocks, axes, 0, 0, tiled=True)]
    broadcast_in_dim x8 -> x6, local copies, waits for them, and re-layouts: 3.75 us -> 0.41 us  [shards(): jnp.where(lax.iota(jnp.int32, nzl)[:, None] == izl, positive[None, :], -1)]
    unnamed x18 -> x22, local copies, waits for them, and re-layouts: 5.08 us -> 8.34 us
    pallas_call x8 -> x10, Pallas kernels: 14.8 us -> 15.2 us  [call(): pl.pallas_call(kernel, out_shape=outs, in_specs=[pl.BlockSpec(memory_spac...]
  transfers between devices with their start and end apart: 9 -> 5, of which waited for: 7 -> 5; matrix products, arithmetic and copies ran while one was open for 1% -> 0% of each run, Pallas kernels for 2% -> 2%
where the time goes in v5:
time: 220 us; the launch traced here: 219 us
  blocking collectives  132 us (60%)
  waiting for transfers between devices  33.6 us (15%)
  starting transfers between devices  25.3 us (12%)
  Pallas kernels  15.2 us (7%)
  local copies, waits for them, and re-layouts  10.1 us (5%)
  between operations  2.57 us (1%)
    all_to_all x6, blocking collectives, exchange(): return lax.all_to_all(blocks, axes, 0, 0, tiled=True)  132 us
    all_to_all x2, waiting for transfers between devices, exchange(): return lax.all_to_all(blocks, axes, 0, 0, tiled=True)  27.3 us
    all_to_all x2, starting transfers between devices, exchange(): return lax.all_to_all(blocks, axes, 0, 0, tiled=True)  18.6 us
    pallas_call x10, Pallas kernels, call(): pl.pallas_call(kernel, out_shape=outs, in_specs=[pl.BlockSpec(memory_spac...  15.2 us
    unnamed x22, local copies, waits for them, and re-layouts  8.34 us
    ppermute x3, starting transfers between devices, swap_cores(): return lax.ppermute(value, 'c', [(0, 1), (1, 0)])  6.63 us
    ppermute x3, waiting for transfers between devices, swap_cores(): return lax.ppermute(value, 'c', [(0, 1), (1, 0)])  6.2 us
  transfers between devices with their start and end apart: 5, of which 5 were waited for; matrix products, arithmetic and copies ran while one was open for 0% of the time, Pallas kernels for 2%

profile of v5, /device:TPU:8, one launch (start us, length us, event | category | flops | bytes accessed | tf_op | source)
XLA Modules:
  0.0 219.0 jit_solution(18164491482695934591)
XLA Ops:
  1.5 0.9 copy-done.8
  3.4 47.8 %all_to_all.40.got_ref = bf16[16,40,1024]{2,1,0:T(8,128)(2,1)S(1)} all-to-all(bf16[16,40,1024]{2,1,0:T(8,128)(2,1)S(1)} %shard_map.86), channel_id=1, replica_groups=mesh['zh'=4,'zl'=2,'yl'=2,'x'=4,'yh'=4,'c'=2] {'zh','yh'}, dimensions={0} | all-to-all | bytes 2621440 | tf_op jit(solution)/shard_map/all_to_all | solution.py:34
  51.4 1.4 copy-done.4
  52.7 11.7 %all-to-all-start.1 = ((bf16[8,32,4096]{2,1,0:T(8,128)(2,1)}), bf16[8,32,4096]{2,1,0:T(8,128)(2,1)}, u32[]{:S(2)}, u32[]{:S(2)}) async-start(bf16[8,32,4096]{2,1,0:T(8,128)(2,1)} %copy-done.4), calls=%async_computation.1 | async-start | bytes 4194304 | tf_op jit(solution)/shard_map/all_to_all | solution.py:34
  64.5 1.9 collective-permute-start
  66.4 2.8 %collective-permute-done.other_ref = bf16[4,128,1024]{2,1,0:T(8,128)(2,1)} collective-permute-done((bf16[4,128,1024]{2,1,0:T(8,128)(2,1)S(1)}, bf16[4,128,1024]{2,1,0:T(8,128)(2,1)}, u32[]{:S(2)}, u32[]{:S(2)}) %collective-permute-start) | collective-permute-done | bytes 1048608 | tf_op jit(solution)/shard_map/ppermute | solution.py:38
  69.2 1.6 copy-done.3
  70.8 4.4 %shard_map.88 = (bf16[64,128]{1,0:T(8,128)(2,1)S(1)}, f32[128,8192]{1,0:T(8,128)S(1)}, f32[128,128]{1,0:T(8,128)S(1)}, f32[4,8192]{1,0:T(4,128)S(1)}, f32[4,128]...) custom-call(s32[1]{0:T(128)} %bitcast.core_ref, bf16[128,8192]{1,0:T(8,128)(2,1)S(1)} %copy-done, ...), custom_call_target="tpu_custom_call" | custom-call | flops 402653184 | bytes 11257856 | tf_op jit(solution)/shard_map/pallas_call | solution.py:45
  75.2 1.9 copy-done.1
  77.9 10.6 %all-to-all-done.1 = bf16[8,32,4096]{2,1,0:T(8,128)(2,1)} async-done(((bf16[8,32,4096]{2,1,0:T(8,128)(2,1)}), bf16[8,32,4096]{2,1,0:T(8,128)(2,1)}, u32[]{:S(2)}, u32[]{:S(2)}) %all-to-all-start.1) | async-done | bytes 2097184 | tf_op jit(solution)/shard_map/all_to_all | solution.py:34
  88.5 6.9 %all-to-all-start.2 = ((bf16[16,16,1024]{2,1,0:T(8,128)(2,1)}), bf16[16,16,1024]{2,1,0:T(8,128)(2,1)}, u32[]{:S(2)}, u32[]{:S(2)}) async-start(bf16[16,16,1024]{2,1,0:T(8,128)(2,1)} %copy-done.5), calls=%async_computation.2 | async-start | bytes 1048576 | tf_op jit(solution)/shard_map/all_to_all | solution.py:34
  96.1 16.7 %all-to-all-done.2.query_ref = bf16[16,16,1024]{2,1,0:T(8,128)(2,1)} async-done(((bf16[16,16,1024]{2,1,0:T(8,128)(2,1)}), bf16[16,16,1024]{2,1,0:T(8,128)(2,1)}, u32[]{:S(2)}, u32[]{:S(2)}) %all-to-all-start.2) | async-done | bytes 524320 | tf_op jit(solution)/shard_map/all_to_all | solution.py:34
  112.8 3.2 %shard_map.89.own_ref = f32[136,256]{1,0:T(8,128)S(1)} custom-call(bf16[16,16,1024]{2,1,0:T(8,128)(2,1)} %all-to-all-done.2.query_ref, bf16[256,4096]{1,0:T(8,128)(2,1)} %bitcast.4.block_ref), custom_call_target="tpu_custom_call" | custom-call | flops 1073741824 | bytes 2760704 | tf_op jit(solution)/shard_map/pallas_call | solution.py:45
  116.0 2.0 collective-permute-start.1
  118.1 1.2 collective-permute-done.1.other_ref
  119.5 12.0 %all_to_all.41.rows_ref = f32[8,1,128]{2,1,0:T(1,128)S(1)} all-to-all(f32[8,1,128]{2,1,0:T(1,128)S(1)} %get-tuple-element.27), channel_id=1, replica_groups=mesh['zh'=4,'zl'=2,'yl'=2,'x'=4,'yh'=4,'c'=2] {'zl','yh'}, dimensions={0} | all-to-all | bytes 8192 | tf_op jit(solution)/shard_map/all_to_all | solution.py:34
  131.5 15.9 %all_to_all.42.cols_ref = f32[32,1,256]{2,1,0:T(1,128)S(1)} all-to-all(f32[32,1,256]{2,1,0:T(1,128)S(1)} %get-tuple-element.28), channel_id=1, replica_groups=mesh['zh'=4,'zl'=2,'yl'=2,'x'=4,'yh'=4,'c'=2] {'zh','yl','x'}, dimensions={0} | all-to-all | bytes 65536 | tf_op jit(solution)/shard_map/all_to_all | solution.py:34
  147.4 2.4 %shard_map.91 = (bf16[16,16,1024]{2,1,0:T(8,128)(2,1)S(1)}, f32[8,128]{1,0:T(8,128)S(1)}) custom-call(f32[128,256]{1,0:T(8,128)S(1)} %get-tuple-element.25.expo_ref, f32[8,256]{1,0:T(8,128)S(1)} %get-tuple-element.26.aux_ref, f32[128,256]{1,0:T(8,128)S(1)} %compare_convert_fusion.onehot_ref, f32[8,1,128]{2,1,0:T(1,128)S(1)} %all_to_all.41.rows_ref, ...), custom_call_target="tpu_custom_call" | custom-call | flops 536870912 | bytes 2932736 | tf_op jit(solution)/shard_map/pallas_call | solution.py:45
  149.9 16.9 %all_to_all.43.got_ref = bf16[16,16,1024]{2,1,0:T(8,128)(2,1)S(1)} all-to-all(bf16[16,16,1024]{2,1,0:T(8,128)(2,1)S(1)} %get-tuple-element.29), channel_id=1, replica_groups=mesh['zh'=4,'zl'=2,'yl'=2,'x'=4,'yh'=4,'c'=2] {'zl','yh','c'}, dimensions={0} | all-to-all | bytes 1048576 | tf_op jit(solution)/shard_map/all_to_all | solution.py:34
  166.8 4.2 %shard_map.92 = (bf16[8,32,16,128]{3,2,1,0:T(8,128)(2,1)S(1)}, bf16[8,32,16,128]{3,2,1,0:T(8,128)(2,1)S(1)}) custom-call(s32[1]{0:T(128)} %bitcast.core_ref, bf16[16,16,1024]{2,1,0:T(8,128)(2,1)S(1)} %all_to_all.43.got_ref, f32[4,8192]{1,0:T(4,128)S(1)} %get-tuple-element.30.unit_ref, f32[4,128]{1,0:T(4,128)S(1)} %get-tuple-element.31.length_ref, ...), custom_call_target="tpu_custom_call" | custom-call | flops 402653184 | bytes 11257856 | tf_op jit(solution)/shard_map/pallas_call | solution.py:45
  170.9 2.7 %collective-permute-start.2 = (bf16[8,32,16,128]{3,2,1,0:T(8,128)(2,1)S(1)}, bf16[8,32,16,128]{3,2,1,0:T(8,128)(2,1)S(1)}, u32[]{:S(2)}, u32[]{:S(2)}) collective-permute-start(bf16[8,32,16,128]{3,2,1,0:T(8,128)(2,1)S(1)} %get-tuple-element.36), channel_id=1, source_target_pairs={{0,1},{1,0},{2,3},{3,2},{4,5},{5,4},{6,7},{7,6},{8,9},{9,8},{10,11... | collective-permute-start | bytes 3145736 | tf_op jit(solution)/shard_map/ppermute | solution.py:38
  173.7 2.3 %collective-permute-done.2.got_ref = bf16[8,32,16,128]{3,2,1,0:T(8,128)(2,1)S(1)} collective-permute-done((bf16[8,32,16,128]{3,2,1,0:T(8,128)(2,1)S(1)}, bf16[8,32,16,128]{3,2,1,0:T(8,128)(2,1)S(1)}, u32[]{:S(2)}, u32[]{:S(2)}) %collective-permute-start.2) | collective-permute-done | bytes 1048608 | tf_op jit(solution)/shard_map/ppermute | solution.py:38
  176.2 21.6 %all_to_all.44.got_ref = bf16[8,33,16,128]{3,2,1,0:T(8,128)(2,1)S(1)} all-to-all(bf16[8,33,16,128]{3,2,1,0:T(8,128)(2,1)S(1)} %shard_map.93), channel_id=1, replica_groups=mesh['zh'=4,'zl'=2,'yl'=2,'x'=4,'yh'=4,'c'=2] {'yl','x'}, dimensions={0} | all-to-all | bytes 2162688 | tf_op jit(solution)/shard_map/all_to_all | solution.py:34
  198.0 18.1 %all_to_all.45.got_ref = bf16[32,32,128]{2,1,0:T(8,128)(2,1)S(1)} all-to-all(bf16[32,32,128]{2,1,0:T(8,128)(2,1)S(1)} %shard_map.94), channel_id=1, replica_groups=mesh['zh'=4,'zl'=2,'yl'=2,'x'=4,'yh'=4,'c'=2] {'zh','zl','yh'}, dimensions={0} | all-to-all | bytes 524288 | tf_op jit(solution)/shard_map/all_to_all | solution.py:34
  (39 shorter events, 5.4 us)
Async XLA Ops:
  0.6 0.9 copy-start.7
  1.5 0.9 copy-start.8
  2.4 0.8 copy-start.9
  51.4 1.4 copy-start.4
  52.7 16.4 %copy-start = (bf16[128,8192]{1,0:T(8,128)(2,1)S(1)}, bf16[128,8192]{1,0:T(8,128)(2,1)}, u32[]{:S(2)}) copy-start(bf16[128,8192]{1,0:T(8,128)(2,1)} %in_ref.3) | copy-start | bytes 6291460
  52.7 16.4 %copy-start.6 = (f32[8192]{0:T(1024)S(1)}, f32[8192]{0:T(1024)}, u32[]{:S(2)}) copy-start(f32[8192]{0:T(1024)} %param.9) | copy-start | bytes 98308
  52.7 35.8 %all-to-all-start.1 = ((bf16[8,32,4096]{2,1,0:T(8,128)(2,1)}), bf16[8,32,4096]{2,1,0:T(8,128)(2,1)}, u32[]{:S(2)}, u32[]{:S(2)}) async-start(bf16[8,32,4096]{2,1,0:T(8,128)(2,1)} %copy-done.4), calls=%async_computation.1 | async-start | bytes 4194304 | tf_op jit(solution)/shard_map/all_to_all | solution.py:34
  64.5 4.7 %collective-permute-start = (bf16[4,128,1024]{2,1,0:T(8,128)(2,1)S(1)}, bf16[4,128,1024]{2,1,0:T(8,128)(2,1)}, u32[]{:S(2)}, u32[]{:S(2)}) collective-permute-start(bf16[4,128,1024]{2,1,0:T(8,128)(2,1)S(1)} %get-tuple-element.20.own_ref), channel_id=1, source_target_pairs={{0,1},{1,0},{2,3},{3,2},{4,5},{5,4},{6,7},{7,6},{8,9},{9,8},{10,11... | collective-permute-start | bytes 3145736 | tf_op jit(solution)/shard_map/ppermute | solution.py:38
  69.2 1.6 copy-start.3
  70.8 24.8 %copy-start.10 = (s32[32]{0:T(128)S(1)}, s32[32]{0:T(128)}, u32[]{:S(2)}) copy-start(s32[32]{0:T(128)} %param.13) | copy-start | bytes 388
  75.2 1.9 copy-start.1
  77.1 0.8 copy-start.5
  88.5 24.3 %all-to-all-start.2 = ((bf16[16,16,1024]{2,1,0:T(8,128)(2,1)}), bf16[16,16,1024]{2,1,0:T(8,128)(2,1)}, u32[]{:S(2)}, u32[]{:S(2)}) async-start(bf16[16,16,1024]{2,1,0:T(8,128)(2,1)} %copy-done.5), calls=%async_computation.2 | async-start | bytes 1048576 | tf_op jit(solution)/shard_map/all_to_all | solution.py:34
  112.8 53.9 %copy-start.2 = (f32[128,8192]{1,0:T(8,128)S(1)}, f32[128,8192]{1,0:T(8,128)}, u32[]{:S(2)}) copy-start(f32[128,8192]{1,0:T(8,128)} %copy-done.1) | copy-start | bytes 12582916
  116.0 3.3 %collective-permute-start.1 = (f32[136,256]{1,0:T(8,128)S(1)}, f32[136,256]{1,0:T(8,128)S(1)}, u32[]{:S(2)}, u32[]{:S(2)}) collective-permute-start(f32[136,256]{1,0:T(8,128)S(1)} %shard_map.89.own_ref), channel_id=1, source_target_pairs={{0,1},{1,0},{2,3},{3,2},{4,5},{5,4},{6,7},{7,6},{8,9},{9,8},{10,11... | collective-permute-start | bytes 417800 | tf_op jit(solution)/shard_map/ppermute | solution.py:38
  170.9 5.0 %collective-permute-start.2 = (bf16[8,32,16,128]{3,2,1,0:T(8,128)(2,1)S(1)}, bf16[8,32,16,128]{3,2,1,0:T(8,128)(2,1)S(1)}, u32[]{:S(2)}, u32[]{:S(2)}) collective-permute-start(bf16[8,32,16,128]{3,2,1,0:T(8,128)(2,1)S(1)} %get-tuple-element.36), channel_id=1, source_target_pairs={{0,1},{1,0},{2,3},{3,2},{4,5},{5,4},{6,7},{7,6},{8,9},{9,8},{10,11... | collective-permute-start | bytes 3145736 | tf_op jit(solution)/shard_map/ppermute | solution.py:38

commit v6 on v5

--- a/solution.py
+++ b/solution.py
@@ -36,6 +36,16 @@
 
 def swap_cores(value):
     return lax.ppermute(value, "c", [(0, 1), (1, 0)])
+
+
+def swap_neighbours(value, nyl, nyh, outer):
+    pairs = []
+    for yh in range(nyh):
+        first, second = yh, nyh + yh
+        if outer:
+            first, second = nyh + yh, (yh + 1) % nyh
+        pairs += [(first, second), (second, first)]
+    return lax.ppermute(value, ("yl", "yh"), pairs)
 
 
 def call(kernel, outs, args, scratch=(), scalars=0, flops=0):
@@ -60,44 +70,14 @@
     return jax.ShapeDtypeStruct(*pair)
 
 
-def pack(nyh, zh_ref, down_ref, up_ref, passages_ref, out_ref):
-    peers, both, _ = out_ref.shape
-    nzh = peers // nyh
-    part = 2 * down_ref.shape[0] // nzh
-    at = pl.ds(pl.multiple_of(lax.rem(zh_ref[0], nzh // 2) * part, part), part)
-    mine = jnp.where(zh_ref[0] < nzh // 2, down_ref[at, :].astype(f32), up_ref[at, :].astype(f32))
-    passages = passages_ref[...].astype(f32)
-    rows = both - part
-    for yh in range(nyh):
-        block = jnp.concatenate([mine, passages[yh * rows:(yh + 1) * rows]], axis=0).astype(bf16)
-        for zh in range(nzh):
-            out_ref[zh * nyh + yh] = block
-
-
-def unpack(nyh, got_ref, mats_ref, out_ref):
-    peers, both, feats = got_ref.shape
-    nzh = peers // nyh
-    part = mats_ref.shape[1] // nzh
-    for yh in range(nyh):
-        passages = []
-        for zh in range(nzh):
-            block = got_ref[zh * nyh + yh].astype(f32)
-            mats_ref[yh, zh * part:(zh + 1) * part, :] = block[:part].astype(bf16)
-            passages.append(block[part:])
-        passages = jnp.concatenate(passages, axis=0).astype(bf16)
-        for i in range(out_ref.shape[0]):
-            out_ref[i, :, yh * feats:(yh + 1) * feats] = passages
-
-
-def adapter_slices(core_ref, own_ref, other_ref):
-    nyh, _, feats = own_ref.shape
-    for yh in range(nyh):
-        for ref, core in ((own_ref, core_ref[0]), (other_ref, 1 - core_ref[0])):
-            at = (yh * 2 + core) * feats
-            yield ref.at[yh], pl.ds(pl.multiple_of(at, feats), feats)
-
-
-def forward(nyh, nc, core_ref, in_ref, frozen_ref, gain_ref, own_ref, other_ref,
+def adapter_slices(place_ref, own_ref, other_ref):
+    slots, _, feats = own_ref.shape
+    for k in range(slots):
+        for ref, place in ((own_ref, place_ref[k]), (other_ref, place_ref[slots + k])):
+            yield ref.at[k], pl.ds(pl.multiple_of(place * feats, feats), feats)
+
+
+def forward(nyh, nc, place_ref, in_ref, frozen_ref, gain_ref, own_ref, other_ref,
             latent_ref, hidden_ref, inv_ref, unit_ref, length_ref, send_ref, part_ref):
     _, both, feats = own_ref.shape
     slices = nyh * nc
@@ -106,7 +86,7 @@
     queries = tokens // LEN
     acc = jnp.zeros((tokens, rank), f32)
     acc_t = jnp.zeros((rank, tokens), f32)
-    for mats_ref, at in adapter_slices(core_ref, own_ref, other_ref):
+    for mats_ref, at in adapter_slices(place_ref, own_ref, other_ref):
         part = in_ref[:, at]
         down = mats_ref[:rank]
         acc += dot_rows(part, down)
@@ -114,7 +94,7 @@
     latent = acc.astype(bf16)
     latent_ref[...] = acc_t.astype(bf16)
     squares = jnp.zeros((tokens, 1), f32)
-    for mats_ref, at in adapter_slices(core_ref, own_ref, other_ref):
+    for mats_ref, at in adapter_slices(place_ref, own_ref, other_ref):
         hidden = frozen_ref[:, at].astype(f32) + adapter_scale_factor * dot(
             latent, mats_ref[rank:]
         )
@@ -223,7 +203,7 @@
     out_ref[...] = total_ref[...].astype(bf16).reshape(out_ref.shape)
 
 
-def backward(nyh, nc, core_ref, got_ref, unit_ref, length_ref, inv_ref, hidden_ref, gain_ref,
+def backward(nyh, nc, place_ref, got_ref, unit_ref, length_ref, inv_ref, hidden_ref, gain_ref,
              in_ref, own_ref, other_ref, latent_ref, keep_ref, send_ref,
              grad_ref, scaled_ref, up_ref, hg_ref):
     _, both, feats = own_ref.shape
@@ -257,7 +237,7 @@
     factor = inv * inv * inv * (jnp.concatenate(mean, axis=0) / width)
     latent_t = latent_ref[...]
     acc = jnp.zeros((rank, tokens), f32)
-    for mats_ref, at in adapter_slices(core_ref, own_ref, other_ref):
+    for mats_ref, at in adapter_slices(place_ref, own_ref, other_ref):
         for q in range(queries):
             of = slice(q * LEN, (q + 1) * LEN)
             hg_ref[of] = (
@@ -267,7 +247,7 @@
         acc += dot_rows(mats_ref[rank:], hidden_grad)
         up_ref[:, at] = adapter_scale_factor * dot(latent_t, hidden_grad)
     latent_grad = (adapter_scale_factor * acc).astype(bf16)
-    first = core_ref[0] == 0
+    first = place_ref[2 * own_ref.shape[0]] == 0
     for f in range(slices):
         down = dot(latent_grad, in_ref[:, f * feats:(f + 1) * feats])
         for x in range(nx):
@@ -340,25 +320,25 @@
     members = nzh * nyl * nx
     shape = jax.ShapeDtypeStruct
     gain = gain.reshape(1, width)
-    core = ic.astype(jnp.int32).reshape(1)
-
-    part = 2 * rank // nzh
-    (sent,) = call(
-        functools.partial(pack, nyh),
-        [shape((nzh * nyh, part + rows, feats), bf16)],
-        [izh.astype(jnp.int32).reshape(1), adapter_a.T, adapter_up_matrix, passages],
-        scalars=1,
-    )
-    own_mats, sent = call(
-        functools.partial(unpack, nyh),
-        [
-            shape((nyh, 2 * rank, feats), bf16),
-            shape((nyl * nx, nzh * rows, half), bf16),
-        ],
-        [exchange(sent, ("zh", "yh"))],
-    )
+
+    sent = jnp.broadcast_to(passages.reshape(1, nyh, rows, feats), (nzh, nyh, rows, feats))
+    got = exchange(sent.reshape(nzh * nyh, rows, feats), ("zh", "yh"))
+
+    mine = jnp.concatenate([adapter_a.T, adapter_up_matrix], axis=0)
+    slots = [mine]
+    for outer in (True, False, True)[: nyh - 1]:
+        slots.append(swap_neighbours(slots[-1], nyl, nyh, outer))
+        if len(slots) == 2:
+            got, slots[1] = lax.optimization_barrier((got, slots[1]))
+    own_mats = jnp.stack(slots)
     other_mats = swap_cores(own_mats)
-    block = exchange(sent, ("yl", "x")).reshape(members * rows, half)
+    side = 1 - 2 * (1 - iyl)
+    places = jnp.stack([iyh, iyh + side, iyh - side, iyh + 2][:nyh]).astype(jnp.int32) % nyh * nc
+    place = jnp.concatenate([places + ic, places + 1 - ic, ic.reshape(1)]).astype(jnp.int32)
+
+    got = got.reshape(nzh, nyh, rows, feats).transpose(0, 2, 1, 3).reshape(nzh * rows, half)
+    got = jnp.broadcast_to(got[None], (nyl * nx, nzh * rows, half))
+    block = exchange(got, ("yl", "x")).reshape(members * rows, half)
     columns = block.shape[0]
 
     latent_t, hidden, inv, unit, length, sent = call(
@@ -371,7 +351,7 @@
             shape((queries, 128), f32),
             shape((ring, nyh * queries, feats), bf16),
         ],
-        [core, adapter_in, frozen, gain, own_mats, other_mats],
+        [place, adapter_in, frozen, gain, own_mats, other_mats],
         scratch=[((nc, nyh * queries, feats), f32)],
         scalars=1,
         flops=6 * tokens * rank * width,
@@ -422,7 +402,7 @@
     keep, send = call(
         functools.partial(backward, nyh, nc),
         [shape((nyl * nx, blocks, 2 * out_rows, cols), bf16)] * 2,
-        [core, got, unit, length, inv, hidden, gain, adapter_in, own_mats, other_mats, latent_t],
+        [place, got, unit, length, inv, hidden, gain, adapter_in, own_mats, other_mats, latent_t],
         scratch=[
             ((nc, nyh * queries, feats), f32),
             ((queries, width), f32),

time: 220 us -> 227 us (1.032)
  blocking collectives: 132 us -> 91 us
  waiting for transfers between devices: 33.6 us -> 60 us
  starting transfers between devices: 25.3 us -> 45.6 us
  other arithmetic: 0.11 us -> 2.38 us
    all_to_all x6 -> x5, blocking collectives: 132 us -> 91 us  [exchange(): return lax.all_to_all(blocks, axes, 0, 0, tiled=True)]
    ppermute x0 -> x3, waiting for transfers between devices: none -> 40.9 us  [swap_neighbours(): return lax.ppermute(value, ('yl', 'yh'), pairs)]
    all_to_all x2 -> x3, waiting for transfers between devices: 27.3 us -> 13.4 us  [exchange(): return lax.all_to_all(blocks, axes, 0, 0, tiled=True)]
    ppermute x0 -> x3, starting transfers between devices: none -> 11.6 us  [swap_neighbours(): return lax.ppermute(value, ('yl', 'yh'), pairs)]
    all_to_all x2 -> x3, starting transfers between devices: 18.6 us -> 26.3 us  [exchange(): return lax.all_to_all(blocks, axes, 0, 0, tiled=True)]
    unnamed x22 -> x16, local copies, waits for them, and re-layouts: 8.34 us -> 4.34 us
    broadcast_in_dim x0 -> x2, local copies, waits for them, and re-layouts: none -> 3.2 us  [the longest x1 1.63 us: shards(): got = jnp.broadcast_to(got[None], (nyl * nx, nzh * rows, half))]
    pallas_call x10 -> x8, Pallas kernels: 15.2 us -> 14.9 us  [call(): pl.pallas_call(kernel, out_shape=outs, in_specs=[pl.BlockSpec(memory_spac...]
  transfers between devices with their start and end apart: 5 -> 9, of which waited for: 5 -> 7; matrix products, arithmetic and copies ran while one was open for 0% -> 1% of each run, Pallas kernels for 2% -> 2%
where the time goes in v6:
time: 227 us; the launch traced here: 226 us
  blocking collectives  91 us (40%)
  waiting for transfers between devices  60 us (26%)
  starting transfers between devices  45.6 us (20%)
  Pallas kernels  14.9 us (7%)
  local copies, waits for them, and re-layouts  9.27 us (4%)
  between operations  2.59 us (1%)
  other arithmetic  2.38 us (1%)
    all_to_all x5, blocking collectives, exchange(): return lax.all_to_all(blocks, axes, 0, 0, tiled=True)  91 us
    ppermute x3, waiting for transfers between devices, swap_neighbours(): return lax.ppermute(value, ('yl', 'yh'), pairs)  40.9 us
    all_to_all x3, starting transfers between devices, exchange(): return lax.all_to_all(blocks, axes, 0, 0, tiled=True)  26.3 us
    pallas_call x8, Pallas kernels, call(): pl.pallas_call(kernel, out_shape=outs, in_specs=[pl.BlockSpec(memory_spac...  14.9 us
    all_to_all x3, waiting for transfers between devices, exchange(): return lax.all_to_all(blocks, axes, 0, 0, tiled=True)  13.4 us
    ppermute x3, starting transfers between devices, swap_neighbours(): return lax.ppermute(value, ('yl', 'yh'), pairs)  11.6 us
    ppermute x3, starting transfers between devices, swap_cores(): return lax.ppermute(value, 'c', [(0, 1), (1, 0)])  7.67 us
    ppermute x3, waiting for transfers between devices, swap_cores(): return lax.ppermute(value, 'c', [(0, 1), (1, 0)])  5.72 us
  transfers between devices with their start and end apart: 9, of which 7 were waited for; matrix products, arithmetic and copies ran while one was open for 1% of the time, Pallas kernels for 2%

profile of v6, /device:TPU:8, one launch (start us, length us, event | category | flops | bytes accessed | tf_op | source)
XLA Modules:
  0.0 225.8 jit_solution(15807771750789192705)
XLA Ops:
  2.2 14.8 %all-to-all-start = ((bf16[16,8,1024]{2,1,0:T(8,128)(2,1)}), bf16[16,8,1024]{2,1,0:T(8,128)(2,1)S(1)}, u32[]{:S(2)}, u32[]{:S(2)}) async-start(bf16[16,8,1024]{2,1,0:T(8,128)(2,1)} %bitcast.9), calls=%async_computation | async-start | bytes 524288 | tf_op jit(solution)/shard_map/all_to_all | solution.py:34
  18.0 4.6 %collective-permute-start = (bf16[128,1024]{1,0:T(8,128)(2,1)S(1)}, bf16[128,1024]{1,0:T(8,128)(2,1)S(1)}, u32[]{:S(2)}, u32[]{:S(2)}) collective-permute-start(bf16[128,1024]{1,0:T(8,128)(2,1)S(1)} %get-tuple-element.41), channel_id=1, source_target_pairs={{32,2},{2,32},{34,4},{4,34},{36,6},{6,36},{38,0},{0,38},{33,3},{3,... | collective-permute-start | bytes 786440 | tf_op jit(solution)/shard_map/ppermute | solution.py:48
  22.6 8.6 %collective-permute-done = bf16[128,1024]{1,0:T(8,128)(2,1)S(1)} collective-permute-done((bf16[128,1024]{1,0:T(8,128)(2,1)S(1)}, bf16[128,1024]{1,0:T(8,128)(2,1)S(1)}, u32[]{:S(2)}, u32[]{:S(2)}) %collective-permute-start) | collective-permute-done | bytes 262176 | tf_op jit(solution)/shard_map/ppermute | solution.py:48
  32.9 6.3 %all-to-all-start.1 = ((bf16[8,32,4096]{2,1,0:T(8,128)(2,1)}), bf16[8,32,4096]{2,1,0:T(8,128)(2,1)}, u32[]{:S(2)}, u32[]{:S(2)}) async-start(bf16[8,32,4096]{2,1,0:T(8,128)(2,1)} %broadcast_in_dim.53), calls=%async_computation.1 | async-start | bytes 4194304 | tf_op jit(solution)/shard_map/all_to_all | solution.py:34
  39.2 2.1 collective-permute-start.1
  41.3 27.0 %collective-permute-done.1 = bf16[128,1024]{1,0:T(8,128)(2,1)S(1)} collective-permute-done((bf16[128,1024]{1,0:T(8,128)(2,1)S(1)}, bf16[128,1024]{1,0:T(8,128)(2,1)S(1)}, u32[]{:S(2)}, u32[]{:S(2)}) %collective-permute-start.1) | collective-permute-done | bytes 262176 | tf_op jit(solution)/shard_map/ppermute | solution.py:48
  68.4 4.9 %collective-permute-start.2 = (bf16[128,1024]{1,0:T(8,128)(2,1)S(1)}, bf16[128,1024]{1,0:T(8,128)(2,1)S(1)}, u32[]{:S(2)}, u32[]{:S(2)}) collective-permute-start(bf16[128,1024]{1,0:T(8,128)(2,1)S(1)} %collective-permute-done.1), channel_id=1, source_target_pairs={{32,2},{2,32},{34,4},{4,34},{36,6},{6,36},{38,0},{0,38},{33,3},{3,... | collective-permute-start | bytes 786440 | tf_op jit(solution)/shard_map/ppermute | solution.py:48
  73.3 5.2 %collective-permute-done.2 = bf16[128,1024]{1,0:T(8,128)(2,1)S(1)} collective-permute-done((bf16[128,1024]{1,0:T(8,128)(2,1)S(1)}, bf16[128,1024]{1,0:T(8,128)(2,1)S(1)}, u32[]{:S(2)}, u32[]{:S(2)}) %collective-permute-start.2) | collective-permute-done | bytes 262176 | tf_op jit(solution)/shard_map/ppermute | solution.py:48
  81.7 2.6 %collective-permute-done.3.other_ref = bf16[4,128,1024]{2,1,0:T(8,128)(2,1)} collective-permute-done((bf16[4,128,1024]{2,1,0:T(8,128)(2,1)S(1)}, bf16[4,128,1024]{2,1,0:T(8,128)(2,1)}, u32[]{:S(2)}, u32[]{:S(2)}) %collective-permute-start.3) | collective-permute-done | bytes 1048608 | tf_op jit(solution)/shard_map/ppermute | solution.py:38
  85.8 4.4 %shard_map.86 = (bf16[64,128]{1,0:T(8,128)(2,1)S(1)}, f32[128,8192]{1,0:T(8,128)S(1)}, f32[128,128]{1,0:T(8,128)S(1)}, f32[4,8192]{1,0:T(4,128)S(1)}, f32[4,128]...) custom-call(s32[9]{0:T(128)S(1)} %pad_add_fusion.place_ref, bf16[128,8192]{1,0:T(8,128)(2,1)S(1)} %copy-done, ...), custom_call_target="tpu_custom_call" | custom-call | flops 402653184 | bytes 11257856 | tf_op jit(solution)/shard_map/pallas_call | solution.py:55
  90.2 1.9 copy-done.1
  92.9 5.3 %all-to-all-start.2 = ((bf16[16,16,1024]{2,1,0:T(8,128)(2,1)}), bf16[16,16,1024]{2,1,0:T(8,128)(2,1)}, u32[]{:S(2)}, u32[]{:S(2)}) async-start(bf16[16,16,1024]{2,1,0:T(8,128)(2,1)} %copy-done.4), calls=%async_computation.2 | async-start | bytes 1048576 | tf_op jit(solution)/shard_map/all_to_all | solution.py:34
  98.9 13.4 %all-to-all-done.2.query_ref = bf16[16,16,1024]{2,1,0:T(8,128)(2,1)} async-done(((bf16[16,16,1024]{2,1,0:T(8,128)(2,1)}), bf16[16,16,1024]{2,1,0:T(8,128)(2,1)}, u32[]{:S(2)}, u32[]{:S(2)}) %all-to-all-start.2) | async-done | bytes 524320 | tf_op jit(solution)/shard_map/all_to_all | solution.py:34
  112.3 3.2 %shard_map.87.own_ref = f32[136,256]{1,0:T(8,128)S(1)} custom-call(bf16[16,16,1024]{2,1,0:T(8,128)(2,1)} %all-to-all-done.2.query_ref, bf16[256,4096]{1,0:T(8,128)(2,1)} %bitcast.16.block_ref), custom_call_target="tpu_custom_call" | custom-call | flops 1073741824 | bytes 2760704 | tf_op jit(solution)/shard_map/pallas_call | solution.py:55
  115.5 3.0 %collective-permute-start.4 = (f32[136,256]{1,0:T(8,128)S(1)}, f32[136,256]{1,0:T(8,128)S(1)}, u32[]{:S(2)}, u32[]{:S(2)}) collective-permute-start(f32[136,256]{1,0:T(8,128)S(1)} %shard_map.87.own_ref), channel_id=1, source_target_pairs={{0,1},{1,0},{2,3},{3,2},{4,5},{5,4},{6,7},{7,6},{8,9},{9,8},{10,11... | collective-permute-start | bytes 417800 | tf_op jit(solution)/shard_map/ppermute | solution.py:38
  119.7 14.6 %all_to_all.40.rows_ref = f32[8,1,128]{2,1,0:T(1,128)S(1)} all-to-all(f32[8,1,128]{2,1,0:T(1,128)S(1)} %get-tuple-element.27), channel_id=1, replica_groups=mesh['zh'=4,'zl'=2,'yl'=2,'x'=4,'yh'=4,'c'=2] {'zl','yh'}, dimensions={0} | all-to-all | bytes 8192 | tf_op jit(solution)/shard_map/all_to_all | solution.py:34
  134.4 19.9 %all_to_all.41.cols_ref = f32[32,1,256]{2,1,0:T(1,128)S(1)} all-to-all(f32[32,1,256]{2,1,0:T(1,128)S(1)} %get-tuple-element.28), channel_id=1, replica_groups=mesh['zh'=4,'zl'=2,'yl'=2,'x'=4,'yh'=4,'c'=2] {'zh','yl','x'}, dimensions={0} | all-to-all | bytes 65536 | tf_op jit(solution)/shard_map/all_to_all | solution.py:34
  154.3 2.4 %shard_map.89 = (bf16[16,16,1024]{2,1,0:T(8,128)(2,1)S(1)}, f32[8,128]{1,0:T(8,128)S(1)}) custom-call(f32[128,256]{1,0:T(8,128)S(1)} %get-tuple-element.25.expo_ref, f32[8,256]{1,0:T(8,128)S(1)} %get-tuple-element.26.aux_ref, f32[128,256]{1,0:T(8,128)S(1)} %compare_convert_fusion.onehot_ref, f32[8,1,128]{2,1,0:T(1,128)S(1)} %all_to_all.40.rows_ref, ...), custom_call_target="tpu_custom_call" | custom-call | flops 536870912 | bytes 2932736 | tf_op jit(solution)/shard_map/pallas_call | solution.py:55
  156.8 16.8 %all_to_all.42.got_ref = bf16[16,16,1024]{2,1,0:T(8,128)(2,1)S(1)} all-to-all(bf16[16,16,1024]{2,1,0:T(8,128)(2,1)S(1)} %get-tuple-element.29), channel_id=1, replica_groups=mesh['zh'=4,'zl'=2,'yl'=2,'x'=4,'yh'=4,'c'=2] {'zl','yh','c'}, dimensions={0} | all-to-all | bytes 1048576 | tf_op jit(solution)/shard_map/all_to_all | solution.py:34
  173.6 4.2 %shard_map.90 = (bf16[8,32,16,128]{3,2,1,0:T(8,128)(2,1)S(1)}, bf16[8,32,16,128]{3,2,1,0:T(8,128)(2,1)S(1)}) custom-call(s32[9]{0:T(128)S(1)} %pad_add_fusion.place_ref, bf16[16,16,1024]{2,1,0:T(8,128)(2,1)S(1)} %all_to_all.42.got_ref, f32[4,8192]{1,0:T(4,128)S(1)} %get-tuple-element.30.unit_ref, f32[4,128]{1,0:T(4,128)S(1)} %get-tuple-element.31.length_ref, ...), custom_call_target="tpu_custom_call" | custom-call | flops 402653184 | bytes 11257856 | tf_op jit(solution)/shard_map/pallas_call | solution.py:55
  177.8 2.7 %collective-permute-start.5 = (bf16[8,32,16,128]{3,2,1,0:T(8,128)(2,1)S(1)}, bf16[8,32,16,128]{3,2,1,0:T(8,128)(2,1)S(1)}, u32[]{:S(2)}, u32[]{:S(2)}) collective-permute-start(bf16[8,32,16,128]{3,2,1,0:T(8,128)(2,1)S(1)} %get-tuple-element.36), channel_id=1, source_target_pairs={{0,1},{1,0},{2,3},{3,2},{4,5},{5,4},{6,7},{7,6},{8,9},{9,8},{10,11... | collective-permute-start | bytes 3145736 | tf_op jit(solution)/shard_map/ppermute | solution.py:38
  180.6 2.3 %collective-permute-done.5.got_ref = bf16[8,32,16,128]{3,2,1,0:T(8,128)(2,1)S(1)} collective-permute-done((bf16[8,32,16,128]{3,2,1,0:T(8,128)(2,1)S(1)}, bf16[8,32,16,128]{3,2,1,0:T(8,128)(2,1)S(1)}, u32[]{:S(2)}, u32[]{:S(2)}) %collective-permute-start.5) | collective-permute-done | bytes 1048608 | tf_op jit(solution)/shard_map/ppermute | solution.py:38
  183.1 21.6 %all_to_all.43.got_ref = bf16[8,33,16,128]{3,2,1,0:T(8,128)(2,1)S(1)} all-to-all(bf16[8,33,16,128]{3,2,1,0:T(8,128)(2,1)S(1)} %shard_map.91), channel_id=1, replica_groups=mesh['zh'=4,'zl'=2,'yl'=2,'x'=4,'yh'=4,'c'=2] {'yl','x'}, dimensions={0} | all-to-all | bytes 2162688 | tf_op jit(solution)/shard_map/all_to_all | solution.py:34
  204.9 18.0 %all_to_all.44.got_ref = bf16[32,32,128]{2,1,0:T(8,128)(2,1)S(1)} all-to-all(bf16[32,32,128]{2,1,0:T(8,128)(2,1)S(1)} %shard_map.92), channel_id=1, replica_groups=mesh['zh'=4,'zl'=2,'yl'=2,'x'=4,'yh'=4,'c'=2] {'zh','zl','yh'}, dimensions={0} | all-to-all | bytes 524288 | tf_op jit(solution)/shard_map/all_to_all | solution.py:34
  (45 shorter events, 13.2 us)
Async XLA Ops:
  2.2 29.1 %all-to-all-start = ((bf16[16,8,1024]{2,1,0:T(8,128)(2,1)}), bf16[16,8,1024]{2,1,0:T(8,128)(2,1)S(1)}, u32[]{:S(2)}, u32[]{:S(2)}) async-start(bf16[16,8,1024]{2,1,0:T(8,128)(2,1)} %bitcast.9), calls=%async_computation | async-start | bytes 524288 | tf_op jit(solution)/shard_map/all_to_all | solution.py:34
  18.0 13.2 %collective-permute-start = (bf16[128,1024]{1,0:T(8,128)(2,1)S(1)}, bf16[128,1024]{1,0:T(8,128)(2,1)S(1)}, u32[]{:S(2)}, u32[]{:S(2)}) collective-permute-start(bf16[128,1024]{1,0:T(8,128)(2,1)S(1)} %get-tuple-element.41), channel_id=1, source_target_pairs={{32,2},{2,32},{34,4},{4,34},{36,6},{6,36},{38,0},{0,38},{33,3},{3,... | collective-permute-start | bytes 786440 | tf_op jit(solution)/shard_map/ppermute | solution.py:48
  31.3 7.9 %copy-start.6 = (bf16[128,1024]{1,0:T(8,128)(2,1)}, bf16[128,1024]{1,0:T(8,128)(2,1)S(1)}, u32[]{:S(2)}) copy-start(bf16[128,1024]{1,0:T(8,128)(2,1)S(1)} %collective-permute-done) | copy-start | bytes 786436
  32.9 60.1 %all-to-all-start.1 = ((bf16[8,32,4096]{2,1,0:T(8,128)(2,1)}), bf16[8,32,4096]{2,1,0:T(8,128)(2,1)}, u32[]{:S(2)}, u32[]{:S(2)}) async-start(bf16[8,32,4096]{2,1,0:T(8,128)(2,1)} %broadcast_in_dim.53), calls=%async_computation.1 | async-start | bytes 4194304 | tf_op jit(solution)/shard_map/all_to_all | solution.py:34
  39.2 45.1 %copy-start = (bf16[128,8192]{1,0:T(8,128)(2,1)S(1)}, bf16[128,8192]{1,0:T(8,128)(2,1)}, u32[]{:S(2)}) copy-start(bf16[128,8192]{1,0:T(8,128)(2,1)} %in_ref.3) | copy-start | bytes 6291460
  39.2 45.1 %copy-start.5 = (f32[8192]{0:T(1024)S(1)}, f32[8192]{0:T(1024)}, u32[]{:S(2)}) copy-start(f32[8192]{0:T(1024)} %param.9) | copy-start | bytes 98308
  39.2 29.2 %collective-permute-start.1 = (bf16[128,1024]{1,0:T(8,128)(2,1)S(1)}, bf16[128,1024]{1,0:T(8,128)(2,1)S(1)}, u32[]{:S(2)}, u32[]{:S(2)}) collective-permute-start(bf16[128,1024]{1,0:T(8,128)(2,1)S(1)} %collective-permute-done), channel_id=1, source_target_pairs={{0,32},{32,0},{2,34},{34,2},{4,36},{36,4},{6,38},{38,6},{1,33},{33... | collective-permute-start | bytes 786440 | tf_op jit(solution)/shard_map/ppermute | solution.py:48
  68.4 10.1 %collective-permute-start.2 = (bf16[128,1024]{1,0:T(8,128)(2,1)S(1)}, bf16[128,1024]{1,0:T(8,128)(2,1)S(1)}, u32[]{:S(2)}, u32[]{:S(2)}) collective-permute-start(bf16[128,1024]{1,0:T(8,128)(2,1)S(1)} %collective-permute-done.1), channel_id=1, source_target_pairs={{32,2},{2,32},{34,4},{4,34},{36,6},{6,36},{38,0},{0,38},{33,3},{3,... | collective-permute-start | bytes 786440 | tf_op jit(solution)/shard_map/ppermute | solution.py:48
  79.5 4.7 %collective-permute-start.3 = (bf16[4,128,1024]{2,1,0:T(8,128)(2,1)S(1)}, bf16[4,128,1024]{2,1,0:T(8,128)(2,1)}, u32[]{:S(2)}, u32[]{:S(2)}) collective-permute-start(bf16[4,128,1024]{2,1,0:T(8,128)(2,1)S(1)} %pad_maximum_fusion.own_ref), channel_id=1, source_target_pairs={{0,1},{1,0},{2,3},{3,2},{4,5},{5,4},{6,7},{7,6},{8,9},{9,8},{10,11... | collective-permute-start | bytes 3145736 | tf_op jit(solution)/shard_map/ppermute | solution.py:38
  84.2 1.6 copy-start.3
  85.8 12.6 %copy-start.7 = (s32[32]{0:T(128)S(1)}, s32[32]{0:T(128)}, u32[]{:S(2)}) copy-start(s32[32]{0:T(128)} %param.13) | copy-start | bytes 388
  90.2 1.9 copy-start.1
  92.1 0.8 copy-start.4
  92.9 19.4 %all-to-all-start.2 = ((bf16[16,16,1024]{2,1,0:T(8,128)(2,1)}), bf16[16,16,1024]{2,1,0:T(8,128)(2,1)}, u32[]{:S(2)}, u32[]{:S(2)}) async-start(bf16[16,16,1024]{2,1,0:T(8,128)(2,1)} %copy-done.4), calls=%async_computation.2 | async-start | bytes 1048576 | tf_op jit(solution)/shard_map/all_to_all | solution.py:34
  112.3 61.3 %copy-start.2 = (f32[128,8192]{1,0:T(8,128)S(1)}, f32[128,8192]{1,0:T(8,128)}, u32[]{:S(2)}) copy-start(f32[128,8192]{1,0:T(8,128)} %copy-done.1) | copy-start | bytes 12582916
  115.5 4.0 %collective-permute-start.4 = (f32[136,256]{1,0:T(8,128)S(1)}, f32[136,256]{1,0:T(8,128)S(1)}, u32[]{:S(2)}, u32[]{:S(2)}) collective-permute-start(f32[136,256]{1,0:T(8,128)S(1)} %shard_map.87.own_ref), channel_id=1, source_target_pairs={{0,1},{1,0},{2,3},{3,2},{4,5},{5,4},{6,7},{7,6},{8,9},{9,8},{10,11... | collective-permute-start | bytes 417800 | tf_op jit(solution)/shard_map/ppermute | solution.py:38
  177.8 5.0 %collective-permute-start.5 = (bf16[8,32,16,128]{3,2,1,0:T(8,128)(2,1)S(1)}, bf16[8,32,16,128]{3,2,1,0:T(8,128)(2,1)S(1)}, u32[]{:S(2)}, u32[]{:S(2)}) collective-permute-start(bf16[8,32,16,128]{3,2,1,0:T(8,128)(2,1)S(1)} %get-tuple-element.36), channel_id=1, source_target_pairs={{0,1},{1,0},{2,3},{3,2},{4,5},{5,4},{6,7},{7,6},{8,9},{9,8},{10,11... | collective-permute-start | bytes 3145736 | tf_op jit(solution)/shard_map/ppermute | solution.py:38

commit v7 on v6

--- a/solution.py
+++ b/solution.py
@@ -17,7 +17,7 @@
 
 AXES = ("zh", "zl", "yl", "x", "yh", "c")
 SIZES = (4, 2, 2, 4, 4, 2)
-ROW, COLUMN, RING = ("zl", "yh"), ("zh", "yl", "x"), ("zl", "yh", "c")
+ROW, COLUMN, RING = ("yl", "yh"), ("zh", "zl", "x"), ("yl", "yh", "c")
 MIB = 1 << 20
 f32, bf16 = jnp.float32, jnp.bfloat16
 
@@ -45,6 +45,14 @@
         if outer:
             first, second = nyh + yh, (yh + 1) % nyh
         pairs += [(first, second), (second, first)]
+    return lax.ppermute(value, ("yl", "yh"), pairs)
+
+
+def from_opposite(value, nyl, nyh):
+    pairs = []
+    for yh in range(nyh):
+        for yl in range(nyl):
+            pairs.append(((1 - yl) * nyh + (yh + 2) % nyh, yl * nyh + yh))
     return lax.ppermute(value, ("yl", "yh"), pairs)
 
 
@@ -315,9 +323,9 @@
     queries = tokens // LEN
     group = passages.shape[0]
     rows = group // nyh
-    ny = nzl * nyh
+    ny = nyl * nyh
     ring = ny * nc
-    members = nzh * nyl * nx
+    members = nzh * nzl * nx
     shape = jax.ShapeDtypeStruct
     gain = gain.reshape(1, width)
 
@@ -326,10 +334,11 @@
 
     mine = jnp.concatenate([adapter_a.T, adapter_up_matrix], axis=0)
     slots = [mine]
-    for outer in (True, False, True)[: nyh - 1]:
-        slots.append(swap_neighbours(slots[-1], nyl, nyh, outer))
-        if len(slots) == 2:
-            got, slots[1] = lax.optimization_barrier((got, slots[1]))
+    slots.append(swap_neighbours(mine, nyl, nyh, True))
+    got, slots[1] = lax.optimization_barrier((got, slots[1]))
+    if nyh == 4:
+        slots.append(swap_neighbours(slots[1], nyl, nyh, False))
+        slots.append(from_opposite(mine, nyl, nyh))
     own_mats = jnp.stack(slots)
     other_mats = swap_cores(own_mats)
     side = 1 - 2 * (1 - iyl)
@@ -337,8 +346,8 @@
     place = jnp.concatenate([places + ic, places + 1 - ic, ic.reshape(1)]).astype(jnp.int32)
 
     got = got.reshape(nzh, nyh, rows, feats).transpose(0, 2, 1, 3).reshape(nzh * rows, half)
-    got = jnp.broadcast_to(got[None], (nyl * nx, nzh * rows, half))
-    block = exchange(got, ("yl", "x")).reshape(members * rows, half)
+    got = jnp.broadcast_to(got[None], (nzl * nx, nzh * rows, half))
+    block = exchange(got, ("zl", "x")).reshape(members * rows, half)
     columns = block.shape[0]
 
     latent_t, hidden, inv, unit, length, sent = call(
@@ -361,10 +370,13 @@
 
     count = ring * 8
     at = lax.iota(jnp.int32, columns)
-    at_xy, at_zh, at_row = at // (nzh * rows), at // rows % nzh, at % rows
-    passage_id = ((at_zh * nzl + izl) * nyl * nx + at_xy) * group + iyh * rows + at_row
+    at_zl, at_x, at_zh, at_row = (
+        at // (nx * nzh * rows), at // (nzh * rows) % nx, at // rows % nzh, at % rows
+    )
+    passage_id = ((at_zh * nzl + at_zl) * nyl + iyl) * nx + at_x
+    passage_id = passage_id * group + iyh * rows + at_row
     own_pos = jnp.where(
-        lax.iota(jnp.int32, nzl)[:, None] == izl, positive[None, :], -1
+        lax.iota(jnp.int32, nyl)[:, None] == iyl, positive[None, :], -1
     ).reshape(ring, 1, queries)
     own_pos = jnp.broadcast_to(own_pos, (ring, 8 // queries, queries)).reshape(count)
     onehot = (own_pos[:, None] == passage_id[None, :]).astype(f32)
@@ -398,7 +410,7 @@
 
     out_rows = rank // (nyh * nc)
     cols = width // (nzh * nzl * nyl * nx)
-    blocks = nzh * ny
+    blocks = nzh * nzl * nyh
     keep, send = call(
         functools.partial(backward, nyh, nc),
         [shape((nyl * nx, blocks, 2 * out_rows, cols), bf16)] * 2,
@@ -426,7 +438,7 @@
         [exchange(line, ("zh", "zl", "yh"))],
     )
     adapter_grads = last[: 2 * out_rows].reshape(2, out_rows, cols)
-    total_pairs = group * nzl * members
+    total_pairs = group * nyl * members
     loss = last[2 * out_rows, 0] / (2.0 * total_pairs) + inv_temp
     return (adapter_grads, loss)
 

time: 227 us -> 202 us (0.89)
  the two profiles are of different devices: /device:TPU:8 before, /device:TPU:16 now
where the time goes in v7:
time: 202 us; the launch traced here: 201 us
  blocking collectives  86.3 us (43%)
  waiting for transfers between devices  43.2 us (21%)
  starting transfers between devices  42.8 us (21%)
  Pallas kernels  14.9 us (7%)
  local copies, waits for them, and re-layouts  9.27 us (5%)
  between operations  2.58 us (1%)
  other arithmetic  2.38 us (1%)
    all_to_all x5, blocking collectives, exchange(): return lax.all_to_all(blocks, axes, 0, 0, tiled=True)  86.3 us
    all_to_all x3, starting transfers between devices, exchange(): return lax.all_to_all(blocks, axes, 0, 0, tiled=True)  27.5 us
    all_to_all x3, waiting for transfers between devices, exchange(): return lax.all_to_all(blocks, axes, 0, 0, tiled=True)  18.2 us
    pallas_call x8, Pallas kernels, call(): pl.pallas_call(kernel, out_shape=outs, in_specs=[pl.BlockSpec(memory_spac...  14.9 us
    ppermute x1, waiting for transfers between devices, from_opposite(): return lax.ppermute(value, ('yl', 'yh'), pairs)  10.4 us
    ppermute x2, waiting for transfers between devices, swap_neighbours(): return lax.ppermute(value, ('yl', 'yh'), pairs)  8.33 us
    ppermute x3, waiting for transfers between devices, swap_cores(): return lax.ppermute(value, 'c', [(0, 1), (1, 0)])  6.23 us
    ppermute x3, starting transfers between devices, swap_cores(): return lax.ppermute(value, 'c', [(0, 1), (1, 0)])  5.97 us
  transfers between devices with their start and end apart: 9, of which 7 were waited for; matrix products, arithmetic and copies ran while one was open for 1% of the time, Pallas kernels for 2%

profile of v7, /device:TPU:16, one launch (start us, length us, event | category | flops | bytes accessed | tf_op | source)
XLA Modules:
  0.0 201.3 jit_solution(17477342085002219770)
XLA Ops:
  2.2 15.9 %all-to-all-start = ((bf16[16,8,1024]{2,1,0:T(8,128)(2,1)}), bf16[16,8,1024]{2,1,0:T(8,128)(2,1)S(1)}, u32[]{:S(2)}, u32[]{:S(2)}) async-start(bf16[16,8,1024]{2,1,0:T(8,128)(2,1)} %bitcast.9), calls=%async_computation | async-start | bytes 524288 | tf_op jit(solution)/shard_map/all_to_all | solution.py:34
  21.1 8.3 %collective-permute-done = bf16[128,1024]{1,0:T(8,128)(2,1)S(1)} collective-permute-done((bf16[128,1024]{1,0:T(8,128)(2,1)S(1)}, bf16[128,1024]{1,0:T(8,128)(2,1)S(1)}, u32[]{:S(2)}, u32[]{:S(2)}) %collective-permute-start) | collective-permute-done | bytes 262176 | tf_op jit(solution)/shard_map/ppermute | solution.py:48
  29.4 2.8 %all-to-all-done = bf16[16,8,1024]{2,1,0:T(8,128)(2,1)S(1)} async-done(((bf16[16,8,1024]{2,1,0:T(8,128)(2,1)}), bf16[16,8,1024]{2,1,0:T(8,128)(2,1)S(1)}, u32[]{:S(2)}, u32[]{:S(2)}) %all-to-all-start) | async-done | bytes 262176 | tf_op jit(solution)/shard_map/all_to_all | solution.py:34
  33.9 5.0 %all-to-all-start.1 = ((bf16[8,32,4096]{2,1,0:T(8,128)(2,1)}), bf16[8,32,4096]{2,1,0:T(8,128)(2,1)}, u32[]{:S(2)}, u32[]{:S(2)}) async-start(bf16[8,32,4096]{2,1,0:T(8,128)(2,1)} %broadcast_in_dim.53), calls=%async_computation.1 | async-start | bytes 4194304 | tf_op jit(solution)/shard_map/all_to_all | solution.py:34
  38.9 4.3 %collective-permute-start.2 = (bf16[128,1024]{1,0:T(8,128)(2,1)S(1)}, bf16[128,1024]{1,0:T(8,128)(2,1)S(1)}, u32[]{:S(2)}, u32[]{:S(2)}) collective-permute-start(bf16[128,1024]{1,0:T(8,128)(2,1)S(1)} %get-tuple-element.41), channel_id=1, source_target_pairs={{36,0},{4,32},{38,2},{6,34},{32,4},{0,36},{34,6},{2,38},{37,1},{5,... | collective-permute-start | bytes 786440 | tf_op jit(solution)/shard_map/ppermute | solution.py:56
  43.3 3.0 %collective-permute-start.1 = (bf16[128,1024]{1,0:T(8,128)(2,1)S(1)}, bf16[128,1024]{1,0:T(8,128)(2,1)S(1)}, u32[]{:S(2)}, u32[]{:S(2)}) collective-permute-start(bf16[128,1024]{1,0:T(8,128)(2,1)S(1)} %collective-permute-done), channel_id=1, source_target_pairs={{0,32},{32,0},{2,34},{34,2},{4,36},{36,4},{6,38},{38,6},{1,33},{33... | collective-permute-start | bytes 786440 | tf_op jit(solution)/shard_map/ppermute | solution.py:48
  46.3 10.4 %collective-permute-done.2 = bf16[128,1024]{1,0:T(8,128)(2,1)S(1)} collective-permute-done((bf16[128,1024]{1,0:T(8,128)(2,1)S(1)}, bf16[128,1024]{1,0:T(8,128)(2,1)S(1)}, u32[]{:S(2)}, u32[]{:S(2)}) %collective-permute-start.2) | collective-permute-done | bytes 262176 | tf_op jit(solution)/shard_map/ppermute | solution.py:56
  57.8 1.9 collective-permute-start.3
  59.9 2.6 %collective-permute-done.3.other_ref = bf16[4,128,1024]{2,1,0:T(8,128)(2,1)} collective-permute-done((bf16[4,128,1024]{2,1,0:T(8,128)(2,1)S(1)}, bf16[4,128,1024]{2,1,0:T(8,128)(2,1)}, u32[]{:S(2)}, u32[]{:S(2)}) %collective-permute-start.3) | collective-permute-done | bytes 1048608 | tf_op jit(solution)/shard_map/ppermute | solution.py:38
  64.1 4.4 %shard_map.86 = (bf16[64,128]{1,0:T(8,128)(2,1)S(1)}, f32[128,8192]{1,0:T(8,128)S(1)}, f32[128,128]{1,0:T(8,128)S(1)}, f32[4,8192]{1,0:T(4,128)S(1)}, f32[4,128]...) custom-call(s32[9]{0:T(128)S(1)} %pad_add_fusion.place_ref, bf16[128,8192]{1,0:T(8,128)(2,1)S(1)} %copy-done, ...), custom_call_target="tpu_custom_call" | custom-call | flops 402653184 | bytes 11257856 | tf_op jit(solution)/shard_map/pallas_call | solution.py:63
  68.5 1.9 copy-done.1
  71.2 6.6 %all-to-all-start.2 = ((bf16[16,16,1024]{2,1,0:T(8,128)(2,1)}), bf16[16,16,1024]{2,1,0:T(8,128)(2,1)}, u32[]{:S(2)}, u32[]{:S(2)}) async-start(bf16[16,16,1024]{2,1,0:T(8,128)(2,1)} %copy-done.4), calls=%async_computation.2 | async-start | bytes 1048576 | tf_op jit(solution)/shard_map/all_to_all | solution.py:34
  78.4 15.3 %all-to-all-done.2.query_ref = bf16[16,16,1024]{2,1,0:T(8,128)(2,1)} async-done(((bf16[16,16,1024]{2,1,0:T(8,128)(2,1)}), bf16[16,16,1024]{2,1,0:T(8,128)(2,1)}, u32[]{:S(2)}, u32[]{:S(2)}) %all-to-all-start.2) | async-done | bytes 524320 | tf_op jit(solution)/shard_map/all_to_all | solution.py:34
  93.8 3.2 %shard_map.87.own_ref = f32[136,256]{1,0:T(8,128)S(1)} custom-call(bf16[16,16,1024]{2,1,0:T(8,128)(2,1)} %all-to-all-done.2.query_ref, bf16[256,4096]{1,0:T(8,128)(2,1)} %bitcast.16.block_ref), custom_call_target="tpu_custom_call" | custom-call | flops 1073741824 | bytes 2760704 | tf_op jit(solution)/shard_map/pallas_call | solution.py:63
  97.0 2.0 %collective-permute-start.4 = (f32[136,256]{1,0:T(8,128)S(1)}, f32[136,256]{1,0:T(8,128)S(1)}, u32[]{:S(2)}, u32[]{:S(2)}) collective-permute-start(f32[136,256]{1,0:T(8,128)S(1)} %shard_map.87.own_ref), channel_id=1, source_target_pairs={{0,1},{1,0},{2,3},{3,2},{4,5},{5,4},{6,7},{7,6},{8,9},{9,8},{10,11... | collective-permute-start | bytes 417800 | tf_op jit(solution)/shard_map/ppermute | solution.py:38
  100.5 9.4 %all_to_all.40.rows_ref = f32[8,1,128]{2,1,0:T(1,128)S(1)} all-to-all(f32[8,1,128]{2,1,0:T(1,128)S(1)} %get-tuple-element.27), channel_id=1, replica_groups=mesh['zh'=4,'zl'=2,'yl'=2,'x'=4,'yh'=4,'c'=2] {'yl','yh'}, dimensions={0} | all-to-all | bytes 8192 | tf_op jit(solution)/shard_map/all_to_all | solution.py:34
  109.9 18.9 %all_to_all.41.cols_ref = f32[32,1,256]{2,1,0:T(1,128)S(1)} all-to-all(f32[32,1,256]{2,1,0:T(1,128)S(1)} %get-tuple-element.28), channel_id=1, replica_groups=mesh['zh'=4,'zl'=2,'yl'=2,'x'=4,'yh'=4,'c'=2] {'zh','zl','x'}, dimensions={0} | all-to-all | bytes 65536 | tf_op jit(solution)/shard_map/all_to_all | solution.py:34
  128.8 2.4 %shard_map.89 = (bf16[16,16,1024]{2,1,0:T(8,128)(2,1)S(1)}, f32[8,128]{1,0:T(8,128)S(1)}) custom-call(f32[128,256]{1,0:T(8,128)S(1)} %get-tuple-element.25.expo_ref, f32[8,256]{1,0:T(8,128)S(1)} %get-tuple-element.26.aux_ref, f32[128,256]{1,0:T(8,128)S(1)} %compare_convert_fusion.onehot_ref, f32[8,1,128]{2,1,0:T(1,128)S(1)} %all_to_all.40.rows_ref, ...), custom_call_target="tpu_custom_call" | custom-call | flops 536870912 | bytes 2932736 | tf_op jit(solution)/shard_map/pallas_call | solution.py:63
  131.2 20.7 %all_to_all.42.got_ref = bf16[16,16,1024]{2,1,0:T(8,128)(2,1)S(1)} all-to-all(bf16[16,16,1024]{2,1,0:T(8,128)(2,1)S(1)} %get-tuple-element.29), channel_id=1, replica_groups=mesh['zh'=4,'zl'=2,'yl'=2,'x'=4,'yh'=4,'c'=2] {'yl','yh','c'}, dimensions={0} | all-to-all | bytes 1048576 | tf_op jit(solution)/shard_map/all_to_all | solution.py:34
  151.9 4.2 %shard_map.90 = (bf16[8,32,16,128]{3,2,1,0:T(8,128)(2,1)S(1)}, bf16[8,32,16,128]{3,2,1,0:T(8,128)(2,1)S(1)}) custom-call(s32[9]{0:T(128)S(1)} %pad_add_fusion.place_ref, bf16[16,16,1024]{2,1,0:T(8,128)(2,1)S(1)} %all_to_all.42.got_ref, f32[4,8192]{1,0:T(4,128)S(1)} %get-tuple-element.30.unit_ref, f32[4,128]{1,0:T(4,128)S(1)} %get-tuple-element.31.length_ref, ...), custom_call_target="tpu_custom_call" | custom-call | flops 402653184 | bytes 11257856 | tf_op jit(solution)/shard_map/pallas_call | solution.py:63
  156.1 2.0 %collective-permute-start.5 = (bf16[8,32,16,128]{3,2,1,0:T(8,128)(2,1)S(1)}, bf16[8,32,16,128]{3,2,1,0:T(8,128)(2,1)S(1)}, u32[]{:S(2)}, u32[]{:S(2)}) collective-permute-start(bf16[8,32,16,128]{3,2,1,0:T(8,128)(2,1)S(1)} %get-tuple-element.36), channel_id=1, source_target_pairs={{0,1},{1,0},{2,3},{3,2},{4,5},{5,4},{6,7},{7,6},{8,9},{9,8},{10,11... | collective-permute-start | bytes 3145736 | tf_op jit(solution)/shard_map/ppermute | solution.py:38
  158.2 2.5 %collective-permute-done.5.got_ref = bf16[8,32,16,128]{3,2,1,0:T(8,128)(2,1)S(1)} collective-permute-done((bf16[8,32,16,128]{3,2,1,0:T(8,128)(2,1)S(1)}, bf16[8,32,16,128]{3,2,1,0:T(8,128)(2,1)S(1)}, u32[]{:S(2)}, u32[]{:S(2)}) %collective-permute-start.5) | collective-permute-done | bytes 1048608 | tf_op jit(solution)/shard_map/ppermute | solution.py:38
  160.9 19.2 %all_to_all.43.got_ref = bf16[8,33,16,128]{3,2,1,0:T(8,128)(2,1)S(1)} all-to-all(bf16[8,33,16,128]{3,2,1,0:T(8,128)(2,1)S(1)} %shard_map.91), channel_id=1, replica_groups=mesh['zh'=4,'zl'=2,'yl'=2,'x'=4,'yh'=4,'c'=2] {'yl','x'}, dimensions={0} | all-to-all | bytes 2162688 | tf_op jit(solution)/shard_map/all_to_all | solution.py:34
  180.3 18.0 %all_to_all.44.got_ref = bf16[32,32,128]{2,1,0:T(8,128)(2,1)S(1)} all-to-all(bf16[32,32,128]{2,1,0:T(8,128)(2,1)S(1)} %shard_map.92), channel_id=1, replica_groups=mesh['zh'=4,'zl'=2,'yl'=2,'x'=4,'yh'=4,'c'=2] {'zh','zl','yh'}, dimensions={0} | all-to-all | bytes 524288 | tf_op jit(solution)/shard_map/all_to_all | solution.py:34
  (45 shorter events, 13.5 us)
Async XLA Ops:
  2.2 30.0 %all-to-all-start = ((bf16[16,8,1024]{2,1,0:T(8,128)(2,1)}), bf16[16,8,1024]{2,1,0:T(8,128)(2,1)S(1)}, u32[]{:S(2)}, u32[]{:S(2)}) async-start(bf16[16,8,1024]{2,1,0:T(8,128)(2,1)} %bitcast.9), calls=%async_computation | async-start | bytes 524288 | tf_op jit(solution)/shard_map/all_to_all | solution.py:34
  19.1 10.3 %collective-permute-start = (bf16[128,1024]{1,0:T(8,128)(2,1)S(1)}, bf16[128,1024]{1,0:T(8,128)(2,1)S(1)}, u32[]{:S(2)}, u32[]{:S(2)}) collective-permute-start(bf16[128,1024]{1,0:T(8,128)(2,1)S(1)} %get-tuple-element.41), channel_id=1, source_target_pairs={{32,2},{2,32},{34,4},{4,34},{36,6},{6,36},{38,0},{0,38},{33,3},{3,... | collective-permute-start | bytes 786440 | tf_op jit(solution)/shard_map/ppermute | solution.py:48
  29.4 13.9 %copy-start.6 = (bf16[128,1024]{1,0:T(8,128)(2,1)}, bf16[128,1024]{1,0:T(8,128)(2,1)S(1)}, u32[]{:S(2)}) copy-start(bf16[128,1024]{1,0:T(8,128)(2,1)S(1)} %collective-permute-done) | copy-start | bytes 786436
  33.9 37.3 %all-to-all-start.1 = ((bf16[8,32,4096]{2,1,0:T(8,128)(2,1)}), bf16[8,32,4096]{2,1,0:T(8,128)(2,1)}, u32[]{:S(2)}, u32[]{:S(2)}) async-start(bf16[8,32,4096]{2,1,0:T(8,128)(2,1)} %broadcast_in_dim.53), calls=%async_computation.1 | async-start | bytes 4194304 | tf_op jit(solution)/shard_map/all_to_all | solution.py:34
  38.9 23.6 %copy-start = (bf16[128,8192]{1,0:T(8,128)(2,1)S(1)}, bf16[128,8192]{1,0:T(8,128)(2,1)}, u32[]{:S(2)}) copy-start(bf16[128,8192]{1,0:T(8,128)(2,1)} %in_ref.3) | copy-start | bytes 6291460
  38.9 23.6 %copy-start.5 = (f32[8192]{0:T(1024)S(1)}, f32[8192]{0:T(1024)}, u32[]{:S(2)}) copy-start(f32[8192]{0:T(1024)} %param.9) | copy-start | bytes 98308
  38.9 17.8 %collective-permute-start.2 = (bf16[128,1024]{1,0:T(8,128)(2,1)S(1)}, bf16[128,1024]{1,0:T(8,128)(2,1)S(1)}, u32[]{:S(2)}, u32[]{:S(2)}) collective-permute-start(bf16[128,1024]{1,0:T(8,128)(2,1)S(1)} %get-tuple-element.41), channel_id=1, source_target_pairs={{36,0},{4,32},{38,2},{6,34},{32,4},{0,36},{34,6},{2,38},{37,1},{5,... | collective-permute-start | bytes 786440 | tf_op jit(solution)/shard_map/ppermute | solution.py:56
  43.3 13.5 %collective-permute-start.1 = (bf16[128,1024]{1,0:T(8,128)(2,1)S(1)}, bf16[128,1024]{1,0:T(8,128)(2,1)S(1)}, u32[]{:S(2)}, u32[]{:S(2)}) collective-permute-start(bf16[128,1024]{1,0:T(8,128)(2,1)S(1)} %collective-permute-done), channel_id=1, source_target_pairs={{0,32},{32,0},{2,34},{34,2},{4,36},{36,4},{6,38},{38,6},{1,33},{33... | collective-permute-start | bytes 786440 | tf_op jit(solution)/shard_map/ppermute | solution.py:48
  57.8 4.7 %collective-permute-start.3 = (bf16[4,128,1024]{2,1,0:T(8,128)(2,1)S(1)}, bf16[4,128,1024]{2,1,0:T(8,128)(2,1)}, u32[]{:S(2)}, u32[]{:S(2)}) collective-permute-start(bf16[4,128,1024]{2,1,0:T(8,128)(2,1)S(1)} %pad_maximum_fusion.own_ref), channel_id=1, source_target_pairs={{0,1},{1,0},{2,3},{3,2},{4,5},{5,4},{6,7},{7,6},{8,9},{9,8},{10,11... | collective-permute-start | bytes 3145736 | tf_op jit(solution)/shard_map/ppermute | solution.py:38
  62.5 1.6 copy-start.3
  64.1 13.8 %copy-start.7 = (s32[32]{0:T(128)S(1)}, s32[32]{0:T(128)}, u32[]{:S(2)}) copy-start(s32[32]{0:T(128)} %param.13) | copy-start | bytes 388
  68.5 1.9 copy-start.1
  70.4 0.8 copy-start.4
  71.2 22.6 %all-to-all-start.2 = ((bf16[16,16,1024]{2,1,0:T(8,128)(2,1)}), bf16[16,16,1024]{2,1,0:T(8,128)(2,1)}, u32[]{:S(2)}, u32[]{:S(2)}) async-start(bf16[16,16,1024]{2,1,0:T(8,128)(2,1)} %copy-done.4), calls=%async_computation.2 | async-start | bytes 1048576 | tf_op jit(solution)/shard_map/all_to_all | solution.py:34
  93.8 58.2 %copy-start.2 = (f32[128,8192]{1,0:T(8,128)S(1)}, f32[128,8192]{1,0:T(8,128)}, u32[]{:S(2)}) copy-start(f32[128,8192]{1,0:T(8,128)} %copy-done.1) | copy-start | bytes 12582916
  97.0 3.3 %collective-permute-start.4 = (f32[136,256]{1,0:T(8,128)S(1)}, f32[136,256]{1,0:T(8,128)S(1)}, u32[]{:S(2)}, u32[]{:S(2)}) collective-permute-start(f32[136,256]{1,0:T(8,128)S(1)} %shard_map.87.own_ref), channel_id=1, source_target_pairs={{0,1},{1,0},{2,3},{3,2},{4,5},{5,4},{6,7},{7,6},{8,9},{9,8},{10,11... | collective-permute-start | bytes 417800 | tf_op jit(solution)/shard_map/ppermute | solution.py:38
  156.1 4.6 %collective-permute-start.5 = (bf16[8,32,16,128]{3,2,1,0:T(8,128)(2,1)S(1)}, bf16[8,32,16,128]{3,2,1,0:T(8,128)(2,1)S(1)}, u32[]{:S(2)}, u32[]{:S(2)}) collective-permute-start(bf16[8,32,16,128]{3,2,1,0:T(8,128)(2,1)S(1)} %get-tuple-element.36), channel_id=1, source_target_pairs={{0,1},{1,0},{2,3},{3,2},{4,5},{5,4},{6,7},{7,6},{8,9},{9,8},{10,11... | collective-permute-start | bytes 3145736 | tf_op jit(solution)/shard_map/ppermute | solution.py:38

commit v8 on v7

--- a/solution.py
+++ b/solution.py
@@ -56,26 +56,30 @@
     return lax.ppermute(value, ("yl", "yh"), pairs)
 
 
-def call(kernel, outs, args, scratch=(), scalars=0, flops=0):
-    size = sum(a.size * a.dtype.itemsize for a in list(args[scalars:]) + list(outs))
+VMEM = pl.BlockSpec(memory_space=pltpu.VMEM)
+SMEM = pl.BlockSpec(memory_space=pltpu.SMEM)
+HBM = pl.BlockSpec(memory_space=pltpu.HBM)
+
+
+def call(kernel, outs, args, spaces=None, out_spaces=None, scratch=(), copies=0, flops=0):
+    spaces = spaces or [VMEM] * len(args)
+    out_spaces = out_spaces or [VMEM] * len(outs)
+    size = sum(a.size * a.dtype.itemsize for a in list(args) + list(outs))
     spare = [pltpu.VMEM(shape, kind) for shape, kind in scratch]
-    spare_size = sum(a.size * a.dtype.itemsize for a in map(shape_of, scratch))
+    spare_size = sum(
+        a.size * a.dtype.itemsize for a in (jax.ShapeDtypeStruct(*pair) for pair in scratch)
+    )
+    if copies:
+        spare.append(pltpu.SemaphoreType.DMA((copies,)))
     return pl.pallas_call(
         kernel,
         out_shape=outs,
-        in_specs=[pl.BlockSpec(memory_space=pltpu.SMEM)] * scalars
-        + [pl.BlockSpec(memory_space=pltpu.VMEM)] * (len(args) - scalars),
-        out_specs=[pl.BlockSpec(memory_space=pltpu.VMEM)] * len(outs),
+        in_specs=spaces,
+        out_specs=out_spaces,
         scratch_shapes=spare,
-        compiler_params=pltpu.CompilerParams(
-            vmem_limit_bytes=spare_size + 8 * MIB
-        ),
+        compiler_params=pltpu.CompilerParams(vmem_limit_bytes=spare_size + 8 * MIB),
         cost_estimate=pl.CostEstimate(flops=flops, bytes_accessed=size, transcendentals=0),
     )(*args)
-
-
-def shape_of(pair):
-    return jax.ShapeDtypeStruct(*pair)
 
 
 def adapter_slices(place_ref, own_ref, other_ref):
@@ -85,13 +89,9 @@
             yield ref.at[k], pl.ds(pl.multiple_of(place * feats, feats), feats)
 
 
-def forward(nyh, nc, place_ref, in_ref, frozen_ref, gain_ref, own_ref, other_ref,
-            latent_ref, hidden_ref, inv_ref, unit_ref, length_ref, send_ref, part_ref):
-    _, both, feats = own_ref.shape
-    slices = nyh * nc
-    rank = both // 2
-    tokens, width = in_ref.shape
-    queries = tokens // LEN
+def project(place_ref, in_ref, own_ref, other_ref, latent_ref, latent_t_ref):
+    rank = own_ref.shape[1] // 2
+    tokens = in_ref.shape[0]
     acc = jnp.zeros((tokens, rank), f32)
     acc_t = jnp.zeros((rank, tokens), f32)
     for mats_ref, at in adapter_slices(place_ref, own_ref, other_ref):
@@ -99,21 +99,33 @@
         down = mats_ref[:rank]
         acc += dot_rows(part, down)
         acc_t += dot_rows(down, part)
-    latent = acc.astype(bf16)
-    latent_ref[...] = acc_t.astype(bf16)
+    latent_ref[...] = acc.astype(bf16)
+    latent_t_ref[...] = acc_t.astype(bf16)
+
+
+def hidden_slice(frozen_ref, latent, mats_ref, at):
+    up = mats_ref[mats_ref.shape[0] // 2:]
+    return frozen_ref[:, at].astype(f32) + adapter_scale_factor * dot(latent, up)
+
+
+def forward(nyh, nc, place_ref, latent_ref, frozen_ref, gain_ref, own_ref, other_ref,
+            inv_ref, unit_ref, length_ref, send_ref, hidden, part_ref):
+    feats = own_ref.shape[2]
+    slices = nyh * nc
+    tokens, width = frozen_ref.shape
+    queries = tokens // LEN
+    latent = latent_ref[...]
     squares = jnp.zeros((tokens, 1), f32)
     for mats_ref, at in adapter_slices(place_ref, own_ref, other_ref):
-        hidden = frozen_ref[:, at].astype(f32) + adapter_scale_factor * dot(
-            latent, mats_ref[rank:]
-        )
-        hidden_ref[:, at] = hidden
-        squares += jnp.sum(hidden * hidden, axis=1, keepdims=True)
+        value = hidden_slice(frozen_ref, latent, mats_ref, at)
+        hidden[:, at] = value
+        squares += jnp.sum(value * value, axis=1, keepdims=True)
     inv = lax.rsqrt(squares / width + norm_eps)
     inv_ref[...] = jnp.broadcast_to(inv, inv_ref.shape)
     total = jnp.zeros((queries, 1), f32)
     for f in range(slices):
         at = slice(f * feats, (f + 1) * feats)
-        scaled = hidden_ref[:, at] * inv
+        scaled = hidden[:, at] * inv
         for q in range(queries):
             one = jnp.sum(scaled[q * LEN:(q + 1) * LEN], axis=0, keepdims=True)
             unit_ref[q:q + 1, at] = one * gain_ref[:, at] / LEN
@@ -136,16 +148,31 @@
     return lax.broadcasted_iota(jnp.int32, shape, 0)
 
 
-def score(nyh, query_ref, block_ref, out_ref):
+def start_slices(block_ref, parts, sems):
+    feats = parts.shape[2]
+    copies = [
+        pltpu.make_async_copy(
+            block_ref.at[:, k * feats:(k + 1) * feats], parts.at[k], sems.at[k]
+        )
+        for k in range(parts.shape[0])
+    ]
+    for copy in copies:
+        copy.start()
+    return copies
+
+
+def score(nyh, query_ref, block_ref, out_ref, parts, sems):
     ring, rows, feats = query_ref.shape
     queries = rows // nyh
     columns = block_ref.shape[0]
+    copies = start_slices(block_ref, parts, sems)
     query = query_ref[...].reshape(ring * rows, feats)
     mine = row_index((ring * rows, columns)) // queries % nyh
     total = jnp.zeros((ring * rows, columns), f32)
     gram = jnp.zeros((columns, columns), f32)
     for k in range(nyh):
-        part = block_ref[:, k * feats:(k + 1) * feats]
+        copies[k].wait()
+        part = parts[k]
         total = jnp.where(mine == k, dot_rows(query, part), total)
         gram += dot_rows(part, part)
     total = total.reshape(ring, rows // 8, 8, columns)
@@ -165,7 +192,7 @@
     return jnp.transpose(jnp.broadcast_to(row, (n, n)))
 
 
-def exponentials(own_ref, other_ref, onehot_ref, expo_ref, aux_ref, rows_ref, cols_ref):
+def exponentials(own_ref, other_ref, onehot_ref, expo_ref, aux_ref, sums_ref):
     count, columns = expo_ref.shape
     inv_norm = 1.0 / jnp.sqrt(own_ref[count:count + 1] + other_ref[count:count + 1])
     scores = inv_temp * ((own_ref[:count] + other_ref[:count]) * inv_norm)
@@ -175,21 +202,32 @@
     aux_ref[0:1] = inv_norm
     aux_ref[1:2] = jnp.full((1, columns), hits)
     row = across(jnp.sum(expo, axis=1, keepdims=True))[0:1]
-    for y in range(rows_ref.shape[0]):
-        rows_ref[y] = row
     col = 0.5 * jnp.sum(expo, axis=0, keepdims=True)
+    sums = jnp.concatenate([row, col], axis=1)
+    for i in range(sums_ref.shape[0]):
+        sums_ref[i] = sums
+
+
+def combine(ny, place_ref, got_ref, row_ref, cols_ref):
+    count = row_ref.shape[1]
+    last = place_ref.shape[0] - 1
+    first = place_ref[last - 1] * ny
+    row = functools.reduce(jnp.add, [got_ref[first + y] for y in range(ny)])
+    row_ref[...] = row[:, :count]
+    peers = range(got_ref.shape[0] // ny)
+    col = functools.reduce(jnp.add, [got_ref[zl * ny + place_ref[last]] for zl in peers])
     for i in range(cols_ref.shape[0]):
-        cols_ref[i] = col
-
-
-def weigh(nyh, expo_ref, aux_ref, onehot_ref, rows_ref, cols_ref, block_ref,
-          out_ref, loss_ref, total_ref):
+        cols_ref[i] = col[:, count:]
+
+
+def weigh(nyh, ny, members, expo_ref, aux_ref, onehot_ref, row_ref, cols_ref, block_ref,
+          out_ref, loss_ref, total_ref, parts, sems):
     count, columns = expo_ref.shape
     ring, rows, feats = out_ref.shape
     queries = rows // nyh
-    ny, members = rows_ref.shape[0], cols_ref.shape[0]
-    row = functools.reduce(jnp.add, [rows_ref[y] for y in range(ny)])
-    col = functools.reduce(jnp.add, [cols_ref[i] for i in range(members)])
+    copies = start_slices(block_ref, parts, sems)
+    row = row_ref[...]
+    col = functools.reduce(jnp.add, [cols_ref[i] for i in range(cols_ref.shape[0])])
     loss = (
         0.5 * jnp.sum(jnp.log(row), axis=1, keepdims=True) / ny
         + jnp.sum(jnp.log(col), axis=1, keepdims=True) / members
@@ -203,7 +241,8 @@
     weights = weights.reshape(ring * rows, columns).astype(bf16)
     mine = row_index((ring * rows, feats)) // queries % nyh
     for k in range(nyh):
-        part = inv_temp * dot(weights, block_ref[:, k * feats:(k + 1) * feats])
+        copies[k].wait()
+        part = inv_temp * dot(weights, parts[k])
         if k == 0:
             total_ref[...] = part
         else:
@@ -211,9 +250,9 @@
     out_ref[...] = total_ref[...].astype(bf16).reshape(out_ref.shape)
 
 
-def backward(nyh, nc, place_ref, got_ref, unit_ref, length_ref, inv_ref, hidden_ref, gain_ref,
-             in_ref, own_ref, other_ref, latent_ref, keep_ref, send_ref,
-             grad_ref, scaled_ref, up_ref, hg_ref):
+def backward(nyh, nc, place_ref, got_ref, unit_ref, length_ref, inv_ref, frozen_ref, gain_ref,
+             in_ref, own_ref, other_ref, latent_ref, latent_t_ref, keep_ref, send_ref,
+             grad_ref, scaled_ref, up_ref, hg_ref, hidden):
     _, both, feats = own_ref.shape
     slices = nyh * nc
     rank = both // 2
@@ -232,6 +271,9 @@
         grad = grad_ref[f % nc, f // nc * queries:(f // nc + 1) * queries, :]
         inner += jnp.sum(unit_ref[:, at] * grad, axis=1, keepdims=True)
     length = length_ref[:, :1]
+    latent = latent_ref[...]
+    for mats_ref, at in adapter_slices(place_ref, own_ref, other_ref):
+        hidden[:, at] = hidden_slice(frozen_ref, latent, mats_ref, at)
     mean = [jnp.zeros((LEN, 1), f32) for q in range(queries)]
     for f in range(slices):
         at = slice(f * feats, (f + 1) * feats)
@@ -239,17 +281,17 @@
         pooled_grad = (grad - unit_ref[:, at] * inner) / length
         scaled_ref[:, at] = pooled_grad / LEN * gain_ref[:, at]
         for q in range(queries):
-            product = hidden_ref[q * LEN:(q + 1) * LEN, at] * scaled_ref[q:q + 1, at]
+            product = hidden[q * LEN:(q + 1) * LEN, at] * scaled_ref[q:q + 1, at]
             mean[q] += jnp.sum(product, axis=1, keepdims=True)
     inv = inv_ref[:, :1]
     factor = inv * inv * inv * (jnp.concatenate(mean, axis=0) / width)
-    latent_t = latent_ref[...]
+    latent_t = latent_t_ref[...]
     acc = jnp.zeros((rank, tokens), f32)
     for mats_ref, at in adapter_slices(place_ref, own_ref, other_ref):
         for q in range(queries):
             of = slice(q * LEN, (q + 1) * LEN)
             hg_ref[of] = (
-                inv[of] * scaled_ref[q:q + 1, at] - hidden_ref[of, at] * factor[of]
+                inv[of] * scaled_ref[q:q + 1, at] - hidden[of, at] * factor[of]
             ).astype(bf16)
         hidden_grad = hg_ref[...]
         acc += dot_rows(mats_ref[rank:], hidden_grad)
@@ -302,14 +344,14 @@
     out_ref[:, rows:] = jnp.broadcast_to(split_rows(loss, rows, cols)[None], (blocks, rows, cols))
 
 
-def add_last(got_ref, out_ref):
+def add_last(total_pairs, got_ref, out_ref, loss_ref):
     total = got_ref[0].astype(f32)
     for i in range(1, got_ref.shape[0]):
         total += got_ref[i].astype(f32)
-    rows = out_ref.shape[0] - 8
-    out_ref[:rows] = total[:rows]
-    loss = jnp.sum(total[rows:], axis=0, keepdims=True)
-    out_ref[rows:] = jnp.broadcast_to(loss, (8, out_ref.shape[1]))
+    rows = out_ref.shape[1]
+    out_ref[0] = total[:rows]
+    out_ref[1] = total[rows:2 * rows]
+    loss_ref[0, 0] = jnp.sum(total[2 * rows:, :1]) / (2.0 * total_pairs) + inv_temp
 
 
 def shards(sizes, adapter_in, frozen, gain, adapter_a, adapter_up_matrix, passages, positive):
@@ -343,27 +385,33 @@
     other_mats = swap_cores(own_mats)
     side = 1 - 2 * (1 - iyl)
     places = jnp.stack([iyh, iyh + side, iyh - side, iyh + 2][:nyh]).astype(jnp.int32) % nyh * nc
-    place = jnp.concatenate([places + ic, places + 1 - ic, ic.reshape(1)]).astype(jnp.int32)
+    ends = jnp.stack([ic, izl, iyl * nyh + iyh])
+    place = jnp.concatenate([places + ic, places + 1 - ic, ends]).astype(jnp.int32)
 
     got = got.reshape(nzh, nyh, rows, feats).transpose(0, 2, 1, 3).reshape(nzh * rows, half)
     got = jnp.broadcast_to(got[None], (nzl * nx, nzh * rows, half))
     block = exchange(got, ("zl", "x")).reshape(members * rows, half)
     columns = block.shape[0]
 
-    latent_t, hidden, inv, unit, length, sent = call(
+    latent, latent_t = call(
+        project,
+        [shape((tokens, rank), bf16), shape((rank, tokens), bf16)],
+        [place, adapter_in, own_mats, other_mats],
+        spaces=[SMEM, VMEM, VMEM, VMEM],
+        flops=4 * tokens * rank * width,
+    )
+    inv, unit, length, sent = call(
         functools.partial(forward, nyh, nc),
         [
-            shape((rank, tokens), bf16),
-            shape((tokens, width), f32),
             shape((tokens, 128), f32),
             shape((queries, width), f32),
             shape((queries, 128), f32),
             shape((ring, nyh * queries, feats), bf16),
         ],
-        [place, adapter_in, frozen, gain, own_mats, other_mats],
-        scratch=[((nc, nyh * queries, feats), f32)],
-        scalars=1,
-        flops=6 * tokens * rank * width,
+        [place, latent, frozen, gain, own_mats, other_mats],
+        spaces=[SMEM] + [VMEM] * 5,
+        scratch=[((tokens, width), f32), ((nc, nyh * queries, feats), f32)],
+        flops=2 * tokens * rank * width,
     )
     sent, block = lax.optimization_barrier((sent, block))
     query = exchange(sent, RING)
@@ -384,26 +432,34 @@
         functools.partial(score, nyh),
         [shape((count + 8, columns), f32)],
         [query, block],
+        spaces=[VMEM, HBM],
+        scratch=[((nyh, columns, feats), bf16)],
+        copies=nyh,
         flops=4 * ring * nyh * queries * columns * half,
     )
     other = swap_cores(own)
-    expo, aux, by_row, by_col = call(
+    expo, aux, sent = call(
         exponentials,
         [
             shape((count, columns), f32),
             shape((8, columns), f32),
-            shape((ny, 1, count), f32),
-            shape((members, 1, columns), f32),
+            shape((nzl * ny, 1, count + columns), f32),
         ],
         [own, other, onehot],
     )
-    by_row = exchange(by_row, ROW)
-    by_col = exchange(by_col, COLUMN)
+    row, sent = call(
+        functools.partial(combine, ny),
+        [shape((1, count), f32), shape((nzh * nx, 1, columns), f32)],
+        [place, exchange(sent, ("zl", *ROW))],
+        spaces=[SMEM, VMEM],
+    )
     sent, loss = call(
-        functools.partial(weigh, nyh),
+        functools.partial(weigh, nyh, ny, members),
         [shape((ring, nyh * queries, feats), bf16), shape((8, 128), f32)],
-        [expo, aux, onehot, by_row, by_col, block],
-        scratch=[((ring * nyh * queries, feats), f32)],
+        [expo, aux, onehot, row, exchange(sent, ("zh", "x")), block],
+        spaces=[VMEM] * 5 + [HBM],
+        scratch=[((ring * nyh * queries, feats), f32), ((nyh, columns, feats), bf16)],
+        copies=nyh,
         flops=2 * ring * nyh * queries * columns * half,
     )
     got = exchange(sent, RING)
@@ -414,15 +470,19 @@
     keep, send = call(
         functools.partial(backward, nyh, nc),
         [shape((nyl * nx, blocks, 2 * out_rows, cols), bf16)] * 2,
-        [place, got, unit, length, inv, hidden, gain, adapter_in, own_mats, other_mats, latent_t],
+        [
+            place, got, unit, length, inv, frozen, gain, adapter_in, own_mats, other_mats,
+            latent, latent_t,
+        ],
+        spaces=[SMEM] + [VMEM] * 11,
         scratch=[
             ((nc, nyh * queries, feats), f32),
             ((queries, width), f32),
             ((rank, width), f32),
             ((tokens, feats), bf16),
+            ((tokens, width), f32),
         ],
-        scalars=1,
-        flops=6 * tokens * rank * width,
+        flops=8 * tokens * rank * width,
     )
     (chip,) = call(
         join,
@@ -432,15 +492,13 @@
     (line,) = call(
         add_line, [shape((blocks, 4 * out_rows, cols), bf16)], [exchange(chip, ("yl", "x"))]
     )
-    (last,) = call(
-        add_last,
-        [shape((2 * out_rows + 8, cols), f32)],
+    adapter_grads, loss = call(
+        functools.partial(add_last, group * nyl * members),
+        [shape((2, out_rows, cols), f32), shape((1, 1), f32)],
         [exchange(line, ("zh", "zl", "yh"))],
-    )
-    adapter_grads = last[: 2 * out_rows].reshape(2, out_rows, cols)
-    total_pairs = group * nyl * members
-    loss = last[2 * out_rows, 0] / (2.0 * total_pairs) + inv_temp
-    return (adapter_grads, loss)
+        out_spaces=[VMEM, SMEM],
+    )
+    return (adapter_grads, loss.reshape(()))
 
 
 def build(mesh, sizes):

time: 202 us -> 199 us (0.985)
  local copies, waits for them, and re-layouts: 9.27 us -> 5.43 us
    unnamed x16 -> x12, local copies, waits for them, and re-layouts: 4.34 us -> 1.61 us
    pallas_call x8 -> x10, Pallas kernels: 14.9 us -> 16.5 us  [call(): pl.pallas_call(kernel, out_shape=outs, in_specs=spaces, out_specs=out_spa...]
  transfers between devices with their start and end apart: 9 -> 9, of which waited for: 7 -> 7; matrix products, arithmetic and copies ran while one was open for 1% -> 1% of each run, Pallas kernels for 2% -> 3%
where the time goes in v8:
time: 199 us; the launch traced here: 198 us
  blocking collectives  88.3 us (44%)
  waiting for transfers between devices  43 us (22%)
  starting transfers between devices  42.7 us (21%)
  Pallas kernels  16.5 us (8%)
  local copies, waits for them, and re-layouts  5.43 us (3%)
    all_to_all x5, blocking collectives, exchange(): return lax.all_to_all(blocks, axes, 0, 0, tiled=True)  88.3 us
    all_to_all x3, starting transfers between devices, exchange(): return lax.all_to_all(blocks, axes, 0, 0, tiled=True)  27.5 us
    all_to_all x3, waiting for transfers between devices, exchange(): return lax.all_to_all(blocks, axes, 0, 0, tiled=True)  18.1 us
    pallas_call x10, Pallas kernels, call(): pl.pallas_call(kernel, out_shape=outs, in_specs=spaces, out_specs=out_spa...  16.5 us
    ppermute x1, waiting for transfers between devices, from_opposite(): return lax.ppermute(value, ('yl', 'yh'), pairs)  10.4 us
    ppermute x2, waiting for transfers between devices, swap_neighbours(): return lax.ppermute(value, ('yl', 'yh'), pairs)  8.33 us
    ppermute x3, waiting for transfers between devices, swap_cores(): return lax.ppermute(value, 'c', [(0, 1), (1, 0)])  6.15 us
    ppermute x3, starting transfers between devices, swap_cores(): return lax.ppermute(value, 'c', [(0, 1), (1, 0)])  6.04 us
  transfers between devices with their start and end apart: 9, of which 7 were waited for; matrix products, arithmetic and copies ran while one was open for 1% of the time, Pallas kernels for 3%

profile of v8, /device:TPU:16, one launch (start us, length us, event | category | flops | bytes accessed | tf_op | source)
XLA Modules:
  0.0 198.1 jit_solution(4511178813217260435)
XLA Ops:
  2.2 15.9 %all-to-all-start = ((bf16[16,8,1024]{2,1,0:T(8,128)(2,1)}), bf16[16,8,1024]{2,1,0:T(8,128)(2,1)S(1)}, u32[]{:S(2)}, u32[]{:S(2)}) async-start(bf16[16,8,1024]{2,1,0:T(8,128)(2,1)} %bitcast.10), calls=%async_computation | async-start | bytes 524288 | tf_op jit(solution)/shard_map/all_to_all | solution.py:34
  19.1 1.9 collective-permute-start
  21.1 8.3 %collective-permute-done = bf16[128,1024]{1,0:T(8,128)(2,1)S(1)} collective-permute-done((bf16[128,1024]{1,0:T(8,128)(2,1)S(1)}, bf16[128,1024]{1,0:T(8,128)(2,1)S(1)}, u32[]{:S(2)}, u32[]{:S(2)}) %collective-permute-start) | collective-permute-done | bytes 262176 | tf_op jit(solution)/shard_map/ppermute | solution.py:48
  29.4 2.8 %all-to-all-done = bf16[16,8,1024]{2,1,0:T(8,128)(2,1)S(1)} async-done(((bf16[16,8,1024]{2,1,0:T(8,128)(2,1)}), bf16[16,8,1024]{2,1,0:T(8,128)(2,1)S(1)}, u32[]{:S(2)}, u32[]{:S(2)}) %all-to-all-start) | async-done | bytes 262176 | tf_op jit(solution)/shard_map/all_to_all | solution.py:34
  33.8 5.0 %all-to-all-start.1 = ((bf16[8,32,4096]{2,1,0:T(8,128)(2,1)}), bf16[8,32,4096]{2,1,0:T(8,128)(2,1)}, u32[]{:S(2)}, u32[]{:S(2)}) async-start(bf16[8,32,4096]{2,1,0:T(8,128)(2,1)} %broadcast_in_dim.53), calls=%async_computation.1 | async-start | bytes 4194304 | tf_op jit(solution)/shard_map/all_to_all | solution.py:34
  38.8 4.2 %collective-permute-start.2 = (bf16[128,1024]{1,0:T(8,128)(2,1)S(1)}, bf16[128,1024]{1,0:T(8,128)(2,1)S(1)}, u32[]{:S(2)}, u32[]{:S(2)}) collective-permute-start(bf16[128,1024]{1,0:T(8,128)(2,1)S(1)} %get-tuple-element.47), channel_id=1, source_target_pairs={{36,0},{4,32},{38,2},{6,34},{32,4},{0,36},{34,6},{2,38},{37,1},{5,... | collective-permute-start | bytes 786440 | tf_op jit(solution)/shard_map/ppermute | solution.py:56
  43.0 3.0 %collective-permute-start.1 = (bf16[128,1024]{1,0:T(8,128)(2,1)S(1)}, bf16[128,1024]{1,0:T(8,128)(2,1)S(1)}, u32[]{:S(2)}, u32[]{:S(2)}) collective-permute-start(bf16[128,1024]{1,0:T(8,128)(2,1)S(1)} %collective-permute-done), channel_id=1, source_target_pairs={{0,32},{32,0},{2,34},{34,2},{4,36},{36,4},{6,38},{38,6},{1,33},{33... | collective-permute-start | bytes 786440 | tf_op jit(solution)/shard_map/ppermute | solution.py:48
  46.0 10.4 %collective-permute-done.2 = bf16[128,1024]{1,0:T(8,128)(2,1)S(1)} collective-permute-done((bf16[128,1024]{1,0:T(8,128)(2,1)S(1)}, bf16[128,1024]{1,0:T(8,128)(2,1)S(1)}, u32[]{:S(2)}, u32[]{:S(2)}) %collective-permute-start.2) | collective-permute-done | bytes 262176 | tf_op jit(solution)/shard_map/ppermute | solution.py:56
  56.6 1.9 collective-permute-start.3
  58.7 2.4 %collective-permute-done.3.other_ref = bf16[4,128,1024]{2,1,0:T(8,128)(2,1)S(1)} collective-permute-done((bf16[4,128,1024]{2,1,0:T(8,128)(2,1)S(1)}, bf16[4,128,1024]{2,1,0:T(8,128)(2,1)S(1)}, u32[]{:S(2)}, u32[]{:S(2)}) %collective-permute-start.3) | collective-permute-done | bytes 1048608 | tf_op jit(solution)/shard_map/ppermute | solution.py:38
  64.6 3.2 %shard_map.87 = (f32[128,128]{1,0:T(8,128)S(1)}, f32[4,8192]{1,0:T(4,128)S(1)}, f32[4,128]{1,0:T(4,128)S(1)}, bf16[16,16,1024]{2,1,0:T(8,128)(2,1)}) custom-call(s32[11]{0:T(128)S(1)} %concatenate.6.place_ref, bf16[128,64]{1,0:T(8,128)(2,1)S(1)} %get-tuple-element.24.latent_ref, bf16[128,8192]{1,0:T(8,128)(2,1)S(1)} %copy-done.2, f32[1,8192]{1,0:T(1,128)S(1)} %bitcast.25, ...), custom_call_target="tpu_custom_call" | custom-call | flops 134217728 | bytes 4966444 | tf_op jit(solution)/shard_map/pallas_call | solution.py:74
  67.9 6.6 %all-to-all-start.2 = ((bf16[16,16,1024]{2,1,0:T(8,128)(2,1)}), bf16[16,16,1024]{2,1,0:T(8,128)(2,1)S(1)}, u32[]{:S(2)}, u32[]{:S(2)}) async-start(bf16[16,16,1024]{2,1,0:T(8,128)(2,1)} %get-tuple-element.27), calls=%async_computation.2 | async-start | bytes 1048576 | tf_op jit(solution)/shard_map/all_to_all | solution.py:34
  75.1 15.2 %all-to-all-done.2.query_ref = bf16[16,16,1024]{2,1,0:T(8,128)(2,1)S(1)} async-done(((bf16[16,16,1024]{2,1,0:T(8,128)(2,1)}), bf16[16,16,1024]{2,1,0:T(8,128)(2,1)S(1)}, u32[]{:S(2)}, u32[]{:S(2)}) %all-to-all-start.2) | async-done | bytes 524320 | tf_op jit(solution)/shard_map/all_to_all | solution.py:34
  90.3 3.3 %shard_map.88.own_ref = f32[136,256]{1,0:T(8,128)S(1)} custom-call(bf16[16,16,1024]{2,1,0:T(8,128)(2,1)S(1)} %all-to-all-done.2.query_ref, bf16[256,4096]{1,0:T(8,128)(2,1)} %bitcast.18.block_ref), custom_call_target="tpu_custom_call" | custom-call | flops 1073741824 | bytes 2760704 | tf_op jit(solution)/shard_map/pallas_call | solution.py:74
  93.7 2.1 %collective-permute-start.4 = (f32[136,256]{1,0:T(8,128)S(1)}, f32[136,256]{1,0:T(8,128)S(1)}, u32[]{:S(2)}, u32[]{:S(2)}) collective-permute-start(f32[136,256]{1,0:T(8,128)S(1)} %shard_map.88.own_ref), channel_id=1, source_target_pairs={{0,1},{1,0},{2,3},{3,2},{4,5},{5,4},{6,7},{7,6},{8,9},{9,8},{10,11... | collective-permute-start | bytes 417800 | tf_op jit(solution)/shard_map/ppermute | solution.py:38
  97.3 11.6 %all_to_all.40.got_ref = f32[16,1,384]{2,1,0:T(1,128)S(1)} all-to-all(f32[16,1,384]{2,1,0:T(1,128)S(1)} %get-tuple-element.31), channel_id=1, replica_groups=mesh['zh'=4,'zl'=2,'yl'=2,'x'=4,'yh'=4,'c'=2] {'zl','yl','yh'}, dimensions={0} | all-to-all | bytes 49152 | tf_op jit(solution)/shard_map/all_to_all | solution.py:34
  109.4 18.6 %all_to_all.41.cols_ref = f32[16,1,256]{2,1,0:T(1,128)S(1)} all-to-all(f32[16,1,256]{2,1,0:T(1,128)S(1)} %get-tuple-element.33), channel_id=1, replica_groups=mesh['zh'=4,'zl'=2,'yl'=2,'x'=4,'yh'=4,'c'=2] {'zh','x'}, dimensions={0} | all-to-all | bytes 32768 | tf_op jit(solution)/shard_map/all_to_all | solution.py:34
  128.0 2.3 %shard_map.91 = (bf16[16,16,1024]{2,1,0:T(8,128)(2,1)S(1)}, f32[8,128]{1,0:T(8,128)S(1)}) custom-call(f32[128,256]{1,0:T(8,128)S(1)} %get-tuple-element.29.expo_ref, f32[8,256]{1,0:T(8,128)S(1)} %get-tuple-element.30.aux_ref, f32[128,256]{1,0:T(8,128)S(1)} %compare_convert_fusion.onehot_ref, f32[1,128]{1,0:T(1,128)S(1)} %get-tuple-element.32.row_ref, ...), custom_call_target="tpu_custom_call" | custom-call | flops 536870912 | bytes 2912768 | tf_op jit(solution)/shard_map/pallas_call | solution.py:74
  130.4 20.6 %all_to_all.42.got_ref = bf16[16,16,1024]{2,1,0:T(8,128)(2,1)S(1)} all-to-all(bf16[16,16,1024]{2,1,0:T(8,128)(2,1)S(1)} %get-tuple-element.34), channel_id=1, replica_groups=mesh['zh'=4,'zl'=2,'yl'=2,'x'=4,'yh'=4,'c'=2] {'yl','yh','c'}, dimensions={0} | all-to-all | bytes 1048576 | tf_op jit(solution)/shard_map/all_to_all | solution.py:34
  151.0 4.0 %shard_map.92 = (bf16[8,32,16,128]{3,2,1,0:T(8,128)(2,1)S(1)}, bf16[8,32,16,128]{3,2,1,0:T(8,128)(2,1)S(1)}) custom-call(s32[11]{0:T(128)S(1)} %concatenate.6.place_ref, bf16[16,16,1024]{2,1,0:T(8,128)(2,1)S(1)} %all_to_all.42.got_ref, f32[4,8192]{1,0:T(4,128)S(1)} %get-tuple-element.35.unit_ref, f32[4,128]{1,0:T(4,128)S(1)} %get-tuple-element.36.length_ref, ...), custom_call_target="tpu_custom_call" | custom-call | flops 536870912 | bytes 9177132 | tf_op jit(solution)/shard_map/pallas_call | solution.py:74
  155.0 2.0 %collective-permute-start.5 = (bf16[8,32,16,128]{3,2,1,0:T(8,128)(2,1)S(1)}, bf16[8,32,16,128]{3,2,1,0:T(8,128)(2,1)S(1)}, u32[]{:S(2)}, u32[]{:S(2)}) collective-permute-start(bf16[8,32,16,128]{3,2,1,0:T(8,128)(2,1)S(1)} %get-tuple-element.40), channel_id=1, source_target_pairs={{0,1},{1,0},{2,3},{3,2},{4,5},{5,4},{6,7},{7,6},{8,9},{9,8},{10,11... | collective-permute-start | bytes 3145736 | tf_op jit(solution)/shard_map/ppermute | solution.py:38
  157.0 2.5 %collective-permute-done.5.got_ref = bf16[8,32,16,128]{3,2,1,0:T(8,128)(2,1)S(1)} collective-permute-done((bf16[8,32,16,128]{3,2,1,0:T(8,128)(2,1)S(1)}, bf16[8,32,16,128]{3,2,1,0:T(8,128)(2,1)S(1)}, u32[]{:S(2)}, u32[]{:S(2)}) %collective-permute-start.5) | collective-permute-done | bytes 1048608 | tf_op jit(solution)/shard_map/ppermute | solution.py:38
  159.8 19.2 %all_to_all.43.got_ref = bf16[8,33,16,128]{3,2,1,0:T(8,128)(2,1)S(1)} all-to-all(bf16[8,33,16,128]{3,2,1,0:T(8,128)(2,1)S(1)} %shard_map.93), channel_id=1, replica_groups=mesh['zh'=4,'zl'=2,'yl'=2,'x'=4,'yh'=4,'c'=2] {'yl','x'}, dimensions={0} | all-to-all | bytes 2162688 | tf_op jit(solution)/shard_map/all_to_all | solution.py:34
  179.2 18.3 %all_to_all.44.got_ref = bf16[32,32,128]{2,1,0:T(8,128)(2,1)S(1)} all-to-all(bf16[32,32,128]{2,1,0:T(8,128)(2,1)S(1)} %shard_map.94), channel_id=1, replica_groups=mesh['zh'=4,'zl'=2,'yl'=2,'x'=4,'yh'=4,'c'=2] {'zh','zl','yh'}, dimensions={0} | all-to-all | bytes 524288 | tf_op jit(solution)/shard_map/all_to_all | solution.py:34
  (41 shorter events, 11.6 us)
Async XLA Ops:
  2.2 30.0 %all-to-all-start = ((bf16[16,8,1024]{2,1,0:T(8,128)(2,1)}), bf16[16,8,1024]{2,1,0:T(8,128)(2,1)S(1)}, u32[]{:S(2)}, u32[]{:S(2)}) async-start(bf16[16,8,1024]{2,1,0:T(8,128)(2,1)} %bitcast.10), calls=%async_computation | async-start | bytes 524288 | tf_op jit(solution)/shard_map/all_to_all | solution.py:34
  19.1 10.3 %collective-permute-start = (bf16[128,1024]{1,0:T(8,128)(2,1)S(1)}, bf16[128,1024]{1,0:T(8,128)(2,1)S(1)}, u32[]{:S(2)}, u32[]{:S(2)}) collective-permute-start(bf16[128,1024]{1,0:T(8,128)(2,1)S(1)} %get-tuple-element.47), channel_id=1, source_target_pairs={{32,2},{2,32},{34,4},{4,34},{36,6},{6,36},{38,0},{0,38},{33,3},{3,... | collective-permute-start | bytes 786440 | tf_op jit(solution)/shard_map/ppermute | solution.py:48
  33.8 34.1 %all-to-all-start.1 = ((bf16[8,32,4096]{2,1,0:T(8,128)(2,1)}), bf16[8,32,4096]{2,1,0:T(8,128)(2,1)}, u32[]{:S(2)}, u32[]{:S(2)}) async-start(bf16[8,32,4096]{2,1,0:T(8,128)(2,1)} %broadcast_in_dim.53), calls=%async_computation.1 | async-start | bytes 4194304 | tf_op jit(solution)/shard_map/all_to_all | solution.py:34
  38.8 17.7 %collective-permute-start.2 = (bf16[128,1024]{1,0:T(8,128)(2,1)S(1)}, bf16[128,1024]{1,0:T(8,128)(2,1)S(1)}, u32[]{:S(2)}, u32[]{:S(2)}) collective-permute-start(bf16[128,1024]{1,0:T(8,128)(2,1)S(1)} %get-tuple-element.47), channel_id=1, source_target_pairs={{36,0},{4,32},{38,2},{6,34},{32,4},{0,36},{34,6},{2,38},{37,1},{5,... | collective-permute-start | bytes 786440 | tf_op jit(solution)/shard_map/ppermute | solution.py:56
  43.0 13.5 %collective-permute-start.1 = (bf16[128,1024]{1,0:T(8,128)(2,1)S(1)}, bf16[128,1024]{1,0:T(8,128)(2,1)S(1)}, u32[]{:S(2)}, u32[]{:S(2)}) collective-permute-start(bf16[128,1024]{1,0:T(8,128)(2,1)S(1)} %collective-permute-done), channel_id=1, source_target_pairs={{0,32},{32,0},{2,34},{34,2},{4,36},{36,4},{6,38},{38,6},{1,33},{33... | collective-permute-start | bytes 786440 | tf_op jit(solution)/shard_map/ppermute | solution.py:48
  56.6 4.6 %collective-permute-start.3 = (bf16[4,128,1024]{2,1,0:T(8,128)(2,1)S(1)}, bf16[4,128,1024]{2,1,0:T(8,128)(2,1)S(1)}, u32[]{:S(2)}, u32[]{:S(2)}) collective-permute-start(bf16[4,128,1024]{2,1,0:T(8,128)(2,1)S(1)} %pad_maximum_fusion.own_ref), channel_id=1, source_target_pairs={{0,1},{1,0},{2,3},{3,2},{4,5},{5,4},{6,7},{7,6},{8,9},{9,8},{10,11... | collective-permute-start | bytes 3145736 | tf_op jit(solution)/shard_map/ppermute | solution.py:38
  61.2 1.6 copy-start
  62.8 1.8 copy-start.2
  62.8 1.9 copy-start.4
  64.6 10.0 %copy-start.5 = (s32[32]{0:T(128)S(1)}, s32[32]{0:T(128)}, u32[]{:S(2)}) copy-start(s32[32]{0:T(128)} %param.13) | copy-start | bytes 388
  67.9 22.5 %all-to-all-start.2 = ((bf16[16,16,1024]{2,1,0:T(8,128)(2,1)}), bf16[16,16,1024]{2,1,0:T(8,128)(2,1)S(1)}, u32[]{:S(2)}, u32[]{:S(2)}) async-start(bf16[16,16,1024]{2,1,0:T(8,128)(2,1)} %get-tuple-element.27), calls=%async_computation.2 | async-start | bytes 1048576 | tf_op jit(solution)/shard_map/all_to_all | solution.py:34
  90.3 60.6 %copy-start.3 = (bf16[128,8192]{1,0:T(8,128)(2,1)S(1)}, bf16[128,8192]{1,0:T(8,128)(2,1)}, u32[]{:S(2)}) copy-start(bf16[128,8192]{1,0:T(8,128)(2,1)} %frozen_ref.3) | copy-start | bytes 6291460
  93.7 57.3 %copy-start.1 = (bf16[128,8192]{1,0:T(8,128)(2,1)S(1)}, bf16[128,8192]{1,0:T(8,128)(2,1)}, u32[]{:S(2)}) copy-start(bf16[128,8192]{1,0:T(8,128)(2,1)} %in_ref.3) | copy-start | bytes 6291460
  93.7 3.4 %collective-permute-start.4 = (f32[136,256]{1,0:T(8,128)S(1)}, f32[136,256]{1,0:T(8,128)S(1)}, u32[]{:S(2)}, u32[]{:S(2)}) collective-permute-start(f32[136,256]{1,0:T(8,128)S(1)} %shard_map.88.own_ref), channel_id=1, source_target_pairs={{0,1},{1,0},{2,3},{3,2},{4,5},{5,4},{6,7},{7,6},{8,9},{9,8},{10,11... | collective-permute-start | bytes 417800 | tf_op jit(solution)/shard_map/ppermute | solution.py:38
  155.0 4.6 %collective-permute-start.5 = (bf16[8,32,16,128]{3,2,1,0:T(8,128)(2,1)S(1)}, bf16[8,32,16,128]{3,2,1,0:T(8,128)(2,1)S(1)}, u32[]{:S(2)}, u32[]{:S(2)}) collective-permute-start(bf16[8,32,16,128]{3,2,1,0:T(8,128)(2,1)S(1)} %get-tuple-element.40), channel_id=1, source_target_pairs={{0,1},{1,0},{2,3},{3,2},{4,5},{5,4},{6,7},{7,6},{8,9},{9,8},{10,11... | collective-permute-start | bytes 3145736 | tf_op jit(solution)/shard_map/ppermute | solution.py:38

commit v9 on v8

--- a/solution.py
+++ b/solution.py
@@ -82,25 +82,33 @@
     )(*args)
 
 
-def adapter_slices(place_ref, own_ref, other_ref):
-    slots, _, feats = own_ref.shape
-    for k in range(slots):
-        for ref, place in ((own_ref, place_ref[k]), (other_ref, place_ref[slots + k])):
-            yield ref.at[k], pl.ds(pl.multiple_of(place * feats, feats), feats)
-
-
-def project(place_ref, in_ref, own_ref, other_ref, latent_ref, latent_t_ref):
-    rank = own_ref.shape[1] // 2
+def adapter_slices(place_ref, mats, first=0):
+    slots = (place_ref.shape[0] - 3) // 2
+    for own_ref, other_ref in zip(mats[::2], mats[1::2]):
+        feats = own_ref.shape[2]
+        for k in range(own_ref.shape[0]):
+            for ref, at in ((own_ref, first + k), (other_ref, slots + first + k)):
+                start = pl.multiple_of(place_ref[at] * feats, feats)
+                yield ref.at[k], pl.ds(start, feats)
+        first += own_ref.shape[0]
+
+
+def project(first, place_ref, in_ref, *refs):
+    mats, refs = refs[:2], refs[2:]
+    rank = mats[0].shape[1] // 2
     tokens = in_ref.shape[0]
-    acc = jnp.zeros((tokens, rank), f32)
-    acc_t = jnp.zeros((rank, tokens), f32)
-    for mats_ref, at in adapter_slices(place_ref, own_ref, other_ref):
+    if first == 0:
+        acc, acc_t = jnp.zeros((tokens, rank), f32), jnp.zeros((rank, tokens), f32)
+    else:
+        acc, acc_t = refs[0][...], refs[1][...]
+    for mats_ref, at in adapter_slices(place_ref, mats, first):
         part = in_ref[:, at]
         down = mats_ref[:rank]
         acc += dot_rows(part, down)
         acc_t += dot_rows(down, part)
-    latent_ref[...] = acc.astype(bf16)
-    latent_t_ref[...] = acc_t.astype(bf16)
+    out_ref, out_t_ref = refs[-2:]
+    out_ref[...] = acc.astype(out_ref.dtype)
+    out_t_ref[...] = acc_t.astype(out_t_ref.dtype)
 
 
 def hidden_slice(frozen_ref, latent, mats_ref, at):
@@ -108,15 +116,15 @@
     return frozen_ref[:, at].astype(f32) + adapter_scale_factor * dot(latent, up)
 
 
-def forward(nyh, nc, place_ref, latent_ref, frozen_ref, gain_ref, own_ref, other_ref,
-            inv_ref, unit_ref, length_ref, send_ref, hidden, part_ref):
-    feats = own_ref.shape[2]
+def forward(nyh, nc, place_ref, latent_ref, frozen_ref, gain_ref, *refs):
+    *mats, inv_ref, unit_ref, length_ref, send_ref, hidden, part_ref = refs
+    feats = part_ref.shape[2]
     slices = nyh * nc
     tokens, width = frozen_ref.shape
     queries = tokens // LEN
     latent = latent_ref[...]
     squares = jnp.zeros((tokens, 1), f32)
-    for mats_ref, at in adapter_slices(place_ref, own_ref, other_ref):
+    for mats_ref, at in adapter_slices(place_ref, mats):
         value = hidden_slice(frozen_ref, latent, mats_ref, at)
         hidden[:, at] = value
         squares += jnp.sum(value * value, axis=1, keepdims=True)
@@ -251,9 +259,9 @@
 
 
 def backward(nyh, nc, place_ref, got_ref, unit_ref, length_ref, inv_ref, frozen_ref, gain_ref,
-             in_ref, own_ref, other_ref, latent_ref, latent_t_ref, keep_ref, send_ref,
-             grad_ref, scaled_ref, up_ref, hg_ref, hidden):
-    _, both, feats = own_ref.shape
+             in_ref, latent_ref, latent_t_ref, *refs):
+    *mats, keep_ref, send_ref, grad_ref, scaled_ref, up_ref, hg_ref, hidden = refs
+    _, both, feats = mats[0].shape
     slices = nyh * nc
     rank = both // 2
     tokens, width = in_ref.shape
@@ -272,7 +280,7 @@
         inner += jnp.sum(unit_ref[:, at] * grad, axis=1, keepdims=True)
     length = length_ref[:, :1]
     latent = latent_ref[...]
-    for mats_ref, at in adapter_slices(place_ref, own_ref, other_ref):
+    for mats_ref, at in adapter_slices(place_ref, mats):
         hidden[:, at] = hidden_slice(frozen_ref, latent, mats_ref, at)
     mean = [jnp.zeros((LEN, 1), f32) for q in range(queries)]
     for f in range(slices):
@@ -287,7 +295,7 @@
     factor = inv * inv * inv * (jnp.concatenate(mean, axis=0) / width)
     latent_t = latent_t_ref[...]
     acc = jnp.zeros((rank, tokens), f32)
-    for mats_ref, at in adapter_slices(place_ref, own_ref, other_ref):
+    for mats_ref, at in adapter_slices(place_ref, mats):
         for q in range(queries):
             of = slice(q * LEN, (q + 1) * LEN)
             hg_ref[of] = (
@@ -297,7 +305,7 @@
         acc += dot_rows(mats_ref[rank:], hidden_grad)
         up_ref[:, at] = adapter_scale_factor * dot(latent_t, hidden_grad)
     latent_grad = (adapter_scale_factor * acc).astype(bf16)
-    first = place_ref[2 * own_ref.shape[0]] == 0
+    first = place_ref[place_ref.shape[0] - 3] == 0
     for f in range(slices):
         down = dot(latent_grad, in_ref[:, f * feats:(f + 1) * feats])
         for x in range(nx):
@@ -381,8 +389,6 @@
     if nyh == 4:
         slots.append(swap_neighbours(slots[1], nyl, nyh, False))
         slots.append(from_opposite(mine, nyl, nyh))
-    own_mats = jnp.stack(slots)
-    other_mats = swap_cores(own_mats)
     side = 1 - 2 * (1 - iyl)
     places = jnp.stack([iyh, iyh + side, iyh - side, iyh + 2][:nyh]).astype(jnp.int32) % nyh * nc
     ends = jnp.stack([ic, izl, iyl * nyh + iyh])
@@ -393,13 +399,23 @@
     block = exchange(got, ("zl", "x")).reshape(members * rows, half)
     columns = block.shape[0]
 
-    latent, latent_t = call(
-        project,
-        [shape((tokens, rank), bf16), shape((rank, tokens), bf16)],
-        [place, adapter_in, own_mats, other_mats],
-        spaces=[SMEM, VMEM, VMEM, VMEM],
-        flops=4 * tokens * rank * width,
-    )
+    mats, sums = [], []
+    for some in (slots[:2], slots[2:]):
+        if not some:
+            continue
+        if mats:
+            (some, sums) = lax.optimization_barrier((some, sums))
+        mats.append(jnp.stack(some))
+        mats.append(swap_cores(mats[-1]))
+        kind = bf16 if len(mats) == 2 * nyh // 2 else f32
+        sums = call(
+            functools.partial(project, len(mats) - 2),
+            [shape((tokens, rank), kind), shape((rank, tokens), kind)],
+            [place, adapter_in, *mats[-2:], *sums],
+            spaces=[SMEM] + [VMEM] * (3 + len(sums)),
+            flops=2 * tokens * rank * width,
+        )
+    latent, latent_t = sums
     inv, unit, length, sent = call(
         functools.partial(forward, nyh, nc),
         [
@@ -408,8 +424,8 @@
             shape((queries, 128), f32),
             shape((ring, nyh * queries, feats), bf16),
         ],
-        [place, latent, frozen, gain, own_mats, other_mats],
-        spaces=[SMEM] + [VMEM] * 5,
+        [place, latent, frozen, gain, *mats],
+        spaces=[SMEM] + [VMEM] * (3 + len(mats)),
         scratch=[((tokens, width), f32), ((nc, nyh * queries, feats), f32)],
         flops=2 * tokens * rank * width,
     )
@@ -471,10 +487,9 @@
         functools.partial(backward, nyh, nc),
         [shape((nyl * nx, blocks, 2 * out_rows, cols), bf16)] * 2,
         [
-            place, got, unit, length, inv, frozen, gain, adapter_in, own_mats, other_mats,
-            latent, latent_t,
+            place, got, unit, length, inv, frozen, gain, adapter_in, latent, latent_t, *mats,
         ],
-        spaces=[SMEM] + [VMEM] * 11,
+        spaces=[SMEM] + [VMEM] * (9 + len(mats)),
         scratch=[
             ((nc, nyh * queries, feats), f32),
             ((queries, width), f32),

time: 199 us -> 202 us (1.015)
    ppermute x3 -> x4, starting transfers between devices: 6.04 us -> 8.15 us  [swap_cores(): return lax.ppermute(value, 'c', [(0, 1), (1, 0)])]
    pallas_call x10 -> x11, Pallas kernels: 16.5 us -> 17.3 us  [call(): pl.pallas_call(kernel, out_shape=outs, in_specs=spaces, out_specs=out_spa...]
    ppermute x3 -> x4, waiting for transfers between devices: 6.15 us -> 5.53 us  [swap_cores(): return lax.ppermute(value, 'c', [(0, 1), (1, 0)])]
  transfers between devices with their start and end apart: 9 -> 10, of which waited for: 7 -> 7; matrix products, arithmetic and copies ran while one was open for 1% -> 2% of each run, Pallas kernels for 3% -> 2%
where the time goes in v9:
time: 202 us; the launch traced here: 201 us
  blocking collectives  88.8 us (44%)
  starting transfers between devices  44.2 us (22%)
  waiting for transfers between devices  42.7 us (21%)
  Pallas kernels  17.3 us (9%)
  local copies, waits for them, and re-layouts  4.68 us (2%)
  other arithmetic  2.5 us (1%)
    all_to_all x5, blocking collectives, exchange(): return lax.all_to_all(blocks, axes, 0, 0, tiled=True)  88.8 us
    all_to_all x3, starting transfers between devices, exchange(): return lax.all_to_all(blocks, axes, 0, 0, tiled=True)  26.9 us
    all_to_all x3, waiting for transfers between devices, exchange(): return lax.all_to_all(blocks, axes, 0, 0, tiled=True)  18.2 us
    pallas_call x11, Pallas kernels, call(): pl.pallas_call(kernel, out_shape=outs, in_specs=spaces, out_specs=out_spa...  17.3 us
    ppermute x1, waiting for transfers between devices, from_opposite(): return lax.ppermute(value, ('yl', 'yh'), pairs)  10.7 us
    ppermute x2, waiting for transfers between devices, swap_neighbours(): return lax.ppermute(value, ('yl', 'yh'), pairs)  8.33 us
    ppermute x4, starting transfers between devices, swap_cores(): return lax.ppermute(value, 'c', [(0, 1), (1, 0)])  8.15 us
    ppermute x4, waiting for transfers between devices, swap_cores(): return lax.ppermute(value, 'c', [(0, 1), (1, 0)])  5.53 us
  transfers between devices with their start and end apart: 10, of which 7 were waited for; matrix products, arithmetic and copies ran while one was open for 2% of the time, Pallas kernels for 2%

profile of v9, /device:TPU:16, one launch (start us, length us, event | category | flops | bytes accessed | tf_op | source)
XLA Modules:
  0.0 201.1 jit_solution(5330019104811606200)
XLA Ops:
  2.2 15.9 %all-to-all-start = ((bf16[16,8,1024]{2,1,0:T(8,128)(2,1)}), bf16[16,8,1024]{2,1,0:T(8,128)(2,1)S(1)}, u32[]{:S(2)}, u32[]{:S(2)}) async-start(bf16[16,8,1024]{2,1,0:T(8,128)(2,1)} %bitcast.8), calls=%async_computation | async-start | bytes 524288 | tf_op jit(solution)/shard_map/all_to_all | solution.py:34
  19.1 1.9 collective-permute-start
  21.1 8.3 %collective-permute-done = bf16[128,1024]{1,0:T(8,128)(2,1)S(1)} collective-permute-done((bf16[128,1024]{1,0:T(8,128)(2,1)S(1)}, bf16[128,1024]{1,0:T(8,128)(2,1)S(1)}, u32[]{:S(2)}, u32[]{:S(2)}) %collective-permute-start) | collective-permute-done | bytes 262176 | tf_op jit(solution)/shard_map/ppermute | solution.py:48
  29.4 2.8 %all-to-all-done = bf16[16,8,1024]{2,1,0:T(8,128)(2,1)S(1)} async-done(((bf16[16,8,1024]{2,1,0:T(8,128)(2,1)}), bf16[16,8,1024]{2,1,0:T(8,128)(2,1)S(1)}, u32[]{:S(2)}, u32[]{:S(2)}) %all-to-all-start) | async-done | bytes 262176 | tf_op jit(solution)/shard_map/all_to_all | solution.py:34
  33.8 5.2 %all-to-all-start.1 = ((bf16[8,32,4096]{2,1,0:T(8,128)(2,1)}), bf16[8,32,4096]{2,1,0:T(8,128)(2,1)}, u32[]{:S(2)}, u32[]{:S(2)}) async-start(bf16[8,32,4096]{2,1,0:T(8,128)(2,1)} %broadcast_in_dim.53), calls=%async_computation.1 | async-start | bytes 4194304 | tf_op jit(solution)/shard_map/all_to_all | solution.py:34
  39.0 1.9 collective-permute-start.3
  41.0 4.2 %collective-permute-start.2 = (bf16[128,1024]{1,0:T(8,128)(2,1)S(1)}, bf16[128,1024]{1,0:T(8,128)(2,1)}, u32[]{:S(2)}, u32[]{:S(2)}) collective-permute-start(bf16[128,1024]{1,0:T(8,128)(2,1)S(1)} %get-tuple-element.59), channel_id=1, source_target_pairs={{36,0},{4,32},{38,2},{6,34},{32,4},{0,36},{34,6},{2,38},{37,1},{5,... | collective-permute-start | bytes 786440 | tf_op jit(solution)/shard_map/ppermute | solution.py:56
  45.2 3.0 %collective-permute-start.1 = (bf16[128,1024]{1,0:T(8,128)(2,1)}, bf16[128,1024]{1,0:T(8,128)(2,1)}, u32[]{:S(2)}, u32[]{:S(2)}) collective-permute-start(bf16[128,1024]{1,0:T(8,128)(2,1)} %copy-done.10), channel_id=1, source_target_pairs={{0,32},{32,0},{2,34},{34,2},{4,36},{36,4},{6,38},{38,6},{1,33},{33... | collective-permute-start | bytes 786440 | tf_op jit(solution)/shard_map/ppermute | solution.py:48
  49.7 10.7 %collective-permute-done.2 = bf16[128,1024]{1,0:T(8,128)(2,1)} collective-permute-done((bf16[128,1024]{1,0:T(8,128)(2,1)S(1)}, bf16[128,1024]{1,0:T(8,128)(2,1)}, u32[]{:S(2)}, u32[]{:S(2)}) %collective-permute-start.2) | collective-permute-done | bytes 262176 | tf_op jit(solution)/shard_map/ppermute | solution.py:56
  61.6 1.9 collective-permute-start.4
  66.7 2.4 %shard_map.88 = (f32[128,128]{1,0:T(8,128)S(1)}, f32[4,8192]{1,0:T(4,128)S(1)}, f32[4,128]{1,0:T(4,128)S(1)}, bf16[16,16,1024]{2,1,0:T(8,128)(2,1)S(1)}) custom-call(s32[11]{0:T(128)S(1)} %concatenate.6.place_ref, bf16[128,64]{1,0:T(8,128)(2,1)S(1)} %get-tuple-element.36.latent_ref, bf16[128,8192]{1,0:T(8,128)(2,1)S(1)} %copy-done.1, ...), custom_call_target="tpu_custom_call" | custom-call | flops 134217728 | bytes 4966444 | tf_op jit(solution)/shard_map/pallas_call | solution.py:74
  70.0 5.9 %all-to-all-start.2 = ((bf16[16,16,1024]{2,1,0:T(8,128)(2,1)}), bf16[16,16,1024]{2,1,0:T(8,128)(2,1)}, u32[]{:S(2)}, u32[]{:S(2)}) async-start(bf16[16,16,1024]{2,1,0:T(8,128)(2,1)} %copy-done.8), calls=%async_computation.2 | async-start | bytes 1048576 | tf_op jit(solution)/shard_map/all_to_all | solution.py:34
  76.5 15.3 %all-to-all-done.2.query_ref = bf16[16,16,1024]{2,1,0:T(8,128)(2,1)} async-done(((bf16[16,16,1024]{2,1,0:T(8,128)(2,1)}), bf16[16,16,1024]{2,1,0:T(8,128)(2,1)}, u32[]{:S(2)}, u32[]{:S(2)}) %all-to-all-start.2) | async-done | bytes 524320 | tf_op jit(solution)/shard_map/all_to_all | solution.py:34
  91.8 4.1 %shard_map.89.own_ref = f32[136,256]{1,0:T(8,128)S(1)} custom-call(bf16[16,16,1024]{2,1,0:T(8,128)(2,1)} %all-to-all-done.2.query_ref, bf16[256,4096]{1,0:T(8,128)(2,1)} %bitcast.18.block_ref), custom_call_target="tpu_custom_call" | custom-call | flops 1073741824 | bytes 2760704 | tf_op jit(solution)/shard_map/pallas_call | solution.py:74
  96.0 2.3 %collective-permute-start.5 = (f32[136,256]{1,0:T(8,128)S(1)}, f32[136,256]{1,0:T(8,128)S(1)}, u32[]{:S(2)}, u32[]{:S(2)}) collective-permute-start(f32[136,256]{1,0:T(8,128)S(1)} %shard_map.89.own_ref), channel_id=1, source_target_pairs={{0,1},{1,0},{2,3},{3,2},{4,5},{5,4},{6,7},{7,6},{8,9},{9,8},{10,11... | collective-permute-start | bytes 417800 | tf_op jit(solution)/shard_map/ppermute | solution.py:38
  99.7 11.9 %all_to_all.40.got_ref = f32[16,1,384]{2,1,0:T(1,128)S(1)} all-to-all(f32[16,1,384]{2,1,0:T(1,128)S(1)} %get-tuple-element.43), channel_id=1, replica_groups=mesh['zh'=4,'zl'=2,'yl'=2,'x'=4,'yh'=4,'c'=2] {'zl','yl','yh'}, dimensions={0} | all-to-all | bytes 49152 | tf_op jit(solution)/shard_map/all_to_all | solution.py:34
  112.2 18.7 %all_to_all.41.cols_ref = f32[16,1,256]{2,1,0:T(1,128)S(1)} all-to-all(f32[16,1,256]{2,1,0:T(1,128)S(1)} %get-tuple-element.45), channel_id=1, replica_groups=mesh['zh'=4,'zl'=2,'yl'=2,'x'=4,'yh'=4,'c'=2] {'zh','x'}, dimensions={0} | all-to-all | bytes 32768 | tf_op jit(solution)/shard_map/all_to_all | solution.py:34
  131.0 2.3 %shard_map.92 = (bf16[16,16,1024]{2,1,0:T(8,128)(2,1)S(1)}, f32[8,128]{1,0:T(8,128)S(1)}) custom-call(f32[128,256]{1,0:T(8,128)S(1)} %get-tuple-element.41.expo_ref, f32[8,256]{1,0:T(8,128)S(1)} %get-tuple-element.42.aux_ref, f32[128,256]{1,0:T(8,128)S(1)} %compare_convert_fusion.onehot_ref, f32[1,128]{1,0:T(1,128)S(1)} %get-tuple-element.44.row_ref, ...), custom_call_target="tpu_custom_call" | custom-call | flops 536870912 | bytes 2912768 | tf_op jit(solution)/shard_map/pallas_call | solution.py:74
  133.3 20.6 %all_to_all.42.got_ref = bf16[16,16,1024]{2,1,0:T(8,128)(2,1)S(1)} all-to-all(bf16[16,16,1024]{2,1,0:T(8,128)(2,1)S(1)} %get-tuple-element.46), channel_id=1, replica_groups=mesh['zh'=4,'zl'=2,'yl'=2,'x'=4,'yh'=4,'c'=2] {'yl','yh','c'}, dimensions={0} | all-to-all | bytes 1048576 | tf_op jit(solution)/shard_map/all_to_all | solution.py:34
  153.9 4.0 %shard_map.93 = (bf16[8,32,16,128]{3,2,1,0:T(8,128)(2,1)S(1)}, bf16[8,32,16,128]{3,2,1,0:T(8,128)(2,1)S(1)}) custom-call(s32[11]{0:T(128)S(1)} %concatenate.6.place_ref, bf16[16,16,1024]{2,1,0:T(8,128)(2,1)S(1)} %all_to_all.42.got_ref, f32[4,8192]{1,0:T(4,128)S(1)} %get-tuple-element.47.unit_ref, f32[4,128]{1,0:T(4,128)S(1)} %get-tuple-element.48.length_ref, ...), custom_call_target="tpu_custom_call" | custom-call | flops 536870912 | bytes 9177132 | tf_op jit(solution)/shard_map/pallas_call | solution.py:74
  157.9 2.0 %collective-permute-start.6 = (bf16[8,32,16,128]{3,2,1,0:T(8,128)(2,1)S(1)}, bf16[8,32,16,128]{3,2,1,0:T(8,128)(2,1)S(1)}, u32[]{:S(2)}, u32[]{:S(2)}) collective-permute-start(bf16[8,32,16,128]{3,2,1,0:T(8,128)(2,1)S(1)} %get-tuple-element.52), channel_id=1, source_target_pairs={{0,1},{1,0},{2,3},{3,2},{4,5},{5,4},{6,7},{7,6},{8,9},{9,8},{10,11... | collective-permute-start | bytes 3145736 | tf_op jit(solution)/shard_map/ppermute | solution.py:38
  160.0 2.5 %collective-permute-done.6.got_ref = bf16[8,32,16,128]{3,2,1,0:T(8,128)(2,1)S(1)} collective-permute-done((bf16[8,32,16,128]{3,2,1,0:T(8,128)(2,1)S(1)}, bf16[8,32,16,128]{3,2,1,0:T(8,128)(2,1)S(1)}, u32[]{:S(2)}, u32[]{:S(2)}) %collective-permute-start.6) | collective-permute-done | bytes 1048608 | tf_op jit(solution)/shard_map/ppermute | solution.py:38
  162.7 19.2 %all_to_all.43.got_ref = bf16[8,33,16,128]{3,2,1,0:T(8,128)(2,1)S(1)} all-to-all(bf16[8,33,16,128]{3,2,1,0:T(8,128)(2,1)S(1)} %shard_map.94), channel_id=1, replica_groups=mesh['zh'=4,'zl'=2,'yl'=2,'x'=4,'yh'=4,'c'=2] {'yl','x'}, dimensions={0} | all-to-all | bytes 2162688 | tf_op jit(solution)/shard_map/all_to_all | solution.py:34
  182.1 18.3 %all_to_all.44.got_ref = bf16[32,32,128]{2,1,0:T(8,128)(2,1)S(1)} all-to-all(bf16[32,32,128]{2,1,0:T(8,128)(2,1)S(1)} %shard_map.95), channel_id=1, replica_groups=mesh['zh'=4,'zl'=2,'yl'=2,'x'=4,'yh'=4,'c'=2] {'zh','zl','yh'}, dimensions={0} | all-to-all | bytes 524288 | tf_op jit(solution)/shard_map/all_to_all | solution.py:34
  (57 shorter events, 14.5 us)
Async XLA Ops:
  2.2 30.0 %all-to-all-start = ((bf16[16,8,1024]{2,1,0:T(8,128)(2,1)}), bf16[16,8,1024]{2,1,0:T(8,128)(2,1)S(1)}, u32[]{:S(2)}, u32[]{:S(2)}) async-start(bf16[16,8,1024]{2,1,0:T(8,128)(2,1)} %bitcast.8), calls=%async_computation | async-start | bytes 524288 | tf_op jit(solution)/shard_map/all_to_all | solution.py:34
  19.1 10.3 %collective-permute-start = (bf16[128,1024]{1,0:T(8,128)(2,1)S(1)}, bf16[128,1024]{1,0:T(8,128)(2,1)S(1)}, u32[]{:S(2)}, u32[]{:S(2)}) collective-permute-start(bf16[128,1024]{1,0:T(8,128)(2,1)S(1)} %get-tuple-element.59), channel_id=1, source_target_pairs={{32,2},{2,32},{34,4},{4,34},{36,6},{6,36},{38,0},{0,38},{33,3},{3,... | collective-permute-start | bytes 786440 | tf_op jit(solution)/shard_map/ppermute | solution.py:48
  29.4 9.6 %copy-start.10 = (bf16[128,1024]{1,0:T(8,128)(2,1)}, bf16[128,1024]{1,0:T(8,128)(2,1)S(1)}, u32[]{:S(2)}) copy-start(bf16[128,1024]{1,0:T(8,128)(2,1)S(1)} %collective-permute-done) | copy-start | bytes 786436
  33.8 14.6 %copy-start = (bf16[128,8192]{1,0:T(8,128)(2,1)S(1)}, bf16[128,8192]{1,0:T(8,128)(2,1)}, u32[]{:S(2)}) copy-start(bf16[128,8192]{1,0:T(8,128)(2,1)} %in_ref.5) | copy-start | bytes 6291460
  33.8 36.2 %all-to-all-start.1 = ((bf16[8,32,4096]{2,1,0:T(8,128)(2,1)}), bf16[8,32,4096]{2,1,0:T(8,128)(2,1)}, u32[]{:S(2)}, u32[]{:S(2)}) async-start(bf16[8,32,4096]{2,1,0:T(8,128)(2,1)} %broadcast_in_dim.53), calls=%async_computation.1 | async-start | bytes 4194304 | tf_op jit(solution)/shard_map/all_to_all | solution.py:34
  39.0 9.4 %collective-permute-start.3 = (bf16[2,128,1024]{2,1,0:T(8,128)(2,1)S(1)}, bf16[2,128,1024]{2,1,0:T(8,128)(2,1)S(1)}, u32[]{:S(2)}, u32[]{:S(2)}) collective-permute-start(bf16[2,128,1024]{2,1,0:T(8,128)(2,1)S(1)} %pad_maximum_fusion.refs_0_), channel_id=1, source_target_pairs={{0,1},{1,0},{2,3},{3,2},{4,5},{5,4},{6,7},{7,6},{8,9},{9,8},{10,11... | collective-permute-start | bytes 1572872 | tf_op jit(solution)/shard_map/ppermute | solution.py:38
  41.0 19.4 %collective-permute-start.2 = (bf16[128,1024]{1,0:T(8,128)(2,1)S(1)}, bf16[128,1024]{1,0:T(8,128)(2,1)}, u32[]{:S(2)}, u32[]{:S(2)}) collective-permute-start(bf16[128,1024]{1,0:T(8,128)(2,1)S(1)} %get-tuple-element.59), channel_id=1, source_target_pairs={{36,0},{4,32},{38,2},{6,34},{32,4},{0,36},{34,6},{2,38},{37,1},{5,... | collective-permute-start | bytes 786440 | tf_op jit(solution)/shard_map/ppermute | solution.py:56
  45.2 15.2 %collective-permute-start.1 = (bf16[128,1024]{1,0:T(8,128)(2,1)}, bf16[128,1024]{1,0:T(8,128)(2,1)}, u32[]{:S(2)}, u32[]{:S(2)}) collective-permute-start(bf16[128,1024]{1,0:T(8,128)(2,1)} %copy-done.10), channel_id=1, source_target_pairs={{0,32},{32,0},{2,34},{34,2},{4,36},{36,4},{6,38},{38,6},{1,33},{33... | collective-permute-start | bytes 786440 | tf_op jit(solution)/shard_map/ppermute | solution.py:48
  48.4 11.9 %copy-start.3 = (bf16[2,128,1024]{2,1,0:T(8,128)(2,1)}, bf16[2,128,1024]{2,1,0:T(8,128)(2,1)S(1)}, u32[]{:S(2)}) copy-start(bf16[2,128,1024]{2,1,0:T(8,128)(2,1)S(1)} %collective-permute-done.3.refs_1_) | copy-start | bytes 1572868
  60.3 6.3 %copy-start.1 = (bf16[128,8192]{1,0:T(8,128)(2,1)S(1)}, bf16[128,8192]{1,0:T(8,128)(2,1)}, u32[]{:S(2)}) copy-start(bf16[128,8192]{1,0:T(8,128)(2,1)} %frozen_ref.3) | copy-start | bytes 6291460
  60.4 6.3 %copy-start.4 = (bf16[2,128,1024]{2,1,0:T(8,128)(2,1)S(1)}, bf16[2,128,1024]{2,1,0:T(8,128)(2,1)}, u32[]{:S(2)}) copy-start(bf16[2,128,1024]{2,1,0:T(8,128)(2,1)} %copy-done.3) | copy-start | bytes 1572868
  60.4 6.3 %copy-start.9 = (f32[8192]{0:T(1024)S(1)}, f32[8192]{0:T(1024)}, u32[]{:S(2)}) copy-start(f32[8192]{0:T(1024)} %param.9) | copy-start | bytes 98308
  61.6 3.8 %collective-permute-start.4 = (bf16[2,128,1024]{2,1,0:T(8,128)(2,1)S(1)}, bf16[2,128,1024]{2,1,0:T(8,128)(2,1)S(1)}, u32[]{:S(2)}, u32[]{:S(2)}) collective-permute-start(bf16[2,128,1024]{2,1,0:T(8,128)(2,1)S(1)} %pad_maximum_fusion.1.refs_0_.refs_2_), channel_id=1, source_target_pairs={{0,1},{1,0},{2,3},{3,2},{4,5},{5,4},{6,7},{7,6},{8,9},{9,8},{10,11... | collective-permute-start | bytes 1572872 | tf_op jit(solution)/shard_map/ppermute | solution.py:38
  65.4 1.3 copy-start.6
  66.7 9.3 %copy-start.11 = (s32[32]{0:T(128)S(1)}, s32[32]{0:T(128)}, u32[]{:S(2)}) copy-start(s32[32]{0:T(128)} %param.13) | copy-start | bytes 388
  69.2 0.8 copy-start.8
  70.0 21.9 %all-to-all-start.2 = ((bf16[16,16,1024]{2,1,0:T(8,128)(2,1)}), bf16[16,16,1024]{2,1,0:T(8,128)(2,1)}, u32[]{:S(2)}, u32[]{:S(2)}) async-start(bf16[16,16,1024]{2,1,0:T(8,128)(2,1)} %copy-done.8), calls=%async_computation.2 | async-start | bytes 1048576 | tf_op jit(solution)/shard_map/all_to_all | solution.py:34
  96.0 57.9 %copy-start.2 = (bf16[128,8192]{1,0:T(8,128)(2,1)S(1)}, bf16[128,8192]{1,0:T(8,128)(2,1)}, u32[]{:S(2)}) copy-start(bf16[128,8192]{1,0:T(8,128)(2,1)} %frozen_ref.3) | copy-start | bytes 6291460
  96.0 57.9 %copy-start.5 = (bf16[2,128,1024]{2,1,0:T(8,128)(2,1)S(1)}, bf16[2,128,1024]{2,1,0:T(8,128)(2,1)}, u32[]{:S(2)}) copy-start(bf16[2,128,1024]{2,1,0:T(8,128)(2,1)} %copy-done.3) | copy-start | bytes 1572868
  96.0 57.9 %copy-start.7 = (bf16[2,128,1024]{2,1,0:T(8,128)(2,1)S(1)}, bf16[2,128,1024]{2,1,0:T(8,128)(2,1)}, u32[]{:S(2)}) copy-start(bf16[2,128,1024]{2,1,0:T(8,128)(2,1)} %copy-done.6) | copy-start | bytes 1572868
  96.0 3.5 %collective-permute-start.5 = (f32[136,256]{1,0:T(8,128)S(1)}, f32[136,256]{1,0:T(8,128)S(1)}, u32[]{:S(2)}, u32[]{:S(2)}) collective-permute-start(f32[136,256]{1,0:T(8,128)S(1)} %shard_map.89.own_ref), channel_id=1, source_target_pairs={{0,1},{1,0},{2,3},{3,2},{4,5},{5,4},{6,7},{7,6},{8,9},{9,8},{10,11... | collective-permute-start | bytes 417800 | tf_op jit(solution)/shard_map/ppermute | solution.py:38
  157.9 4.6 %collective-permute-start.6 = (bf16[8,32,16,128]{3,2,1,0:T(8,128)(2,1)S(1)}, bf16[8,32,16,128]{3,2,1,0:T(8,128)(2,1)S(1)}, u32[]{:S(2)}, u32[]{:S(2)}) collective-permute-start(bf16[8,32,16,128]{3,2,1,0:T(8,128)(2,1)S(1)} %get-tuple-element.52), channel_id=1, source_target_pairs={{0,1},{1,0},{2,3},{3,2},{4,5},{5,4},{6,7},{7,6},{8,9},{9,8},{10,11... | collective-permute-start | bytes 3145736 | tf_op jit(solution)/shard_map/ppermute | solution.py:38

commit v10 on v8

--- a/solution.py
+++ b/solution.py
@@ -192,7 +192,7 @@
     return jnp.transpose(jnp.broadcast_to(row, (n, n)))
 
 
-def exponentials(own_ref, other_ref, onehot_ref, expo_ref, aux_ref, sums_ref):
+def exponentials(own_ref, other_ref, onehot_ref, expo_ref, aux_ref, rows_ref, cols_ref):
     count, columns = expo_ref.shape
     inv_norm = 1.0 / jnp.sqrt(own_ref[count:count + 1] + other_ref[count:count + 1])
     scores = inv_temp * ((own_ref[:count] + other_ref[:count]) * inv_norm)
@@ -202,32 +202,22 @@
     aux_ref[0:1] = inv_norm
     aux_ref[1:2] = jnp.full((1, columns), hits)
     row = across(jnp.sum(expo, axis=1, keepdims=True))[0:1]
+    for y in range(rows_ref.shape[0]):
+        rows_ref[y] = row
     col = 0.5 * jnp.sum(expo, axis=0, keepdims=True)
-    sums = jnp.concatenate([row, col], axis=1)
-    for i in range(sums_ref.shape[0]):
-        sums_ref[i] = sums
-
-
-def combine(ny, place_ref, got_ref, row_ref, cols_ref):
-    count = row_ref.shape[1]
-    last = place_ref.shape[0] - 1
-    first = place_ref[last - 1] * ny
-    row = functools.reduce(jnp.add, [got_ref[first + y] for y in range(ny)])
-    row_ref[...] = row[:, :count]
-    peers = range(got_ref.shape[0] // ny)
-    col = functools.reduce(jnp.add, [got_ref[zl * ny + place_ref[last]] for zl in peers])
     for i in range(cols_ref.shape[0]):
-        cols_ref[i] = col[:, count:]
-
-
-def weigh(nyh, ny, members, expo_ref, aux_ref, onehot_ref, row_ref, cols_ref, block_ref,
+        cols_ref[i] = col
+
+
+def weigh(nyh, expo_ref, aux_ref, onehot_ref, rows_ref, cols_ref, block_ref,
           out_ref, loss_ref, total_ref, parts, sems):
     count, columns = expo_ref.shape
     ring, rows, feats = out_ref.shape
     queries = rows // nyh
     copies = start_slices(block_ref, parts, sems)
-    row = row_ref[...]
-    col = functools.reduce(jnp.add, [cols_ref[i] for i in range(cols_ref.shape[0])])
+    ny, members = rows_ref.shape[0], cols_ref.shape[0]
+    row = functools.reduce(jnp.add, [rows_ref[y] for y in range(ny)])
+    col = functools.reduce(jnp.add, [cols_ref[i] for i in range(members)])
     loss = (
         0.5 * jnp.sum(jnp.log(row), axis=1, keepdims=True) / ny
         + jnp.sum(jnp.log(col), axis=1, keepdims=True) / members
@@ -385,8 +375,7 @@
     other_mats = swap_cores(own_mats)
     side = 1 - 2 * (1 - iyl)
     places = jnp.stack([iyh, iyh + side, iyh - side, iyh + 2][:nyh]).astype(jnp.int32) % nyh * nc
-    ends = jnp.stack([ic, izl, iyl * nyh + iyh])
-    place = jnp.concatenate([places + ic, places + 1 - ic, ends]).astype(jnp.int32)
+    place = jnp.concatenate([places + ic, places + 1 - ic, ic.reshape(1)]).astype(jnp.int32)
 
     got = got.reshape(nzh, nyh, rows, feats).transpose(0, 2, 1, 3).reshape(nzh * rows, half)
     got = jnp.broadcast_to(got[None], (nzl * nx, nzh * rows, half))
@@ -438,25 +427,22 @@
         flops=4 * ring * nyh * queries * columns * half,
     )
     other = swap_cores(own)
-    expo, aux, sent = call(
+    expo, aux, by_row, by_col = call(
         exponentials,
         [
             shape((count, columns), f32),
             shape((8, columns), f32),
-            shape((nzl * ny, 1, count + columns), f32),
+            shape((ny, 1, count), f32),
+            shape((members, 1, columns), f32),
         ],
         [own, other, onehot],
     )
-    row, sent = call(
-        functools.partial(combine, ny),
-        [shape((1, count), f32), shape((nzh * nx, 1, columns), f32)],
-        [place, exchange(sent, ("zl", *ROW))],
-        spaces=[SMEM, VMEM],
-    )
+    by_row = exchange(by_row, ROW)
+    by_col = exchange(by_col, COLUMN)
     sent, loss = call(
-        functools.partial(weigh, nyh, ny, members),
+        functools.partial(weigh, nyh),
         [shape((ring, nyh * queries, feats), bf16), shape((8, 128), f32)],
-        [expo, aux, onehot, row, exchange(sent, ("zh", "x")), block],
+        [expo, aux, onehot, by_row, by_col, block],
         spaces=[VMEM] * 5 + [HBM],
         scratch=[((ring * nyh * queries, feats), f32), ((nyh, columns, feats), bf16)],
         copies=nyh,

time: 199 us -> 196 us (0.985)
  blocking collectives: 88.3 us -> 86.3 us
    pallas_call x10 -> x9, Pallas kernels: 16.5 us -> 15.9 us  [call(): pl.pallas_call(kernel, out_shape=outs, in_specs=spaces, out_specs=out_spa...]
where the time goes in v10:
time: 196 us
  blocking collectives  86.3 us (44%)
  waiting for transfers between devices  43 us (22%)
  starting transfers between devices  42.7 us (22%)
  Pallas kernels  15.9 us (8%)
  local copies, waits for them, and re-layouts  5.35 us (3%)
    all_to_all x5, blocking collectives, exchange(): return lax.all_to_all(blocks, axes, 0, 0, tiled=True)  86.3 us
    all_to_all x3, starting transfers between devices, exchange(): return lax.all_to_all(blocks, axes, 0, 0, tiled=True)  27.5 us
    all_to_all x3, waiting for transfers between devices, exchange(): return lax.all_to_all(blocks, axes, 0, 0, tiled=True)  18.1 us
    pallas_call x9, Pallas kernels, call(): pl.pallas_call(kernel, out_shape=outs, in_specs=spaces, out_specs=out_spa...  15.9 us
    ppermute x1, waiting for transfers between devices, from_opposite(): return lax.ppermute(value, ('yl', 'yh'), pairs)  10.4 us
    ppermute x2, waiting for transfers between devices, swap_neighbours(): return lax.ppermute(value, ('yl', 'yh'), pairs)  8.33 us
    ppermute x3, waiting for transfers between devices, swap_cores(): return lax.ppermute(value, 'c', [(0, 1), (1, 0)])  6.11 us
    ppermute x3, starting transfers between devices, swap_cores(): return lax.ppermute(value, 'c', [(0, 1), (1, 0)])  6.09 us
  transfers between devices with their start and end apart: 9, of which 7 were waited for; matrix products, arithmetic and copies ran while one was open for 1% of the time, Pallas kernels for 3%

profile of v10, /device:TPU:16, one launch (start us, length us, event | category | flops | bytes accessed | tf_op | source)
XLA Modules:
  0.0 195.6 jit_solution(10403495045688366462)
XLA Ops:
  2.2 15.9 %all-to-all-start = ((bf16[16,8,1024]{2,1,0:T(8,128)(2,1)}), bf16[16,8,1024]{2,1,0:T(8,128)(2,1)S(1)}, u32[]{:S(2)}, u32[]{:S(2)}) async-start(bf16[16,8,1024]{2,1,0:T(8,128)(2,1)} %bitcast.8), calls=%async_computation | async-start | bytes 524288 | tf_op jit(solution)/shard_map/all_to_all | solution.py:34
  19.1 1.9 collective-permute-start
  21.1 8.3 %collective-permute-done = bf16[128,1024]{1,0:T(8,128)(2,1)S(1)} collective-permute-done((bf16[128,1024]{1,0:T(8,128)(2,1)S(1)}, bf16[128,1024]{1,0:T(8,128)(2,1)S(1)}, u32[]{:S(2)}, u32[]{:S(2)}) %collective-permute-start) | collective-permute-done | bytes 262176 | tf_op jit(solution)/shard_map/ppermute | solution.py:48
  29.4 2.8 %all-to-all-done = bf16[16,8,1024]{2,1,0:T(8,128)(2,1)S(1)} async-done(((bf16[16,8,1024]{2,1,0:T(8,128)(2,1)}), bf16[16,8,1024]{2,1,0:T(8,128)(2,1)S(1)}, u32[]{:S(2)}, u32[]{:S(2)}) %all-to-all-start) | async-done | bytes 262176 | tf_op jit(solution)/shard_map/all_to_all | solution.py:34
  33.8 5.0 %all-to-all-start.1 = ((bf16[8,32,4096]{2,1,0:T(8,128)(2,1)}), bf16[8,32,4096]{2,1,0:T(8,128)(2,1)}, u32[]{:S(2)}, u32[]{:S(2)}) async-start(bf16[8,32,4096]{2,1,0:T(8,128)(2,1)} %broadcast_in_dim.53), calls=%async_computation.1 | async-start | bytes 4194304 | tf_op jit(solution)/shard_map/all_to_all | solution.py:34
  38.8 4.2 %collective-permute-start.2 = (bf16[128,1024]{1,0:T(8,128)(2,1)S(1)}, bf16[128,1024]{1,0:T(8,128)(2,1)S(1)}, u32[]{:S(2)}, u32[]{:S(2)}) collective-permute-start(bf16[128,1024]{1,0:T(8,128)(2,1)S(1)} %get-tuple-element.45), channel_id=1, source_target_pairs={{36,0},{4,32},{38,2},{6,34},{32,4},{0,36},{34,6},{2,38},{37,1},{5,... | collective-permute-start | bytes 786440 | tf_op jit(solution)/shard_map/ppermute | solution.py:56
  43.0 3.0 %collective-permute-start.1 = (bf16[128,1024]{1,0:T(8,128)(2,1)S(1)}, bf16[128,1024]{1,0:T(8,128)(2,1)S(1)}, u32[]{:S(2)}, u32[]{:S(2)}) collective-permute-start(bf16[128,1024]{1,0:T(8,128)(2,1)S(1)} %collective-permute-done), channel_id=1, source_target_pairs={{0,32},{32,0},{2,34},{34,2},{4,36},{36,4},{6,38},{38,6},{1,33},{33... | collective-permute-start | bytes 786440 | tf_op jit(solution)/shard_map/ppermute | solution.py:48
  46.0 10.4 %collective-permute-done.2 = bf16[128,1024]{1,0:T(8,128)(2,1)S(1)} collective-permute-done((bf16[128,1024]{1,0:T(8,128)(2,1)S(1)}, bf16[128,1024]{1,0:T(8,128)(2,1)S(1)}, u32[]{:S(2)}, u32[]{:S(2)}) %collective-permute-start.2) | collective-permute-done | bytes 262176 | tf_op jit(solution)/shard_map/ppermute | solution.py:56
  56.6 1.9 collective-permute-start.3
  58.7 2.4 %collective-permute-done.3.other_ref = bf16[4,128,1024]{2,1,0:T(8,128)(2,1)S(1)} collective-permute-done((bf16[4,128,1024]{2,1,0:T(8,128)(2,1)S(1)}, bf16[4,128,1024]{2,1,0:T(8,128)(2,1)S(1)}, u32[]{:S(2)}, u32[]{:S(2)}) %collective-permute-start.3) | collective-permute-done | bytes 1048608 | tf_op jit(solution)/shard_map/ppermute | solution.py:38
  64.7 3.2 %shard_map.87 = (f32[128,128]{1,0:T(8,128)S(1)}, f32[4,8192]{1,0:T(4,128)S(1)}, f32[4,128]{1,0:T(4,128)S(1)}, bf16[16,16,1024]{2,1,0:T(8,128)(2,1)}) custom-call(s32[9]{0:T(128)S(1)} %pad_add_fusion.place_ref, bf16[128,64]{1,0:T(8,128)(2,1)S(1)} %get-tuple-element.23.latent_ref, bf16[128,8192]{1,0:T(8,128)(2,1)S(1)} %copy-done.2, f32[1,8192]{1,0:T(1,128)S(1)} %bitcast.23, ...), custom_call_target="tpu_custom_call" | custom-call | flops 134217728 | bytes 4966436 | tf_op jit(solution)/shard_map/pallas_call | solution.py:74
  67.9 6.6 %all-to-all-start.2 = ((bf16[16,16,1024]{2,1,0:T(8,128)(2,1)}), bf16[16,16,1024]{2,1,0:T(8,128)(2,1)S(1)}, u32[]{:S(2)}, u32[]{:S(2)}) async-start(bf16[16,16,1024]{2,1,0:T(8,128)(2,1)} %get-tuple-element.26), calls=%async_computation.2 | async-start | bytes 1048576 | tf_op jit(solution)/shard_map/all_to_all | solution.py:34
  75.1 15.2 %all-to-all-done.2.query_ref = bf16[16,16,1024]{2,1,0:T(8,128)(2,1)S(1)} async-done(((bf16[16,16,1024]{2,1,0:T(8,128)(2,1)}), bf16[16,16,1024]{2,1,0:T(8,128)(2,1)S(1)}, u32[]{:S(2)}, u32[]{:S(2)}) %all-to-all-start.2) | async-done | bytes 524320 | tf_op jit(solution)/shard_map/all_to_all | solution.py:34
  90.3 3.3 %shard_map.88.own_ref = f32[136,256]{1,0:T(8,128)S(1)} custom-call(bf16[16,16,1024]{2,1,0:T(8,128)(2,1)S(1)} %all-to-all-done.2.query_ref, bf16[256,4096]{1,0:T(8,128)(2,1)} %bitcast.16.block_ref), custom_call_target="tpu_custom_call" | custom-call | flops 1073741824 | bytes 2760704 | tf_op jit(solution)/shard_map/pallas_call | solution.py:74
  93.6 2.1 %collective-permute-start.4 = (f32[136,256]{1,0:T(8,128)S(1)}, f32[136,256]{1,0:T(8,128)S(1)}, u32[]{:S(2)}, u32[]{:S(2)}) collective-permute-start(f32[136,256]{1,0:T(8,128)S(1)} %shard_map.88.own_ref), channel_id=1, source_target_pairs={{0,1},{1,0},{2,3},{3,2},{4,5},{5,4},{6,7},{7,6},{8,9},{9,8},{10,11... | collective-permute-start | bytes 417800 | tf_op jit(solution)/shard_map/ppermute | solution.py:38
  97.2 9.4 %all_to_all.40.rows_ref = f32[8,1,128]{2,1,0:T(1,128)S(1)} all-to-all(f32[8,1,128]{2,1,0:T(1,128)S(1)} %get-tuple-element.30), channel_id=1, replica_groups=mesh['zh'=4,'zl'=2,'yl'=2,'x'=4,'yh'=4,'c'=2] {'yl','yh'}, dimensions={0} | all-to-all | bytes 8192 | tf_op jit(solution)/shard_map/all_to_all | solution.py:34
  106.6 19.0 %all_to_all.41.cols_ref = f32[32,1,256]{2,1,0:T(1,128)S(1)} all-to-all(f32[32,1,256]{2,1,0:T(1,128)S(1)} %get-tuple-element.31), channel_id=1, replica_groups=mesh['zh'=4,'zl'=2,'yl'=2,'x'=4,'yh'=4,'c'=2] {'zh','zl','x'}, dimensions={0} | all-to-all | bytes 65536 | tf_op jit(solution)/shard_map/all_to_all | solution.py:34
  125.6 2.3 %shard_map.90 = (bf16[16,16,1024]{2,1,0:T(8,128)(2,1)S(1)}, f32[8,128]{1,0:T(8,128)S(1)}) custom-call(f32[128,256]{1,0:T(8,128)S(1)} %get-tuple-element.28.expo_ref, f32[8,256]{1,0:T(8,128)S(1)} %get-tuple-element.29.aux_ref, f32[128,256]{1,0:T(8,128)S(1)} %compare_convert_fusion.onehot_ref, f32[8,1,128]{2,1,0:T(1,128)S(1)} %all_to_all.40.rows_ref, ...), custom_call_target="tpu_custom_call" | custom-call | flops 536870912 | bytes 2932736 | tf_op jit(solution)/shard_map/pallas_call | solution.py:74
  127.9 20.7 %all_to_all.42.got_ref = bf16[16,16,1024]{2,1,0:T(8,128)(2,1)S(1)} all-to-all(bf16[16,16,1024]{2,1,0:T(8,128)(2,1)S(1)} %get-tuple-element.32), channel_id=1, replica_groups=mesh['zh'=4,'zl'=2,'yl'=2,'x'=4,'yh'=4,'c'=2] {'yl','yh','c'}, dimensions={0} | all-to-all | bytes 1048576 | tf_op jit(solution)/shard_map/all_to_all | solution.py:34
  148.6 4.0 %shard_map.91 = (bf16[8,32,16,128]{3,2,1,0:T(8,128)(2,1)S(1)}, bf16[8,32,16,128]{3,2,1,0:T(8,128)(2,1)S(1)}) custom-call(s32[9]{0:T(128)S(1)} %pad_add_fusion.place_ref, bf16[16,16,1024]{2,1,0:T(8,128)(2,1)S(1)} %all_to_all.42.got_ref, f32[4,8192]{1,0:T(4,128)S(1)} %get-tuple-element.33.unit_ref, f32[4,128]{1,0:T(4,128)S(1)} %get-tuple-element.34.length_ref, ...), custom_call_target="tpu_custom_call" | custom-call | flops 536870912 | bytes 9177124 | tf_op jit(solution)/shard_map/pallas_call | solution.py:74
  152.6 2.0 %collective-permute-start.5 = (bf16[8,32,16,128]{3,2,1,0:T(8,128)(2,1)S(1)}, bf16[8,32,16,128]{3,2,1,0:T(8,128)(2,1)S(1)}, u32[]{:S(2)}, u32[]{:S(2)}) collective-permute-start(bf16[8,32,16,128]{3,2,1,0:T(8,128)(2,1)S(1)} %get-tuple-element.38), channel_id=1, source_target_pairs={{0,1},{1,0},{2,3},{3,2},{4,5},{5,4},{6,7},{7,6},{8,9},{9,8},{10,11... | collective-permute-start | bytes 3145736 | tf_op jit(solution)/shard_map/ppermute | solution.py:38
  154.7 2.5 %collective-permute-done.5.got_ref = bf16[8,32,16,128]{3,2,1,0:T(8,128)(2,1)S(1)} collective-permute-done((bf16[8,32,16,128]{3,2,1,0:T(8,128)(2,1)S(1)}, bf16[8,32,16,128]{3,2,1,0:T(8,128)(2,1)S(1)}, u32[]{:S(2)}, u32[]{:S(2)}) %collective-permute-start.5) | collective-permute-done | bytes 1048608 | tf_op jit(solution)/shard_map/ppermute | solution.py:38
  157.4 19.2 %all_to_all.43.got_ref = bf16[8,33,16,128]{3,2,1,0:T(8,128)(2,1)S(1)} all-to-all(bf16[8,33,16,128]{3,2,1,0:T(8,128)(2,1)S(1)} %shard_map.92), channel_id=1, replica_groups=mesh['zh'=4,'zl'=2,'yl'=2,'x'=4,'yh'=4,'c'=2] {'yl','x'}, dimensions={0} | all-to-all | bytes 2162688 | tf_op jit(solution)/shard_map/all_to_all | solution.py:34
  176.8 18.1 %all_to_all.44.got_ref = bf16[32,32,128]{2,1,0:T(8,128)(2,1)S(1)} all-to-all(bf16[32,32,128]{2,1,0:T(8,128)(2,1)S(1)} %shard_map.93), channel_id=1, replica_groups=mesh['zh'=4,'zl'=2,'yl'=2,'x'=4,'yh'=4,'c'=2] {'zh','zl','yh'}, dimensions={0} | all-to-all | bytes 524288 | tf_op jit(solution)/shard_map/all_to_all | solution.py:34
  (40 shorter events, 11.1 us)
Async XLA Ops:
  2.2 30.0 %all-to-all-start = ((bf16[16,8,1024]{2,1,0:T(8,128)(2,1)}), bf16[16,8,1024]{2,1,0:T(8,128)(2,1)S(1)}, u32[]{:S(2)}, u32[]{:S(2)}) async-start(bf16[16,8,1024]{2,1,0:T(8,128)(2,1)} %bitcast.8), calls=%async_computation | async-start | bytes 524288 | tf_op jit(solution)/shard_map/all_to_all | solution.py:34
  19.1 10.3 %collective-permute-start = (bf16[128,1024]{1,0:T(8,128)(2,1)S(1)}, bf16[128,1024]{1,0:T(8,128)(2,1)S(1)}, u32[]{:S(2)}, u32[]{:S(2)}) collective-permute-start(bf16[128,1024]{1,0:T(8,128)(2,1)S(1)} %get-tuple-element.45), channel_id=1, source_target_pairs={{32,2},{2,32},{34,4},{4,34},{36,6},{6,36},{38,0},{0,38},{33,3},{3,... | collective-permute-start | bytes 786440 | tf_op jit(solution)/shard_map/ppermute | solution.py:48
  33.8 34.1 %all-to-all-start.1 = ((bf16[8,32,4096]{2,1,0:T(8,128)(2,1)}), bf16[8,32,4096]{2,1,0:T(8,128)(2,1)}, u32[]{:S(2)}, u32[]{:S(2)}) async-start(bf16[8,32,4096]{2,1,0:T(8,128)(2,1)} %broadcast_in_dim.53), calls=%async_computation.1 | async-start | bytes 4194304 | tf_op jit(solution)/shard_map/all_to_all | solution.py:34
  38.8 17.7 %collective-permute-start.2 = (bf16[128,1024]{1,0:T(8,128)(2,1)S(1)}, bf16[128,1024]{1,0:T(8,128)(2,1)S(1)}, u32[]{:S(2)}, u32[]{:S(2)}) collective-permute-start(bf16[128,1024]{1,0:T(8,128)(2,1)S(1)} %get-tuple-element.45), channel_id=1, source_target_pairs={{36,0},{4,32},{38,2},{6,34},{32,4},{0,36},{34,6},{2,38},{37,1},{5,... | collective-permute-start | bytes 786440 | tf_op jit(solution)/shard_map/ppermute | solution.py:56
  43.0 13.5 %collective-permute-start.1 = (bf16[128,1024]{1,0:T(8,128)(2,1)S(1)}, bf16[128,1024]{1,0:T(8,128)(2,1)S(1)}, u32[]{:S(2)}, u32[]{:S(2)}) collective-permute-start(bf16[128,1024]{1,0:T(8,128)(2,1)S(1)} %collective-permute-done), channel_id=1, source_target_pairs={{0,32},{32,0},{2,34},{34,2},{4,36},{36,4},{6,38},{38,6},{1,33},{33... | collective-permute-start | bytes 786440 | tf_op jit(solution)/shard_map/ppermute | solution.py:48
  56.6 4.6 %collective-permute-start.3 = (bf16[4,128,1024]{2,1,0:T(8,128)(2,1)S(1)}, bf16[4,128,1024]{2,1,0:T(8,128)(2,1)S(1)}, u32[]{:S(2)}, u32[]{:S(2)}) collective-permute-start(bf16[4,128,1024]{2,1,0:T(8,128)(2,1)S(1)} %pad_maximum_fusion.own_ref), channel_id=1, source_target_pairs={{0,1},{1,0},{2,3},{3,2},{4,5},{5,4},{6,7},{7,6},{8,9},{9,8},{10,11... | collective-permute-start | bytes 3145736 | tf_op jit(solution)/shard_map/ppermute | solution.py:38
  61.2 1.6 copy-start
  62.8 1.8 copy-start.2
  62.8 1.9 copy-start.4
  64.6 10.0 %copy-start.5 = (s32[32]{0:T(128)S(1)}, s32[32]{0:T(128)}, u32[]{:S(2)}) copy-start(s32[32]{0:T(128)} %param.13) | copy-start | bytes 388
  67.9 22.5 %all-to-all-start.2 = ((bf16[16,16,1024]{2,1,0:T(8,128)(2,1)}), bf16[16,16,1024]{2,1,0:T(8,128)(2,1)S(1)}, u32[]{:S(2)}, u32[]{:S(2)}) async-start(bf16[16,16,1024]{2,1,0:T(8,128)(2,1)} %get-tuple-element.26), calls=%async_computation.2 | async-start | bytes 1048576 | tf_op jit(solution)/shard_map/all_to_all | solution.py:34
  90.3 58.3 %copy-start.3 = (bf16[128,8192]{1,0:T(8,128)(2,1)S(1)}, bf16[128,8192]{1,0:T(8,128)(2,1)}, u32[]{:S(2)}) copy-start(bf16[128,8192]{1,0:T(8,128)(2,1)} %frozen_ref.3) | copy-start | bytes 6291460
  93.6 55.0 %copy-start.1 = (bf16[128,8192]{1,0:T(8,128)(2,1)S(1)}, bf16[128,8192]{1,0:T(8,128)(2,1)}, u32[]{:S(2)}) copy-start(bf16[128,8192]{1,0:T(8,128)(2,1)} %in_ref.3) | copy-start | bytes 6291460
  93.6 3.4 %collective-permute-start.4 = (f32[136,256]{1,0:T(8,128)S(1)}, f32[136,256]{1,0:T(8,128)S(1)}, u32[]{:S(2)}, u32[]{:S(2)}) collective-permute-start(f32[136,256]{1,0:T(8,128)S(1)} %shard_map.88.own_ref), channel_id=1, source_target_pairs={{0,1},{1,0},{2,3},{3,2},{4,5},{5,4},{6,7},{7,6},{8,9},{9,8},{10,11... | collective-permute-start | bytes 417800 | tf_op jit(solution)/shard_map/ppermute | solution.py:38
  152.6 4.6 %collective-permute-start.5 = (bf16[8,32,16,128]{3,2,1,0:T(8,128)(2,1)S(1)}, bf16[8,32,16,128]{3,2,1,0:T(8,128)(2,1)S(1)}, u32[]{:S(2)}, u32[]{:S(2)}) collective-permute-start(bf16[8,32,16,128]{3,2,1,0:T(8,128)(2,1)S(1)} %get-tuple-element.38), channel_id=1, source_target_pairs={{0,1},{1,0},{2,3},{3,2},{4,5},{5,4},{6,7},{7,6},{8,9},{9,8},{10,11... | collective-permute-start | bytes 3145736 | tf_op jit(solution)/shard_map/ppermute | solution.py:38

commit v11 on v10

--- a/solution.py
+++ b/solution.py
@@ -240,7 +240,7 @@
     out_ref[...] = total_ref[...].astype(bf16).reshape(out_ref.shape)
 
 
-def backward(nyh, nc, place_ref, got_ref, unit_ref, length_ref, inv_ref, frozen_ref, gain_ref,
+def backward(nyh, nc, nzl, place_ref, got_ref, unit_ref, length_ref, inv_ref, frozen_ref, gain_ref,
              in_ref, own_ref, other_ref, latent_ref, latent_t_ref, keep_ref, send_ref,
              grad_ref, scaled_ref, up_ref, hg_ref, hidden):
     _, both, feats = own_ref.shape
@@ -248,7 +248,8 @@
     rank = both // 2
     tokens, width = in_ref.shape
     queries = tokens // LEN
-    nx, _, pair_rows, cols = keep_ref.shape
+    peers, _, pair_rows, cols = keep_ref.shape
+    line = peers // nzl
     out_rows = pair_rows // 2
     for c in range(nc):
         total = got_ref[c].astype(f32)
@@ -290,7 +291,7 @@
     first = place_ref[2 * own_ref.shape[0]] == 0
     for f in range(slices):
         down = dot(latent_grad, in_ref[:, f * feats:(f + 1) * feats])
-        for x in range(nx):
+        for x in range(line):
             lanes = slice(x * cols, (x + 1) * cols)
             spot = slice(f * feats + x * cols, f * feats + (x + 1) * cols)
             for yh in range(nyh):
@@ -300,8 +301,8 @@
                     tiles.append(
                         jnp.concatenate([down[of, lanes], up_ref[of, spot]], axis=0).astype(bf16)
                     )
-                keep_ref[x, f * nyh + yh] = jnp.where(first, tiles[0], tiles[1])
-                send_ref[x, f * nyh + yh] = jnp.where(first, tiles[1], tiles[0])
+                keep_ref[f % nzl * line + x, f // nzl * nyh + yh] = jnp.where(first, tiles[0], tiles[1])
+                send_ref[f % nzl * line + x, f // nzl * nyh + yh] = jnp.where(first, tiles[1], tiles[0])
 
 
 def split_rows(value, rows, cols):
@@ -452,10 +453,11 @@
 
     out_rows = rank // (nyh * nc)
     cols = width // (nzh * nzl * nyl * nx)
-    blocks = nzh * nzl * nyh
+    blocks = nzh * nyh
+    peers = nzl * nyl * nx
     keep, send = call(
-        functools.partial(backward, nyh, nc),
-        [shape((nyl * nx, blocks, 2 * out_rows, cols), bf16)] * 2,
+        functools.partial(backward, nyh, nc, nzl),
+        [shape((peers, blocks, 2 * out_rows, cols), bf16)] * 2,
         [
             place, got, unit, length, inv, frozen, gain, adapter_in, own_mats, other_mats,
             latent, latent_t,
@@ -472,16 +474,16 @@
     )
     (chip,) = call(
         join,
-        [shape((nyl * nx, blocks + 1, 2 * out_rows, cols), bf16)],
+        [shape((peers, blocks + 1, 2 * out_rows, cols), bf16)],
         [keep, swap_cores(send), loss],
     )
     (line,) = call(
-        add_line, [shape((blocks, 4 * out_rows, cols), bf16)], [exchange(chip, ("yl", "x"))]
+        add_line, [shape((blocks, 4 * out_rows, cols), bf16)], [exchange(chip, ("zl", "yl", "x"))]
     )
     adapter_grads, loss = call(
         functools.partial(add_last, group * nyl * members),
         [shape((2, out_rows, cols), f32), shape((1, 1), f32)],
-        [exchange(line, ("zh", "zl", "yh"))],
+        [exchange(line, ("zh", "yh"))],
         out_spaces=[VMEM, SMEM],
     )
     return (adapter_grads, loss.reshape(()))

time: 196 us -> 196 us (level)
  the two profiles are of different devices: /device:TPU:16 before, /device:TPU:2 now
where the time goes in v11:
time: 196 us; the launch traced here: 195 us
  blocking collectives  83.9 us (43%)
  starting transfers between devices  48.8 us (25%)
  waiting for transfers between devices  39.3 us (20%)
  Pallas kernels  15.9 us (8%)
  local copies, waits for them, and re-layouts  5.35 us (3%)
    all_to_all x5, blocking collectives, exchange(): return lax.all_to_all(blocks, axes, 0, 0, tiled=True)  83.9 us
    all_to_all x3, starting transfers between devices, exchange(): return lax.all_to_all(blocks, axes, 0, 0, tiled=True)  28.2 us
    pallas_call x9, Pallas kernels, call(): pl.pallas_call(kernel, out_shape=outs, in_specs=spaces, out_specs=out_spa...  15.9 us
    all_to_all x3, waiting for transfers between devices, exchange(): return lax.all_to_all(blocks, axes, 0, 0, tiled=True)  15.8 us
    ppermute x2, waiting for transfers between devices, swap_neighbours(): return lax.ppermute(value, ('yl', 'yh'), pairs)  10.6 us
    ppermute x3, starting transfers between devices, swap_cores(): return lax.ppermute(value, 'c', [(0, 1), (1, 0)])  8.43 us
    ppermute x2, starting transfers between devices, swap_neighbours(): return lax.ppermute(value, ('yl', 'yh'), pairs)  8.08 us
    ppermute x1, waiting for transfers between devices, from_opposite(): return lax.ppermute(value, ('yl', 'yh'), pairs)  7.27 us
  transfers between devices with their start and end apart: 9, of which 7 were waited for; matrix products, arithmetic and copies ran while one was open for 1% of the time, Pallas kernels for 3%

profile of v11, /device:TPU:2, one launch (start us, length us, event | category | flops | bytes accessed | tf_op | source)
XLA Modules:
  0.0 195.5 jit_solution(15044696959097714258)
XLA Ops:
  2.2 15.7 %all-to-all-start = ((bf16[16,8,1024]{2,1,0:T(8,128)(2,1)}), bf16[16,8,1024]{2,1,0:T(8,128)(2,1)S(1)}, u32[]{:S(2)}, u32[]{:S(2)}) async-start(bf16[16,8,1024]{2,1,0:T(8,128)(2,1)} %bitcast.8), calls=%async_computation | async-start | bytes 524288 | tf_op jit(solution)/shard_map/all_to_all | solution.py:34
  18.9 5.2 %collective-permute-start = (bf16[128,1024]{1,0:T(8,128)(2,1)S(1)}, bf16[128,1024]{1,0:T(8,128)(2,1)S(1)}, u32[]{:S(2)}, u32[]{:S(2)}) collective-permute-start(bf16[128,1024]{1,0:T(8,128)(2,1)S(1)} %get-tuple-element.45), channel_id=1, source_target_pairs={{32,2},{2,32},{34,4},{4,34},{36,6},{6,36},{38,0},{0,38},{33,3},{3,... | collective-permute-start | bytes 786440 | tf_op jit(solution)/shard_map/ppermute | solution.py:48
  24.1 8.7 %collective-permute-done = bf16[128,1024]{1,0:T(8,128)(2,1)S(1)} collective-permute-done((bf16[128,1024]{1,0:T(8,128)(2,1)S(1)}, bf16[128,1024]{1,0:T(8,128)(2,1)S(1)}, u32[]{:S(2)}, u32[]{:S(2)}) %collective-permute-start) | collective-permute-done | bytes 262176 | tf_op jit(solution)/shard_map/ppermute | solution.py:48
  34.3 5.7 %all-to-all-start.1 = ((bf16[8,32,4096]{2,1,0:T(8,128)(2,1)}), bf16[8,32,4096]{2,1,0:T(8,128)(2,1)}, u32[]{:S(2)}, u32[]{:S(2)}) async-start(bf16[8,32,4096]{2,1,0:T(8,128)(2,1)} %broadcast_in_dim.53), calls=%async_computation.1 | async-start | bytes 4194304 | tf_op jit(solution)/shard_map/all_to_all | solution.py:34
  40.1 4.0 %collective-permute-start.2 = (bf16[128,1024]{1,0:T(8,128)(2,1)S(1)}, bf16[128,1024]{1,0:T(8,128)(2,1)S(1)}, u32[]{:S(2)}, u32[]{:S(2)}) collective-permute-start(bf16[128,1024]{1,0:T(8,128)(2,1)S(1)} %get-tuple-element.45), channel_id=1, source_target_pairs={{36,0},{4,32},{38,2},{6,34},{32,4},{0,36},{34,6},{2,38},{37,1},{5,... | collective-permute-start | bytes 786440 | tf_op jit(solution)/shard_map/ppermute | solution.py:56
  44.1 2.9 %collective-permute-start.1 = (bf16[128,1024]{1,0:T(8,128)(2,1)S(1)}, bf16[128,1024]{1,0:T(8,128)(2,1)S(1)}, u32[]{:S(2)}, u32[]{:S(2)}) collective-permute-start(bf16[128,1024]{1,0:T(8,128)(2,1)S(1)} %collective-permute-done), channel_id=1, source_target_pairs={{0,32},{32,0},{2,34},{34,2},{4,36},{36,4},{6,38},{38,6},{1,33},{33... | collective-permute-start | bytes 786440 | tf_op jit(solution)/shard_map/ppermute | solution.py:48
  47.0 7.3 %collective-permute-done.2 = bf16[128,1024]{1,0:T(8,128)(2,1)S(1)} collective-permute-done((bf16[128,1024]{1,0:T(8,128)(2,1)S(1)}, bf16[128,1024]{1,0:T(8,128)(2,1)S(1)}, u32[]{:S(2)}, u32[]{:S(2)}) %collective-permute-start.2) | collective-permute-done | bytes 262176 | tf_op jit(solution)/shard_map/ppermute | solution.py:56
  54.3 1.9 collective-permute-done.1
  56.3 1.9 collective-permute-start.3
  58.5 2.4 %collective-permute-done.3.other_ref = bf16[4,128,1024]{2,1,0:T(8,128)(2,1)S(1)} collective-permute-done((bf16[4,128,1024]{2,1,0:T(8,128)(2,1)S(1)}, bf16[4,128,1024]{2,1,0:T(8,128)(2,1)S(1)}, u32[]{:S(2)}, u32[]{:S(2)}) %collective-permute-start.3) | collective-permute-done | bytes 1048608 | tf_op jit(solution)/shard_map/ppermute | solution.py:38
  64.4 3.2 %shard_map.87 = (f32[128,128]{1,0:T(8,128)S(1)}, f32[4,8192]{1,0:T(4,128)S(1)}, f32[4,128]{1,0:T(4,128)S(1)}, bf16[16,16,1024]{2,1,0:T(8,128)(2,1)}) custom-call(s32[9]{0:T(128)S(1)} %pad_add_fusion.place_ref, bf16[128,64]{1,0:T(8,128)(2,1)S(1)} %get-tuple-element.23.latent_ref, bf16[128,8192]{1,0:T(8,128)(2,1)S(1)} %copy-done.2, f32[1,8192]{1,0:T(1,128)S(1)} %bitcast.23, ...), custom_call_target="tpu_custom_call" | custom-call | flops 134217728 | bytes 4966436 | tf_op jit(solution)/shard_map/pallas_call | solution.py:74
  67.6 6.8 %all-to-all-start.2 = ((bf16[16,16,1024]{2,1,0:T(8,128)(2,1)}), bf16[16,16,1024]{2,1,0:T(8,128)(2,1)S(1)}, u32[]{:S(2)}, u32[]{:S(2)}) async-start(bf16[16,16,1024]{2,1,0:T(8,128)(2,1)} %get-tuple-element.26), calls=%async_computation.2 | async-start | bytes 1048576 | tf_op jit(solution)/shard_map/all_to_all | solution.py:34
  75.1 15.7 %all-to-all-done.2.query_ref = bf16[16,16,1024]{2,1,0:T(8,128)(2,1)S(1)} async-done(((bf16[16,16,1024]{2,1,0:T(8,128)(2,1)}), bf16[16,16,1024]{2,1,0:T(8,128)(2,1)S(1)}, u32[]{:S(2)}, u32[]{:S(2)}) %all-to-all-start.2) | async-done | bytes 524320 | tf_op jit(solution)/shard_map/all_to_all | solution.py:34
  90.9 3.3 %shard_map.88.own_ref = f32[136,256]{1,0:T(8,128)S(1)} custom-call(bf16[16,16,1024]{2,1,0:T(8,128)(2,1)S(1)} %all-to-all-done.2.query_ref, bf16[256,4096]{1,0:T(8,128)(2,1)} %bitcast.16.block_ref), custom_call_target="tpu_custom_call" | custom-call | flops 1073741824 | bytes 2760704 | tf_op jit(solution)/shard_map/pallas_call | solution.py:74
  94.1 3.4 %collective-permute-start.4 = (f32[136,256]{1,0:T(8,128)S(1)}, f32[136,256]{1,0:T(8,128)S(1)}, u32[]{:S(2)}, u32[]{:S(2)}) collective-permute-start(f32[136,256]{1,0:T(8,128)S(1)} %shard_map.88.own_ref), channel_id=1, source_target_pairs={{0,1},{1,0},{2,3},{3,2},{4,5},{5,4},{6,7},{7,6},{8,9},{9,8},{10,11... | collective-permute-start | bytes 417800 | tf_op jit(solution)/shard_map/ppermute | solution.py:38
  98.7 10.2 %all_to_all.40.rows_ref = f32[8,1,128]{2,1,0:T(1,128)S(1)} all-to-all(f32[8,1,128]{2,1,0:T(1,128)S(1)} %get-tuple-element.30), channel_id=1, replica_groups=mesh['zh'=4,'zl'=2,'yl'=2,'x'=4,'yh'=4,'c'=2] {'yl','yh'}, dimensions={0} | all-to-all | bytes 8192 | tf_op jit(solution)/shard_map/all_to_all | solution.py:34
  108.9 17.7 %all_to_all.41.cols_ref = f32[32,1,256]{2,1,0:T(1,128)S(1)} all-to-all(f32[32,1,256]{2,1,0:T(1,128)S(1)} %get-tuple-element.31), channel_id=1, replica_groups=mesh['zh'=4,'zl'=2,'yl'=2,'x'=4,'yh'=4,'c'=2] {'zh','zl','x'}, dimensions={0} | all-to-all | bytes 65536 | tf_op jit(solution)/shard_map/all_to_all | solution.py:34
  126.7 2.3 %shard_map.90 = (bf16[16,16,1024]{2,1,0:T(8,128)(2,1)S(1)}, f32[8,128]{1,0:T(8,128)S(1)}) custom-call(f32[128,256]{1,0:T(8,128)S(1)} %get-tuple-element.28.expo_ref, f32[8,256]{1,0:T(8,128)S(1)} %get-tuple-element.29.aux_ref, f32[128,256]{1,0:T(8,128)S(1)} %compare_convert_fusion.onehot_ref, f32[8,1,128]{2,1,0:T(1,128)S(1)} %all_to_all.40.rows_ref, ...), custom_call_target="tpu_custom_call" | custom-call | flops 536870912 | bytes 2932736 | tf_op jit(solution)/shard_map/pallas_call | solution.py:74
  129.0 19.0 %all_to_all.42.got_ref = bf16[16,16,1024]{2,1,0:T(8,128)(2,1)S(1)} all-to-all(bf16[16,16,1024]{2,1,0:T(8,128)(2,1)S(1)} %get-tuple-element.32), channel_id=1, replica_groups=mesh['zh'=4,'zl'=2,'yl'=2,'x'=4,'yh'=4,'c'=2] {'yl','yh','c'}, dimensions={0} | all-to-all | bytes 1048576 | tf_op jit(solution)/shard_map/all_to_all | solution.py:34
  148.0 4.0 %shard_map.91 = (bf16[16,16,16,128]{3,2,1,0:T(8,128)(2,1)S(1)}, bf16[16,16,16,128]{3,2,1,0:T(8,128)(2,1)S(1)}) custom-call(s32[9]{0:T(128)S(1)} %pad_add_fusion.place_ref, bf16[16,16,1024]{2,1,0:T(8,128)(2,1)S(1)} %all_to_all.42.got_ref, f32[4,8192]{1,0:T(4,128)S(1)} %get-tuple-element.33.unit_ref, f32[4,128]{1,0:T(4,128)S(1)} %get-tuple-element.34.length_ref, ...), custom_call_target="tpu_custom_call" | custom-call | flops 536870912 | bytes 9177124 | tf_op jit(solution)/shard_map/pallas_call | solution.py:74
  152.0 3.2 %collective-permute-start.5 = (bf16[16,16,16,128]{3,2,1,0:T(8,128)(2,1)S(1)}, bf16[16,16,16,128]{3,2,1,0:T(8,128)(2,1)S(1)}, u32[]{:S(2)}, u32[]{:S(2)}) collective-permute-start(bf16[16,16,16,128]{3,2,1,0:T(8,128)(2,1)S(1)} %get-tuple-element.38), channel_id=1, source_target_pairs={{0,1},{1,0},{2,3},{3,2},{4,5},{5,4},{6,7},{7,6},{8,9},{9,8},{10,11... | collective-permute-start | bytes 3145736 | tf_op jit(solution)/shard_map/ppermute | solution.py:38
  155.2 2.3 %collective-permute-done.5.got_ref = bf16[16,16,16,128]{3,2,1,0:T(8,128)(2,1)S(1)} collective-permute-done((bf16[16,16,16,128]{3,2,1,0:T(8,128)(2,1)S(1)}, bf16[16,16,16,128]{3,2,1,0:T(8,128)(2,1)S(1)}, u32[]{:S(2)}, u32[]{:S(2)}) %collective-permute-start.5) | collective-permute-done | bytes 1048608 | tf_op jit(solution)/shard_map/ppermute | solution.py:38
  157.7 20.9 %all_to_all.43.got_ref = bf16[16,17,16,128]{3,2,1,0:T(8,128)(2,1)S(1)} all-to-all(bf16[16,17,16,128]{3,2,1,0:T(8,128)(2,1)S(1)} %shard_map.92), channel_id=1, replica_groups=mesh['zh'=4,'zl'=2,'yl'=2,'x'=4,'yh'=4,'c'=2] {'zl','yl','x'}, dimensions={0} | all-to-all | bytes 2228224 | tf_op jit(solution)/shard_map/all_to_all | solution.py:34
  178.8 16.0 %all_to_all.44.got_ref = bf16[16,32,128]{2,1,0:T(8,128)(2,1)S(1)} all-to-all(bf16[16,32,128]{2,1,0:T(8,128)(2,1)S(1)} %shard_map.93), channel_id=1, replica_groups=mesh['zh'=4,'zl'=2,'yl'=2,'x'=4,'yh'=4,'c'=2] {'zh','yh'}, dimensions={0} | all-to-all | bytes 262144 | tf_op jit(solution)/shard_map/all_to_all | solution.py:34
  (40 shorter events, 10.8 us)
Async XLA Ops:
  2.2 30.6 %all-to-all-start = ((bf16[16,8,1024]{2,1,0:T(8,128)(2,1)}), bf16[16,8,1024]{2,1,0:T(8,128)(2,1)S(1)}, u32[]{:S(2)}, u32[]{:S(2)}) async-start(bf16[16,8,1024]{2,1,0:T(8,128)(2,1)} %bitcast.8), calls=%async_computation | async-start | bytes 524288 | tf_op jit(solution)/shard_map/all_to_all | solution.py:34
  18.9 13.9 %collective-permute-start = (bf16[128,1024]{1,0:T(8,128)(2,1)S(1)}, bf16[128,1024]{1,0:T(8,128)(2,1)S(1)}, u32[]{:S(2)}, u32[]{:S(2)}) collective-permute-start(bf16[128,1024]{1,0:T(8,128)(2,1)S(1)} %get-tuple-element.45), channel_id=1, source_target_pairs={{32,2},{2,32},{34,4},{4,34},{36,6},{6,36},{38,0},{0,38},{33,3},{3,... | collective-permute-start | bytes 786440 | tf_op jit(solution)/shard_map/ppermute | solution.py:48
  34.3 33.3 %all-to-all-start.1 = ((bf16[8,32,4096]{2,1,0:T(8,128)(2,1)}), bf16[8,32,4096]{2,1,0:T(8,128)(2,1)}, u32[]{:S(2)}, u32[]{:S(2)}) async-start(bf16[8,32,4096]{2,1,0:T(8,128)(2,1)} %broadcast_in_dim.53), calls=%async_computation.1 | async-start | bytes 4194304 | tf_op jit(solution)/shard_map/all_to_all | solution.py:34
  40.1 14.2 %collective-permute-start.2 = (bf16[128,1024]{1,0:T(8,128)(2,1)S(1)}, bf16[128,1024]{1,0:T(8,128)(2,1)S(1)}, u32[]{:S(2)}, u32[]{:S(2)}) collective-permute-start(bf16[128,1024]{1,0:T(8,128)(2,1)S(1)} %get-tuple-element.45), channel_id=1, source_target_pairs={{36,0},{4,32},{38,2},{6,34},{32,4},{0,36},{34,6},{2,38},{37,1},{5,... | collective-permute-start | bytes 786440 | tf_op jit(solution)/shard_map/ppermute | solution.py:56
  44.1 12.1 %collective-permute-start.1 = (bf16[128,1024]{1,0:T(8,128)(2,1)S(1)}, bf16[128,1024]{1,0:T(8,128)(2,1)S(1)}, u32[]{:S(2)}, u32[]{:S(2)}) collective-permute-start(bf16[128,1024]{1,0:T(8,128)(2,1)S(1)} %collective-permute-done), channel_id=1, source_target_pairs={{0,32},{32,0},{2,34},{34,2},{4,36},{36,4},{6,38},{38,6},{1,33},{33... | collective-permute-start | bytes 786440 | tf_op jit(solution)/shard_map/ppermute | solution.py:48
  56.3 4.6 %collective-permute-start.3 = (bf16[4,128,1024]{2,1,0:T(8,128)(2,1)S(1)}, bf16[4,128,1024]{2,1,0:T(8,128)(2,1)S(1)}, u32[]{:S(2)}, u32[]{:S(2)}) collective-permute-start(bf16[4,128,1024]{2,1,0:T(8,128)(2,1)S(1)} %pad_maximum_fusion.own_ref), channel_id=1, source_target_pairs={{0,1},{1,0},{2,3},{3,2},{4,5},{5,4},{6,7},{7,6},{8,9},{9,8},{10,11... | collective-permute-start | bytes 3145736 | tf_op jit(solution)/shard_map/ppermute | solution.py:38
  60.9 1.6 copy-start
  62.5 1.8 copy-start.2
  62.5 1.9 copy-start.4
  64.4 10.3 %copy-start.5 = (s32[32]{0:T(128)S(1)}, s32[32]{0:T(128)}, u32[]{:S(2)}) copy-start(s32[32]{0:T(128)} %param.13) | copy-start | bytes 388
  67.6 23.3 %all-to-all-start.2 = ((bf16[16,16,1024]{2,1,0:T(8,128)(2,1)}), bf16[16,16,1024]{2,1,0:T(8,128)(2,1)S(1)}, u32[]{:S(2)}, u32[]{:S(2)}) async-start(bf16[16,16,1024]{2,1,0:T(8,128)(2,1)} %get-tuple-element.26), calls=%async_computation.2 | async-start | bytes 1048576 | tf_op jit(solution)/shard_map/all_to_all | solution.py:34
  90.9 57.2 %copy-start.3 = (bf16[128,8192]{1,0:T(8,128)(2,1)S(1)}, bf16[128,8192]{1,0:T(8,128)(2,1)}, u32[]{:S(2)}) copy-start(bf16[128,8192]{1,0:T(8,128)(2,1)} %frozen_ref.3) | copy-start | bytes 6291460
  94.1 53.9 %copy-start.1 = (bf16[128,8192]{1,0:T(8,128)(2,1)S(1)}, bf16[128,8192]{1,0:T(8,128)(2,1)}, u32[]{:S(2)}) copy-start(bf16[128,8192]{1,0:T(8,128)(2,1)} %in_ref.3) | copy-start | bytes 6291460
  94.1 4.3 %collective-permute-start.4 = (f32[136,256]{1,0:T(8,128)S(1)}, f32[136,256]{1,0:T(8,128)S(1)}, u32[]{:S(2)}, u32[]{:S(2)}) collective-permute-start(f32[136,256]{1,0:T(8,128)S(1)} %shard_map.88.own_ref), channel_id=1, source_target_pairs={{0,1},{1,0},{2,3},{3,2},{4,5},{5,4},{6,7},{7,6},{8,9},{9,8},{10,11... | collective-permute-start | bytes 417800 | tf_op jit(solution)/shard_map/ppermute | solution.py:38
  152.0 5.4 %collective-permute-start.5 = (bf16[16,16,16,128]{3,2,1,0:T(8,128)(2,1)S(1)}, bf16[16,16,16,128]{3,2,1,0:T(8,128)(2,1)S(1)}, u32[]{:S(2)}, u32[]{:S(2)}) collective-permute-start(bf16[16,16,16,128]{3,2,1,0:T(8,128)(2,1)S(1)} %get-tuple-element.38), channel_id=1, source_target_pairs={{0,1},{1,0},{2,3},{3,2},{4,5},{5,4},{6,7},{7,6},{8,9},{9,8},{10,11... | collective-permute-start | bytes 3145736 | tf_op jit(solution)/shard_map/ppermute | solution.py:38
